TPU v7x, 512 devices: a whole 4x4x16 slice. The times are simulated.
512 devices in a mesh: ctx: 64 (over z, y), head: 8 (over x, core).
Axes of the slice: x: 4, y: 4, z: 16, core: 2. Of those that a mesh axis runs over, the one named last changes fastest.
Arguments:
- query_rows: bfloat16 [65536, 2048], P(('ctx', 'head')), may hold values from -2.5 to 2.5
- key_rows: bfloat16 [65536, 2048], P(('ctx', 'head')), may hold values from -2.5 to 2.5
- value_rows: bfloat16 [65536, 2048], P(('ctx', 'head')), may hold values from -6 to 6
- grad_rows: bfloat16 [65536, 2048], P(('ctx', 'head')), may hold values from -6 to 6
Outputs:
- attended: bfloat16 [65536, 2048], P(('ctx', 'head'))
- grad_query: bfloat16 [65536, 2048], P(('ctx', 'head'))
- grad_key: bfloat16 [65536, 2048], P(('ctx', 'head'))
- grad_value: bfloat16 [65536, 2048], P(('ctx', 'head'))
All inputs are finite; a program needn't handle non-finite values.
Results may differ from a plain program's by a relative error of at most 0.0075.
Values may be sent and summed in bfloat16 or wider, within the bound.
No kernel may reach another device: no remote copies, remote signals or barrier semaphores. Data moves between devices by JAX's collectives and lax.ppermute only.
A program may use at most 64 MiB of HBM per device.

v0:
```python
import jax
import jax.numpy as jnp
from jax import lax
from jax.sharding import PartitionSpec as P

HEAD_DIM = 128


def entering(part, axis, combine, identity, reverse):
    count = lax.axis_size(axis)
    place = lax.axis_index(axis)
    ahead = count - 1 - place if reverse else place
    gathered = lax.all_gather(part, axis)
    state = jnp.zeros_like(part) + jnp.asarray(identity, part.dtype)

    def one(step, state):
        source = count - 1 - step if reverse else step
        return combine(state, lax.dynamic_index_in_dim(gathered, source, 0, False))

    return lax.fori_loop(0, ahead, one, state)


def add_states(earlier, later_term):
    return earlier + later_term


def attend(query_in, keys_in, values_in, grads_in):
    count = query_in.shape[0]
    outer_shape = query_in.shape
    head_dim = query_in.shape[-1]
    query = query_in.reshape(count, -1, head_dim)
    keys = keys_in.reshape(count, -1, head_dim)
    values = values_in.reshape(count, -1, head_dim)
    grads = grads_in.reshape(count, -1, head_dim)
    kv_span = jnp.einsum("shd,she->hde", keys, values, preferred_element_type=jnp.float32)
    prior = entering(kv_span, "ctx", add_states, jnp.zeros_like(kv_span), False)
    prior_bf = prior.astype(jnp.bfloat16)
    rows = lax.broadcasted_iota(jnp.int32, (count, count), 0)
    cols = lax.broadcasted_iota(jnp.int32, (count, count), 1)
    mask = (rows >= cols)[None]
    scores = jnp.einsum("thd,shd->hts", query, keys, preferred_element_type=jnp.float32)
    local = jnp.where(mask, scores, 0.0).astype(jnp.bfloat16)
    mixed = jnp.einsum("hts,she->the", local, values, preferred_element_type=jnp.float32)
    mixed = mixed + jnp.einsum("thd,hde->the", query, prior_bf, preferred_element_type=jnp.float32)
    scale = lax.rsqrt(jnp.mean(mixed * mixed, axis=-1, keepdims=True) + 1e-06)
    attended = (mixed * scale).astype(jnp.bfloat16)
    grad_f = grads.astype(jnp.float32)
    inner_mean = jnp.mean(grad_f * mixed, axis=-1, keepdims=True)
    dmixed = (scale * grad_f - mixed * scale * scale * scale * inner_mean).astype(jnp.bfloat16)
    state_grad = jnp.einsum("thd,the->hde", query, dmixed, preferred_element_type=jnp.float32)
    later = entering(state_grad, "ctx", add_states, jnp.zeros_like(state_grad), True)
    later_bf = later.astype(jnp.bfloat16)
    dscore = jnp.einsum("the,she->hts", dmixed, values, preferred_element_type=jnp.float32)
    dlocal = jnp.where(mask, dscore, 0.0).astype(jnp.bfloat16)
    grad_query = jnp.einsum("hts,shd->thd", dlocal, keys, preferred_element_type=jnp.float32)
    grad_query = grad_query + jnp.einsum(
        "the,hde->thd", dmixed, prior_bf, preferred_element_type=jnp.float32
    )
    grad_key = jnp.einsum("hts,thd->shd", dlocal, query, preferred_element_type=jnp.float32)
    grad_key = grad_key + jnp.einsum(
        "she,hde->shd", values, later_bf, preferred_element_type=jnp.float32
    )
    grad_value = jnp.einsum("hts,the->she", local, dmixed, preferred_element_type=jnp.float32)
    grad_value = grad_value + jnp.einsum(
        "shd,hde->she", keys, later_bf, preferred_element_type=jnp.float32
    )
    return (
        attended.reshape(outer_shape),
        grad_query.astype(jnp.bfloat16).reshape(outer_shape),
        grad_key.astype(jnp.bfloat16).reshape(outer_shape),
        grad_value.astype(jnp.bfloat16).reshape(outer_shape),
    )


def per_device(query_rows, key_rows, value_rows, grad_rows):
    tokens = query_rows.shape[0]
    width = query_rows.shape[1]
    groups = lax.axis_size("head")
    per_group = width // (groups * HEAD_DIM)
    grouped = (tokens, groups, per_group, HEAD_DIM)
    query = query_rows.reshape(grouped)
    keys = key_rows.reshape(grouped)
    values = value_rows.reshape(grouped)
    grads = grad_rows.reshape(grouped)
    moved = (
        lax.all_to_all(query, "head", split_axis=1, concat_axis=0, tiled=True),
        lax.all_to_all(keys, "head", split_axis=1, concat_axis=0, tiled=True),
        lax.all_to_all(values, "head", split_axis=1, concat_axis=0, tiled=True),
        lax.all_to_all(grads, "head", split_axis=1, concat_axis=0, tiled=True),
    )
    results = attend(moved[0], moved[1], moved[2], moved[3])
    back = (
        lax.all_to_all(results[0], "head", split_axis=0, concat_axis=1, tiled=True),
        lax.all_to_all(results[1], "head", split_axis=0, concat_axis=1, tiled=True),
        lax.all_to_all(results[2], "head", split_axis=0, concat_axis=1, tiled=True),
        lax.all_to_all(results[3], "head", split_axis=0, concat_axis=1, tiled=True),
    )
    return (
        back[0].reshape(tokens, width),
        back[1].reshape(tokens, width),
        back[2].reshape(tokens, width),
        back[3].reshape(tokens, width),
    )


def solution(mesh):
    placed = (
        P(("ctx", "head"), None),
        P(("ctx", "head"), None),
        P(("ctx", "head"), None),
        P(("ctx", "head"), None),
    )
    return jax.shard_map(
        per_device,
        mesh=mesh,
        in_specs=placed,
        out_specs=(
            P(("ctx", "head"), None),
            P(("ctx", "head"), None),
            P(("ctx", "head"), None),
            P(("ctx", "head"), None),
        ),
        check_vma=False,
    )
```

profile of v0, /device:TPU:1, one launch (start us, length us, event | category | flops | bytes accessed | tf_op | source)
XLA Modules:
  0.0 525.8 jit_solution(1196314330391220964)
XLA Ops:
  7.2 1.3 copy.57
  8.5 1.0 copy.58
  9.5 10.3 %all-to-all-start.1 = ((bf16[128,8,2,128]{3,0,2,1:T(8,128)(2,1)}), bf16[128,8,2,128]{3,0,2,1:T(8,128)(2,1)S(1)}, u32[]{:S(2)}, u32[]{:S(2)}) async-start(bf16[128,8,2,128]{3,0,2,1:T(8,128)(2,1)} %copy.58), calls=%async_computation.1 | async-start | bytes 1048576 | tf_op jit(solution)/shard_map/all_to_all | solution.py:87
  19.8 2.0 copy.60
  21.8 7.5 %all-to-all-done.1 = bf16[128,8,2,128]{3,0,2,1:T(8,128)(2,1)S(1)} async-done(((bf16[128,8,2,128]{3,0,2,1:T(8,128)(2,1)}), bf16[128,8,2,128]{3,0,2,1:T(8,128)(2,1)S(1)}, u32[]{:S(2)}, u32[]{:S(2)}) %all-to-all-start.1) | async-done | bytes 524320 | tf_op jit(solution)/shard_map/all_to_all | solution.py:87
  29.3 4.4 all-to-all-start.2
  33.7 9.4 %all-to-all-done.2 = bf16[128,8,2,128]{0,3,2,1:T(8,128)(2,1)S(1)} async-done(((bf16[128,8,2,128]{0,3,2,1:T(8,128)(2,1)}), bf16[128,8,2,128]{0,3,2,1:T(8,128)(2,1)S(1)}, u32[]{:S(2)}, u32[]{:S(2)}) %all-to-all-start.2) | async-done | bytes 524320 | tf_op jit(solution)/shard_map/all_to_all | solution.py:88
  43.8 1.0 fusion.15
  45.1 1.0 copy.55
  46.1 4.3 all-to-all-start
  50.4 1.0 copy.67
  51.3 8.5 %all-to-all-done = bf16[128,8,2,128]{3,0,2,1:T(8,128)(2,1)S(1)} async-done(((bf16[128,8,2,128]{3,0,2,1:T(8,128)(2,1)}), bf16[128,8,2,128]{3,0,2,1:T(8,128)(2,1)S(1)}, u32[]{:S(2)}, u32[]{:S(2)}) %all-to-all-start) | async-done | bytes 524320 | tf_op jit(solution)/shard_map/all_to_all | solution.py:86
  59.8 4.3 all-to-all-start.4
  64.1 1.3 iota_compare_fusion
  65.5 8.1 %all-to-all-done.4 = bf16[128,8,2,128]{0,3,2,1:T(8,128)(2,1)S(1)} async-done(((bf16[128,8,2,128]{0,3,2,1:T(8,128)(2,1)}), bf16[128,8,2,128]{0,3,2,1:T(8,128)(2,1)S(1)}, u32[]{:S(2)}, u32[]{:S(2)}) %all-to-all-start.4) | async-done | bytes 524320 | tf_op jit(solution)/shard_map/all_to_all | solution.py:89
  73.7 1.7 copy.68
  75.4 1.4 reshape.100
  76.8 4.7 select_convert_fusion.1
  81.4 111.1 %all-gather.5.cloned.1.call-done = f32[128,128,128]{2,1,0:T(8,128)} async-done(((f32[2,128,128]{2,1,0:T(8,128)}), f32[128,128,128]{2,1,0:T(8,128)}) %all-gather.5.cloned.1.call-update) | async-done | bytes 8388624 | tf_op jit(solution)/shard_map/all_gather | solution.py:13
  192.9 3.8 multiply_reduce_fusion
  196.8 1.1 subtract_convert_fusion
  198.9 2.0 copy.65
  200.9 12.7 %all-to-all-start.3 = ((bf16[1024,1,2,128]{3,2,1,0:T(2,128)(2,1)}), bf16[1024,1,2,128]{3,2,1,0:T(2,128)(2,1)S(1)}, u32[]{:S(2)}, u32[]{:S(2)}) async-start(bf16[1024,1,2,128]{3,2,1,0:T(2,128)(2,1)} %copy.65), calls=%async_computation.3 | async-start | bytes 1048576 | tf_op jit(solution)/shard_map/all_to_all | solution.py:93
  214.0 2.8 select_convert_fusion
  216.8 1.9 copy-done
  218.7 1.3 fusion.8
  220.0 1.3 copy.73
  221.3 185.9 %all-gather.7.cloned.1.call-done = f32[128,128,128]{2,1,0:T(8,128)} async-done(((f32[2,128,128]{2,1,0:T(8,128)}), f32[128,128,128]{2,1,0:T(8,128)}) %all-gather.7.cloned.1.call-update) | async-done | bytes 8388624 | tf_op jit(solution)/shard_map/all_gather | solution.py:13
  407.3 60.5 %while.23 = (s32[]{:T(128)}, f32[2,128,128]{2,1,0:T(8,128)S(1)}, s32[]{:T(128)}, f32[64,2,128,128]{3,2,1,0:T(8,128)}, s32[]{:T(128)}, /*index=5*/s32[]{:T(128)}, s32[]{:T(128)}, s32[]{:T(128)}) while((s32[]{:T(128)}, f32[2,128,128]{2,1,0:T(8,128)S(1)}, s32[]{:T(128)}, f32[64,2,128,128]{3,2,1,0:T(8,128)}, s32[]{:T(128)}, /*index=5*/s32[]{:T(128)}, ...), condition=%wide.region_5.6_spmd, body=%wide.region_4.5_spmd.sunk | while | flops 32774 | bytes 393359 | solution.py:20
  407.3 0.9 bitcast_add_fusion.5
  408.2 0.9 bitcast_add_fusion.5
  409.2 0.9 bitcast_add_fusion.5
  410.2 0.9 bitcast_add_fusion.5
  411.1 0.9 bitcast_add_fusion.5
  412.1 0.9 bitcast_add_fusion.5
  413.0 0.9 bitcast_add_fusion.5
  414.0 0.9 bitcast_add_fusion.5
  415.0 0.9 bitcast_add_fusion.5
  415.9 0.9 bitcast_add_fusion.5
  416.9 0.9 bitcast_add_fusion.5
  417.8 0.9 bitcast_add_fusion.5
  418.8 0.9 bitcast_add_fusion.5
  419.8 0.9 bitcast_add_fusion.5
  420.7 0.9 bitcast_add_fusion.5
  421.7 0.9 bitcast_add_fusion.5
  422.6 0.9 bitcast_add_fusion.5
  423.6 0.9 bitcast_add_fusion.5
  424.6 0.9 bitcast_add_fusion.5
  425.5 0.9 bitcast_add_fusion.5
  426.5 0.9 bitcast_add_fusion.5
  467.8 12.6 %all-to-all-start.5 = ((bf16[1024,1,2,128]{3,2,1,0:T(2,128)(2,1)}), bf16[1024,1,2,128]{3,2,1,0:T(2,128)(2,1)S(1)}, u32[]{:S(2)}, u32[]{:S(2)}) async-start(bf16[1024,1,2,128]{3,2,1,0:T(2,128)(2,1)} %copy.73), calls=%async_computation.5 | async-start | bytes 1048576 | tf_op jit(solution)/shard_map/all_to_all | solution.py:94
  480.7 3.0 fusion.6
  483.7 1.1 copy.82
  484.8 5.1 all-to-all-done.5
  489.8 4.3 all-to-all-start.7
  494.4 3.7 fusion.7
  498.2 1.3 copy.79
  499.5 4.1 all-to-all-done.7
  503.6 4.3 all-to-all-start.6
  508.2 1.2 reshape.92
  509.8 1.2 reshape.95
  511.3 1.2 reshape.99
  512.5 4.9 all-to-all-done.6
  517.7 1.2 reshape.97
  (72 shorter events, 44.3 us)
Async XLA Ops:
  8.5 36.3 %copy-start.1 = (bf16[128,2048]{1,0:T(8,128)(2,1)S(1)}, bf16[128,2048]{1,0:T(8,128)(2,1)}, u32[]{:S(2)}) copy-start(bf16[128,2048]{1,0:T(8,128)(2,1)} %param.8) | copy-start | bytes 1572868
  9.5 19.8 %all-to-all-start.1 = ((bf16[128,8,2,128]{3,0,2,1:T(8,128)(2,1)}), bf16[128,8,2,128]{3,0,2,1:T(8,128)(2,1)S(1)}, u32[]{:S(2)}, u32[]{:S(2)}) async-start(bf16[128,8,2,128]{3,0,2,1:T(8,128)(2,1)} %copy.58), calls=%async_computation.1 | async-start | bytes 1048576 | tf_op jit(solution)/shard_map/all_to_all | solution.py:87
  29.3 21.1 %copy-start.2 = (bf16[128,2048]{1,0:T(8,128)(2,1)S(1)}, bf16[128,2048]{1,0:T(8,128)(2,1)}, u32[]{:S(2)}) copy-start(bf16[128,2048]{1,0:T(8,128)(2,1)} %param.11) | copy-start | bytes 1572868
  29.3 13.9 %all-to-all-start.2 = ((bf16[128,8,2,128]{0,3,2,1:T(8,128)(2,1)}), bf16[128,8,2,128]{0,3,2,1:T(8,128)(2,1)S(1)}, u32[]{:S(2)}, u32[]{:S(2)}) async-start(bf16[128,8,2,128]{0,3,2,1:T(8,128)(2,1)} %bitcast.10), calls=%async_computation.2 | async-start | bytes 1048576 | tf_op jit(solution)/shard_map/all_to_all | solution.py:88
  33.7 158.9 %all-gather.5.cloned.1.call-start = ((), (), s32[]{:S(2)}) async-start(), calls=%async_computation.8 | async-start | bytes 8519680 | tf_op jit(solution)/shard_map/all_gather | solution.py:13
  46.1 13.8 %all-to-all-start = ((bf16[128,8,2,128]{3,0,2,1:T(8,128)(2,1)}), bf16[128,8,2,128]{3,0,2,1:T(8,128)(2,1)S(1)}, u32[]{:S(2)}, u32[]{:S(2)}) async-start(bf16[128,8,2,128]{3,0,2,1:T(8,128)(2,1)} %copy.55), calls=%async_computation | async-start | bytes 1048576 | tf_op jit(solution)/shard_map/all_to_all | solution.py:86
  59.8 13.8 %all-to-all-start.4 = ((bf16[128,8,2,128]{0,3,2,1:T(8,128)(2,1)}), bf16[128,8,2,128]{0,3,2,1:T(8,128)(2,1)S(1)}, u32[]{:S(2)}, u32[]{:S(2)}) async-start(bf16[128,8,2,128]{0,3,2,1:T(8,128)(2,1)} %bitcast.19), calls=%async_computation.4 | async-start | bytes 1048576 | tf_op jit(solution)/shard_map/all_to_all | solution.py:89
  64.1 343.1 %all-gather.7.cloned.1.call-start = ((), (), s32[]{:S(2)}) async-start(), calls=%async_computation.9 | async-start | bytes 8519680 | tf_op jit(solution)/shard_map/all_gather | solution.py:13
  200.9 266.8 %all-to-all-start.3 = ((bf16[1024,1,2,128]{3,2,1,0:T(2,128)(2,1)}), bf16[1024,1,2,128]{3,2,1,0:T(2,128)(2,1)S(1)}, u32[]{:S(2)}, u32[]{:S(2)}) async-start(bf16[1024,1,2,128]{3,2,1,0:T(2,128)(2,1)} %copy.65), calls=%async_computation.3 | async-start | bytes 1048576 | tf_op jit(solution)/shard_map/all_to_all | solution.py:93
  216.8 1.9 copy-start
  467.8 22.1 %all-to-all-start.5 = ((bf16[1024,1,2,128]{3,2,1,0:T(2,128)(2,1)}), bf16[1024,1,2,128]{3,2,1,0:T(2,128)(2,1)S(1)}, u32[]{:S(2)}, u32[]{:S(2)}) async-start(bf16[1024,1,2,128]{3,2,1,0:T(2,128)(2,1)} %copy.73), calls=%async_computation.5 | async-start | bytes 1048576 | tf_op jit(solution)/shard_map/all_to_all | solution.py:94
  489.8 13.8 %all-to-all-start.7 = ((bf16[1024,1,2,128]{3,2,1,0:T(2,128)(2,1)}), bf16[1024,1,2,128]{3,2,1,0:T(2,128)(2,1)S(1)}, u32[]{:S(2)}, u32[]{:S(2)}) async-start(bf16[1024,1,2,128]{3,2,1,0:T(2,128)(2,1)} %copy.82), calls=%async_computation.7 | async-start | bytes 1048576 | tf_op jit(solution)/shard_map/all_to_all | solution.py:96
  503.6 13.8 %all-to-all-start.6 = ((bf16[1024,1,2,128]{3,2,1,0:T(2,128)(2,1)}), bf16[1024,1,2,128]{3,2,1,0:T(2,128)(2,1)S(1)}, u32[]{:S(2)}, u32[]{:S(2)}) async-start(bf16[1024,1,2,128]{3,2,1,0:T(2,128)(2,1)} %copy.79), calls=%async_computation.6 | async-start | bytes 1048576 | tf_op jit(solution)/shard_map/all_to_all | solution.py:95
Sparse Core Ops, SparseCore 0:
  44.9 147.6 all-gather.4
  199.1 208.1 all-gather.6
where the time goes:
time: 528 us; the launch traced here: 526 us
  waiting for transfers between devices  345 us (65%)
  other arithmetic  61.6 us (12%)
  starting transfers between devices  57 us (11%)
  local copies, waits for them, and re-layouts  25 us (5%)
  matrix products  21.9 us (4%)
  between operations  14.2 us (3%)
    all_gather x2, waiting for transfers between devices, entering(): gathered = lax.all_gather(part, axis)  297 us
    add x63, other arithmetic, add_states(): return earlier + later_term  59.1 us
    all_to_all x1, starting transfers between devices, per_device(): lax.all_to_all(results[0], 'head', split_axis=0, concat_axis=1, tiled=True)  12.7 us
    all_to_all x1, starting transfers between devices, per_device(): lax.all_to_all(results[1], 'head', split_axis=0, concat_axis=1, tiled=True)  12.6 us
  transfers between devices with their start and end apart: 10, of which 9 were waited for; matrix products, arithmetic and copies ran while one was open for 18% of the time, Pallas kernels for 0%

commit v1 on v0

v1 whole, which is shorter than its diff:
```python
import functools

import jax
import jax.numpy as jnp
from jax import lax
from jax.experimental import pallas as pl
from jax.experimental.pallas import tpu as pltpu
from jax.sharding import Mesh, PartitionSpec as P

HEAD_DIM = 128
VMEM_LIMIT = 48 * 1024 * 1024
f32 = jnp.float32
bf16 = jnp.bfloat16


def dot_nn(a, b):
    return lax.dot_general(a, b, (((1,), (0,)), ((), ())), preferred_element_type=f32)


def dot_nt(a, b):
    return lax.dot_general(a, b, (((1,), (1,)), ((), ())), preferred_element_type=f32)


def dot_tn(a, b):
    return lax.dot_general(a, b, (((0,), (0,)), ((), ())), preferred_element_type=f32)


def call(kernel, out_shape, operands, flops=0, smem=()):
    in_specs = [
        pl.BlockSpec(memory_space=pltpu.SMEM if i in smem else pltpu.VMEM)
        for i in range(len(operands))
    ]
    outs = jax.tree.leaves(out_shape)
    moved = sum(x.size * x.dtype.itemsize for x in list(operands) + outs)
    return pl.pallas_call(
        kernel,
        out_shape=out_shape,
        in_specs=in_specs,
        out_specs=jax.tree.map(lambda _: pl.BlockSpec(memory_space=pltpu.VMEM), out_shape),
        compiler_params=pltpu.CompilerParams(vmem_limit_bytes=VMEM_LIMIT),
        cost_estimate=pl.CostEstimate(flops=flops, bytes_accessed=moved, transcendentals=0),
    )(*operands)


def head_slices(width):
    return [(h, slice(h * HEAD_DIM, (h + 1) * HEAD_DIM)) for h in range(width // HEAD_DIM)]


def causal(count):
    rows = lax.broadcasted_iota(jnp.int32, (count, count), 0)
    cols = lax.broadcasted_iota(jnp.int32, (count, count), 1)
    return rows >= cols


def state_kernel(k_ref, v_ref, out_ref):
    for h, cols in head_slices(k_ref.shape[1]):
        out_ref[h] = dot_tn(k_ref[:, cols], v_ref[:, cols]).astype(bf16)


def total_kernel(parts_ref, out_ref):
    total = parts_ref[0].astype(f32)
    for j in range(1, parts_ref.shape[0]):
        total = total + parts_ref[j].astype(f32)
    total = total.astype(bf16)
    for j in range(out_ref.shape[0]):
        out_ref[j] = total


def running_kernel(reverse, place_ref, parts_ref, totals_ref, out_ref):
    place = place_ref[0]
    acc = jnp.zeros(out_ref.shape[1:], f32)
    for z in range(totals_ref.shape[0]):
        wanted = z > place if reverse else z < place
        acc = acc + jnp.where(wanted, totals_ref[z].astype(f32), 0.0)
    order = range(parts_ref.shape[0])
    for j in reversed(order) if reverse else order:
        out_ref[j] = acc.astype(bf16)
        acc = acc + parts_ref[j].astype(f32)


def local_kernel(q_ref, k_ref, v_ref, local_ref, inner_ref):
    mask = causal(q_ref.shape[0])
    for h, cols in head_slices(q_ref.shape[1]):
        scores = dot_nt(q_ref[:, cols], k_ref[:, cols])
        local = jnp.where(mask, scores, 0.0).astype(bf16)
        local_ref[h] = local
        inner_ref[:, cols] = dot_nn(local, v_ref[:, cols])


def mixed_kernel(q_ref, g_ref, inner_ref, prior_ref, attended_ref, dy_ref, state_ref):
    for h, cols in head_slices(q_ref.shape[1]):
        query = q_ref[:, cols]
        mixed = inner_ref[:, cols] + dot_nn(query, prior_ref[h])
        scale = lax.rsqrt(jnp.mean(mixed * mixed, axis=-1, keepdims=True) + 1e-06)
        attended_ref[:, cols] = (mixed * scale).astype(bf16)
        grad = g_ref[:, cols].astype(f32)
        inner_mean = jnp.mean(grad * mixed, axis=-1, keepdims=True)
        dy = (scale * grad - mixed * (scale * scale * scale * inner_mean)).astype(bf16)
        dy_ref[:, cols] = dy
        state_ref[h] = dot_tn(query, dy).astype(bf16)


def side_kernel(q_ref, k_ref, v_ref, dy_ref, local_ref, prior_ref, gq_ref, gk_ref, gv_ref):
    mask = causal(q_ref.shape[0])
    for h, cols in head_slices(q_ref.shape[1]):
        dy = dy_ref[:, cols]
        dlocal = jnp.where(mask, dot_nt(dy, v_ref[:, cols]), 0.0).astype(bf16)
        gq_ref[:, cols] = (
            dot_nn(dlocal, k_ref[:, cols]) + dot_nt(dy, prior_ref[h])
        ).astype(bf16)
        gk_ref[:, cols] = dot_tn(dlocal, q_ref[:, cols])
        gv_ref[:, cols] = dot_tn(local_ref[h], dy)


def last_kernel(k_ref, v_ref, gk_ref, gv_ref, later_ref, out_k_ref, out_v_ref):
    for h, cols in head_slices(k_ref.shape[1]):
        later = later_ref[h]
        out_k_ref[:, cols] = (gk_ref[:, cols] + dot_nt(v_ref[:, cols], later)).astype(bf16)
        out_v_ref[:, cols] = (gv_ref[:, cols] + dot_nn(k_ref[:, cols], later)).astype(bf16)


def scan_states(states, reverse):
    heads, dim, _ = states.shape
    peers = lax.axis_size("plane")
    planes = lax.axis_size("z")
    rows = heads * dim // peers
    place = lax.axis_index("z").astype(jnp.int32).reshape(1)
    parts = lax.all_to_all(states.reshape(peers, rows, dim), "plane", 0, 0, tiled=True)
    sent = call(total_kernel, jax.ShapeDtypeStruct((planes, rows, dim), bf16), (parts,))
    totals = lax.all_to_all(sent, "z", 0, 0, tiled=True)
    running = call(
        functools.partial(running_kernel, reverse),
        jax.ShapeDtypeStruct((peers, rows, dim), bf16),
        (place, parts, totals),
        smem=(0,),
    )
    back = lax.all_to_all(running, "plane", 0, 0, tiled=True)
    return back.reshape(heads, dim, dim)


def per_device(query, keys, values, grads):
    tokens, width = query.shape
    heads = width // HEAD_DIM
    wide = jax.ShapeDtypeStruct((tokens, width), f32)
    narrow = jax.ShapeDtypeStruct((tokens, width), bf16)
    state = jax.ShapeDtypeStruct((heads, HEAD_DIM, HEAD_DIM), bf16)
    square = jax.ShapeDtypeStruct((heads, tokens, tokens), bf16)
    unit = 2 * tokens * width * HEAD_DIM
    kv = call(state_kernel, state, (keys, values), unit)
    prior = scan_states(kv, False)
    local, inner = call(local_kernel, (square, wide), (query, keys, values), 2 * unit)
    attended, dy, gq = call(
        mixed_kernel, (narrow, narrow, state), (query, grads, inner, prior), 2 * unit
    )
    later = scan_states(gq, True)
    grad_query, gk_side, gv_side = call(
        side_kernel, (narrow, wide, wide), (query, keys, values, dy, local, prior), 5 * unit
    )
    grad_key, grad_value = call(
        last_kernel, (narrow, narrow), (keys, values, gk_side, gv_side, later), 2 * unit
    )
    return attended, grad_query, grad_key, grad_value


def solution(mesh):
    planes = 16
    split = Mesh(mesh.devices.reshape(planes, -1), ("z", "plane"))
    placed = P(("z", "plane"), None)
    return jax.shard_map(
        per_device,
        mesh=split,
        in_specs=(placed,) * 4,
        out_specs=(placed,) * 4,
        check_vma=False,
    )
```

time: 528 us -> 139 us (0.26)
  waiting for transfers between devices: 345 us -> 27.3 us
  other arithmetic: 61.6 us -> 0 us
  blocking collectives: 0 us -> 55.7 us
  starting transfers between devices: 57 us -> 31.7 us
  matrix products: 21.9 us -> 0 us
  local copies, waits for them, and re-layouts: 25 us -> 10.2 us
  between operations: 14.2 us -> 0.74 us
  Pallas kernels: 0 us -> 12.3 us
    all_gather x2 -> x0, waiting for transfers between devices: 297 us -> none  [entering(): gathered = lax.all_gather(part, axis)]
    add x63 -> x0, other arithmetic: 59.1 us -> none  [add_states(): return earlier + later_term]
    all_to_all x0 -> x3, blocking collectives: none -> 55.7 us  [the longest x2 36.4 us: scan_states(): lax.all_to_all(states.reshape(peers, rows, dim), 'plane', 0, 0, tiled=True)]
    all_to_all x8 -> x3, starting transfers between devices: 57 us -> 31.7 us  [the longest x2 18.1 us: scan_states(): back = lax.all_to_all(running, 'plane', 0, 0, tiled=True)]
    dot_general x12 -> x0, matrix products: 21.9 us -> none  [the longest x1 4.65 us: attend(): jnp.einsum('thd,shd->hts', query, keys, preferred_element_type=jnp.float32)]
    all_to_all x8 -> x3, waiting for transfers between devices: 47.5 us -> 27.3 us  [the longest x1 13.8 us: scan_states(): totals = lax.all_to_all(sent, 'z', 0, 0, tiled=True)]
    reshape x11 -> x0, local copies, waits for them, and re-layouts: 12.8 us -> none  [the longest x1 2.01 us: attend(): attended.reshape(outer_shape)]
    pallas_call x0 -> x9, Pallas kernels: none -> 12.3 us  [call(): pl.pallas_call(kernel, out_shape=out_shape, in_specs=in_specs, out_specs=...]
  transfers between devices with their start and end apart: 10 -> 3, of which waited for: 9 -> 3; matrix products, arithmetic and copies ran while one was open for 18% -> 0% of each run, Pallas kernels for 0% -> 4%
where the time goes in v1:
time: 139 us; the launch traced here: 138 us
  blocking collectives  55.7 us (40%)
  starting transfers between devices  31.7 us (23%)
  waiting for transfers between devices  27.3 us (20%)
  Pallas kernels  12.3 us (9%)
  local copies, waits for them, and re-layouts  10.2 us (7%)
    all_to_all x2, blocking collectives, scan_states(): lax.all_to_all(states.reshape(peers, rows, dim), 'plane', 0, 0, tiled=True)  36.4 us
    all_to_all x1, blocking collectives, scan_states(): totals = lax.all_to_all(sent, 'z', 0, 0, tiled=True)  19.3 us
    all_to_all x2, starting transfers between devices, scan_states(): back = lax.all_to_all(running, 'plane', 0, 0, tiled=True)  18.1 us
    all_to_all x1, waiting for transfers between devices, scan_states(): totals = lax.all_to_all(sent, 'z', 0, 0, tiled=True)  13.8 us
    all_to_all x1, starting transfers between devices, scan_states(): totals = lax.all_to_all(sent, 'z', 0, 0, tiled=True)  13.7 us
    all_to_all x2, waiting for transfers between devices, scan_states(): back = lax.all_to_all(running, 'plane', 0, 0, tiled=True)  13.5 us
    pallas_call x9, Pallas kernels, call(): pl.pallas_call(kernel, out_shape=out_shape, in_specs=in_specs, out_specs=...  12.3 us
    unnamed x28, local copies, waits for them, and re-layouts  10.2 us
  transfers between devices with their start and end apart: 3, of which 3 were waited for; matrix products, arithmetic and copies ran while one was open for 0% of the time, Pallas kernels for 4%

profile of v1, /device:TPU:1, one launch (start us, length us, event | category | flops | bytes accessed | tf_op | source)
XLA Modules:
  0.0 137.9 jit_solution(12947541868387370553)
XLA Ops:
  0.6 0.0 copy-start
  0.6 1.0 copy-done
  1.7 0.0 copy-start.2
  1.7 1.0 copy-done.2
  2.7 0.3 shard_map.76
  3.1 21.2 %all_to_all.30.parts_ref = bf16[32,64,128]{2,1,0:T(8,128)(2,1)S(1)} all-to-all(bf16[32,64,128]{2,1,0:T(8,128)(2,1)S(1)} %bitcast.8), channel_id=1, replica_groups=mesh['ctx'=64,'head'=8] {'ctx':(16)4,'head'}, dimensions={0} | all-to-all | bytes 1048576 | tf_op jit(solution)/shard_map/all_to_all | solution.py:128
  24.2 0.8 shard_map.77
  25.0 13.7 %all-to-all-start.1 = ((bf16[16,64,128]{2,1,0:T(8,128)(2,1)}), bf16[16,64,128]{2,1,0:T(8,128)(2,1)S(1)}, u32[]{:S(2)}, u32[]{:S(2)}) async-start(bf16[16,64,128]{2,1,0:T(8,128)(2,1)} %shard_map.77), calls=%async_computation.1 | async-start | bytes 524288 | tf_op jit(solution)/shard_map/all_to_all | solution.py:130
  38.7 13.8 %all-to-all-done.1.totals_ref = bf16[16,64,128]{2,1,0:T(8,128)(2,1)S(1)} async-done(((bf16[16,64,128]{2,1,0:T(8,128)(2,1)}), bf16[16,64,128]{2,1,0:T(8,128)(2,1)S(1)}, u32[]{:S(2)}, u32[]{:S(2)}) %all-to-all-start.1) | async-done | bytes 262176 | tf_op jit(solution)/shard_map/all_to_all | solution.py:130
  52.5 0.0 copy-start.4
  52.5 0.9 shard_map.78
  53.5 0.0 copy-start.1
  53.5 0.0 copy-start.3
  53.5 9.0 %all-to-all-start.2 = ((bf16[32,64,128]{2,1,0:T(8,128)(2,1)}), bf16[32,64,128]{2,1,0:T(8,128)(2,1)S(1)}, u32[]{:S(2)}, u32[]{:S(2)}) async-start(bf16[32,64,128]{2,1,0:T(8,128)(2,1)} %shard_map.78), calls=%async_computation.2 | async-start | bytes 1048576 | tf_op jit(solution)/shard_map/all_to_all | solution.py:137
  62.5 0.0 copy-done.4
  62.5 0.0 copy-done.1
  62.5 0.0 copy-done.3
  62.5 2.6 %shard_map.75 = (bf16[16,128,128]{2,1,0:T(8,128)(2,1)S(1)}, f32[128,2048]{1,0:T(8,128)S(1)}) custom-call(bf16[128,2048]{1,0:T(8,128)(2,1)S(1)} %copy-done.4, bf16[128,2048]{1,0:T(8,128)(2,1)S(1)} %copy-done.1, bf16[128,2048]{1,0:T(8,128)(2,1)S(1)} %copy-done.3), custom_call_target="tpu_custom_call" | custom-call | flops 134217728 | bytes 3145728 | tf_op jit(solution)/shard_map/pallas_call | solution.py:35
  65.1 0.0 copy-start.10
  65.1 0.8 copy-done.10
  65.9 8.3 %all-to-all-done.2 = bf16[32,64,128]{2,1,0:T(8,128)(2,1)S(1)} async-done(((bf16[32,64,128]{2,1,0:T(8,128)(2,1)}), bf16[32,64,128]{2,1,0:T(8,128)(2,1)S(1)}, u32[]{:S(2)}, u32[]{:S(2)}) %all-to-all-start.2) | async-done | bytes 524320 | tf_op jit(solution)/shard_map/all_to_all | solution.py:137
  74.2 0.0 copy-start.9
  74.2 1.0 copy-done.9
  75.2 1.7 %shard_map.79 = (bf16[128,2048]{1,0:T(8,128)(2,1)}, bf16[128,2048]{1,0:T(8,128)(2,1)S(1)}, bf16[16,128,128]{2,1,0:T(8,128)(2,1)S(1)}) custom-call(bf16[128,2048]{1,0:T(8,128)(2,1)S(1)} %copy-done.4, bf16[128,2048]{1,0:T(8,128)(2,1)S(1)} %copy-done.9, f32[128,2048]{1,0:T(8,128)S(1)} %get-tuple-element.14.inner_ref, bf16[16,128,128]{2,1,0:T(8,128)(2,1)S(1)} %bitcast.5), custom_call_target="tpu_custom_call" | custom-call | flops 134217728 | bytes 4194304 | tf_op jit(solution)/shard_map/pallas_call | solution.py:35
  76.9 0.0 copy-start.12
  76.9 0.8 copy-done.12
  77.7 15.2 %all_to_all.31.parts_ref = bf16[32,64,128]{2,1,0:T(8,128)(2,1)S(1)} all-to-all(bf16[32,64,128]{2,1,0:T(8,128)(2,1)S(1)} %bitcast.9), channel_id=1, replica_groups=mesh['ctx'=64,'head'=8] {'ctx':(16)4,'head'}, dimensions={0} | all-to-all | bytes 1048576 | tf_op jit(solution)/shard_map/all_to_all | solution.py:128
  92.9 0.1 shard_map.81
  93.0 19.3 %all_to_all.32.totals_ref = bf16[16,64,128]{2,1,0:T(8,128)(2,1)S(1)} all-to-all(bf16[16,64,128]{2,1,0:T(8,128)(2,1)S(1)} %shard_map.81), channel_id=1, replica_groups=mesh['ctx'=64,'head'=8] {'ctx':(1)16}, dimensions={0} | all-to-all | bytes 524288 | tf_op jit(solution)/shard_map/all_to_all | solution.py:130
  112.3 0.9 shard_map.82
  113.2 0.0 copy-start.11
  113.2 9.0 %all-to-all-start.5 = ((bf16[32,64,128]{2,1,0:T(8,128)(2,1)}), bf16[32,64,128]{2,1,0:T(8,128)(2,1)S(1)}, u32[]{:S(2)}, u32[]{:S(2)}) async-start(bf16[32,64,128]{2,1,0:T(8,128)(2,1)} %shard_map.82), calls=%async_computation.5 | async-start | bytes 1048576 | tf_op jit(solution)/shard_map/all_to_all | solution.py:137
  122.2 0.0 copy-done.11
  122.3 0.0 copy-start.13
  122.3 1.0 copy-done.13
  123.3 3.4 %shard_map.80 = (bf16[128,2048]{1,0:T(8,128)(2,1)}, f32[128,2048]{1,0:T(8,128)S(1)}, f32[128,2048]{1,0:T(8,128)S(1)}) custom-call(bf16[128,2048]{1,0:T(8,128)(2,1)S(1)} %copy-done.4, bf16[128,2048]{1,0:T(8,128)(2,1)S(1)} %copy-done.1, bf16[128,2048]{1,0:T(8,128)(2,1)S(1)} %copy-done.3, bf16[128,2048]{1,0:T(8,128)(2,1)S(1)} %copy-done.13, ...), custom_call_target="tpu_custom_call" | custom-call | flops 335544320 | bytes 5767168 | tf_op jit(solution)/shard_map/pallas_call | solution.py:35
  126.7 0.0 copy-start.5
  126.7 1.0 copy-done.5
  127.7 0.0 copy-start.7
  127.7 1.0 copy-done.7
  128.6 5.3 %all-to-all-done.5 = bf16[32,64,128]{2,1,0:T(8,128)(2,1)S(1)} async-done(((bf16[32,64,128]{2,1,0:T(8,128)(2,1)}), bf16[32,64,128]{2,1,0:T(8,128)(2,1)S(1)}, u32[]{:S(2)}, u32[]{:S(2)}) %all-to-all-start.5) | async-done | bytes 524320 | tf_op jit(solution)/shard_map/all_to_all | solution.py:137
  133.9 0.0 copy-start.6
  133.9 1.2 copy-done.6
  135.1 0.0 copy-start.8
  135.1 1.2 copy-done.8
  136.4 1.6 %shard_map.83 = (bf16[128,2048]{1,0:T(8,128)(2,1)}, bf16[128,2048]{1,0:T(8,128)(2,1)}) custom-call(bf16[128,2048]{1,0:T(8,128)(2,1)S(1)} %copy-done.1, bf16[128,2048]{1,0:T(8,128)(2,1)S(1)} %copy-done.3, f32[128,2048]{1,0:T(8,128)S(1)} %copy-done.6, f32[128,2048]{1,0:T(8,128)S(1)} %copy-done.8, bf16[16,128,128]{2,1,0:T(8,128)(2,1)S(1)} %bitcast.7), custom_call_target="tpu_custom_call" | custom-call | flops 134217728 | bytes 4718592 | tf_op jit(solution)/shard_map/pallas_call | solution.py:35
Async XLA Ops:
  0.6 1.0 copy-start
  1.7 1.0 copy-start.2
  25.0 27.5 %all-to-all-start.1 = ((bf16[16,64,128]{2,1,0:T(8,128)(2,1)}), bf16[16,64,128]{2,1,0:T(8,128)(2,1)S(1)}, u32[]{:S(2)}, u32[]{:S(2)}) async-start(bf16[16,64,128]{2,1,0:T(8,128)(2,1)} %shard_map.77), calls=%async_computation.1 | async-start | bytes 524288 | tf_op jit(solution)/shard_map/all_to_all | solution.py:130
  52.5 10.0 %copy-start.4 = (bf16[128,2048]{1,0:T(8,128)(2,1)S(1)}, bf16[128,2048]{1,0:T(8,128)(2,1)}, u32[]{:S(2)}) copy-start(bf16[128,2048]{1,0:T(8,128)(2,1)} %q_ref.5) | copy-start | bytes 1572868
  53.5 9.1 %copy-start.1 = (bf16[128,2048]{1,0:T(8,128)(2,1)S(1)}, bf16[128,2048]{1,0:T(8,128)(2,1)}, u32[]{:S(2)}) copy-start(bf16[128,2048]{1,0:T(8,128)(2,1)} %k_ref.7) | copy-start | bytes 1572868
  53.5 9.1 %copy-start.3 = (bf16[128,2048]{1,0:T(8,128)(2,1)S(1)}, bf16[128,2048]{1,0:T(8,128)(2,1)}, u32[]{:S(2)}) copy-start(bf16[128,2048]{1,0:T(8,128)(2,1)} %v_ref.7) | copy-start | bytes 1572868
  53.5 20.7 %all-to-all-start.2 = ((bf16[32,64,128]{2,1,0:T(8,128)(2,1)}), bf16[32,64,128]{2,1,0:T(8,128)(2,1)S(1)}, u32[]{:S(2)}, u32[]{:S(2)}) async-start(bf16[32,64,128]{2,1,0:T(8,128)(2,1)} %shard_map.78), calls=%async_computation.2 | async-start | bytes 1048576 | tf_op jit(solution)/shard_map/all_to_all | solution.py:137
  65.1 0.8 copy-start.10
  74.2 1.0 copy-start.9
  76.9 0.8 copy-start.12
  113.2 9.0 %copy-start.11 = (bf16[16,128,128]{2,1,0:T(8,128)(2,1)S(1)}, bf16[16,128,128]{2,1,0:T(8,128)(2,1)}, u32[]{:S(2)}) copy-start(bf16[16,128,128]{2,1,0:T(8,128)(2,1)} %copy-done.10) | copy-start | bytes 1572868
  113.2 20.7 %all-to-all-start.5 = ((bf16[32,64,128]{2,1,0:T(8,128)(2,1)}), bf16[32,64,128]{2,1,0:T(8,128)(2,1)S(1)}, u32[]{:S(2)}, u32[]{:S(2)}) async-start(bf16[32,64,128]{2,1,0:T(8,128)(2,1)} %shard_map.82), calls=%async_computation.5 | async-start | bytes 1048576 | tf_op jit(solution)/shard_map/all_to_all | solution.py:137
  122.3 1.0 copy-start.13
  126.7 1.0 copy-start.5
  127.7 1.0 copy-start.7
  133.9 1.2 copy-start.6
  135.1 1.2 copy-start.8

commit v2 on v1

--- a/solution.py
+++ b/solution.py
@@ -8,7 +8,7 @@
 from jax.sharding import Mesh, PartitionSpec as P
 
 HEAD_DIM = 128
-VMEM_LIMIT = 48 * 1024 * 1024
+VMEM_LIMIT = 16 * 1024 * 1024
 f32 = jnp.float32
 bf16 = jnp.bfloat16
 
@@ -69,9 +69,9 @@
 def running_kernel(reverse, place_ref, parts_ref, totals_ref, out_ref):
     place = place_ref[0]
     acc = jnp.zeros(out_ref.shape[1:], f32)
-    for z in range(totals_ref.shape[0]):
-        wanted = z > place if reverse else z < place
-        acc = acc + jnp.where(wanted, totals_ref[z].astype(f32), 0.0)
+    for b in range(totals_ref.shape[0]):
+        wanted = b > place if reverse else b < place
+        acc = acc + jnp.where(wanted, totals_ref[b].astype(f32), 0.0)
     order = range(parts_ref.shape[0])
     for j in reversed(order) if reverse else order:
         out_ref[j] = acc.astype(bf16)
@@ -87,12 +87,12 @@
         inner_ref[:, cols] = dot_nn(local, v_ref[:, cols])
 
 
-def mixed_kernel(q_ref, g_ref, inner_ref, prior_ref, attended_ref, dy_ref, state_ref):
+def mixed_kernel(q_ref, g_ref, inner_ref, prior_ref, normed_ref, dy_ref, state_ref):
     for h, cols in head_slices(q_ref.shape[1]):
         query = q_ref[:, cols]
         mixed = inner_ref[:, cols] + dot_nn(query, prior_ref[h])
         scale = lax.rsqrt(jnp.mean(mixed * mixed, axis=-1, keepdims=True) + 1e-06)
-        attended_ref[:, cols] = (mixed * scale).astype(bf16)
+        normed_ref[:, cols] = (mixed * scale).astype(bf16)
         grad = g_ref[:, cols].astype(f32)
         inner_mean = jnp.mean(grad * mixed, axis=-1, keepdims=True)
         dy = (scale * grad - mixed * (scale * scale * scale * inner_mean)).astype(bf16)
@@ -100,7 +100,10 @@
         state_ref[h] = dot_tn(query, dy).astype(bf16)
 
 
-def side_kernel(q_ref, k_ref, v_ref, dy_ref, local_ref, prior_ref, gq_ref, gk_ref, gv_ref):
+def side_kernel(
+    q_ref, k_ref, v_ref, dy_ref, local_ref, prior_ref, normed_ref, gq_ref, gk_ref, gv_ref, attended_ref
+):
+    attended_ref[...] = normed_ref[...]
     mask = causal(q_ref.shape[0])
     for h, cols in head_slices(q_ref.shape[1]):
         dy = dy_ref[:, cols]
@@ -121,20 +124,20 @@
 
 def scan_states(states, reverse):
     heads, dim, _ = states.shape
-    peers = lax.axis_size("plane")
-    planes = lax.axis_size("z")
+    peers = lax.axis_size("inner")
+    blocks = lax.axis_size("outer")
     rows = heads * dim // peers
-    place = lax.axis_index("z").astype(jnp.int32).reshape(1)
-    parts = lax.all_to_all(states.reshape(peers, rows, dim), "plane", 0, 0, tiled=True)
-    sent = call(total_kernel, jax.ShapeDtypeStruct((planes, rows, dim), bf16), (parts,))
-    totals = lax.all_to_all(sent, "z", 0, 0, tiled=True)
+    place = lax.axis_index("outer").astype(jnp.int32).reshape(1)
+    parts = lax.all_to_all(states.reshape(peers, rows, dim), "inner", 0, 0, tiled=True)
+    sent = call(total_kernel, jax.ShapeDtypeStruct((blocks, rows, dim), bf16), (parts,))
+    totals = lax.all_to_all(sent, "outer", 0, 0, tiled=True)
     running = call(
         functools.partial(running_kernel, reverse),
         jax.ShapeDtypeStruct((peers, rows, dim), bf16),
         (place, parts, totals),
         smem=(0,),
     )
-    back = lax.all_to_all(running, "plane", 0, 0, tiled=True)
+    back = lax.all_to_all(running, "inner", 0, 0, tiled=True)
     return back.reshape(heads, dim, dim)
 
 
@@ -149,12 +152,15 @@
     kv = call(state_kernel, state, (keys, values), unit)
     prior = scan_states(kv, False)
     local, inner = call(local_kernel, (square, wide), (query, keys, values), 2 * unit)
-    attended, dy, gq = call(
+    normed, dy, gq = call(
         mixed_kernel, (narrow, narrow, state), (query, grads, inner, prior), 2 * unit
     )
     later = scan_states(gq, True)
-    grad_query, gk_side, gv_side = call(
-        side_kernel, (narrow, wide, wide), (query, keys, values, dy, local, prior), 5 * unit
+    grad_query, gk_side, gv_side, attended = call(
+        side_kernel,
+        (narrow, wide, wide, narrow),
+        (query, keys, values, dy, local, prior, normed),
+        5 * unit,
     )
     grad_key, grad_value = call(
         last_kernel, (narrow, narrow), (keys, values, gk_side, gv_side, later), 2 * unit
@@ -163,9 +169,8 @@
 
 
 def solution(mesh):
-    planes = 16
-    split = Mesh(mesh.devices.reshape(planes, -1), ("z", "plane"))
-    placed = P(("z", "plane"), None)
+    split = Mesh(mesh.devices.reshape(-1, 64), ("outer", "inner"))
+    placed = P(("outer", "inner"), None)
     return jax.shard_map(
         per_device,
         mesh=split,

time: 139 us -> 132 us (0.950)
  starting transfers between devices: 31.7 us -> 27.8 us
  blocking collectives: 55.7 us -> 53.4 us
  waiting for transfers between devices: 27.3 us -> 25.4 us
  local copies, waits for them, and re-layouts: 10.2 us -> 12 us
    all_to_all x3, starting transfers between devices: 31.7 us -> 27.8 us  [the longest x2 13.9 us: scan_states(): back = lax.all_to_all(running, 'inner', 0, 0, tiled=True)]
    all_to_all x3, blocking collectives: 55.7 us -> 53.4 us  [the longest x2 39.1 us: scan_states(): lax.all_to_all(states.reshape(peers, rows, dim), 'inner', 0, 0, tiled=True)]
    all_to_all x3, waiting for transfers between devices: 27.3 us -> 25.4 us  [the longest x2 13.3 us: scan_states(): back = lax.all_to_all(running, 'inner', 0, 0, tiled=True)]
    unnamed x28 -> x32, local copies, waits for them, and re-layouts: 10.2 us -> 12 us
  transfers between devices with their start and end apart: 3 -> 3, of which waited for: 3 -> 3; matrix products, arithmetic and copies ran while one was open for 0% -> 0% of each run, Pallas kernels for 4% -> 5%
where the time goes in v2:
time: 132 us; the launch traced here: 131 us
  blocking collectives  53.4 us (40%)
  starting transfers between devices  27.8 us (21%)
  waiting for transfers between devices  25.4 us (19%)
  local copies, waits for them, and re-layouts  12 us (9%)
  Pallas kernels  11.7 us (9%)
    all_to_all x2, blocking collectives, scan_states(): lax.all_to_all(states.reshape(peers, rows, dim), 'inner', 0, 0, tiled=True)  39.1 us
    all_to_all x1, blocking collectives, scan_states(): totals = lax.all_to_all(sent, 'outer', 0, 0, tiled=True)  14.3 us
    all_to_all x2, starting transfers between devices, scan_states(): back = lax.all_to_all(running, 'inner', 0, 0, tiled=True)  13.9 us
    all_to_all x1, starting transfers between devices, scan_states(): totals = lax.all_to_all(sent, 'outer', 0, 0, tiled=True)  13.8 us
    all_to_all x2, waiting for transfers between devices, scan_states(): back = lax.all_to_all(running, 'inner', 0, 0, tiled=True)  13.3 us
    all_to_all x1, waiting for transfers between devices, scan_states(): totals = lax.all_to_all(sent, 'outer', 0, 0, tiled=True)  12 us
    unnamed x32, local copies, waits for them, and re-layouts  12 us
    pallas_call x9, Pallas kernels, call(): pl.pallas_call(kernel, out_shape=out_shape, in_specs=in_specs, out_specs=...  11.7 us
  transfers between devices with their start and end apart: 3, of which 3 were waited for; matrix products, arithmetic and copies ran while one was open for 0% of the time, Pallas kernels for 5%

profile of v2, /device:TPU:1, one launch (start us, length us, event | category | flops | bytes accessed | tf_op | source)
XLA Modules:
  0.0 131.0 jit_solution(5601668062355927299)
XLA Ops:
  0.6 0.0 copy-start
  0.6 1.0 copy-done
  1.7 0.0 copy-start.2
  1.7 1.0 copy-done.2
  2.7 0.3 shard_map.76
  3.1 22.4 %all_to_all.30.parts_ref = bf16[64,32,128]{2,1,0:T(8,128)(2,1)S(1)} all-to-all(bf16[64,32,128]{2,1,0:T(8,128)(2,1)S(1)} %bitcast.8), channel_id=1, replica_groups=mesh['ctx'=64,'head'=8] {'ctx':(8)8,'head'}, dimensions={0} | all-to-all | bytes 1048576 | tf_op jit(solution)/shard_map/all_to_all | solution.py:131
  25.5 0.7 shard_map.77
  26.2 13.8 %all-to-all-start.1 = ((bf16[8,32,128]{2,1,0:T(8,128)(2,1)}), bf16[8,32,128]{2,1,0:T(8,128)(2,1)S(1)}, u32[]{:S(2)}, u32[]{:S(2)}) async-start(bf16[8,32,128]{2,1,0:T(8,128)(2,1)} %shard_map.77), calls=%async_computation.1 | async-start | bytes 131072 | tf_op jit(solution)/shard_map/all_to_all | solution.py:133
  40.0 12.0 %all-to-all-done.1.totals_ref = bf16[8,32,128]{2,1,0:T(8,128)(2,1)S(1)} async-done(((bf16[8,32,128]{2,1,0:T(8,128)(2,1)}), bf16[8,32,128]{2,1,0:T(8,128)(2,1)S(1)}, u32[]{:S(2)}, u32[]{:S(2)}) %all-to-all-start.1) | async-done | bytes 65568 | tf_op jit(solution)/shard_map/all_to_all | solution.py:133
  52.1 0.0 copy-start.4
  52.1 0.9 shard_map.78
  52.9 0.0 copy-start.1
  53.0 0.0 copy-start.3
  53.0 6.9 %all-to-all-start.2 = ((bf16[64,32,128]{2,1,0:T(8,128)(2,1)}), bf16[64,32,128]{2,1,0:T(8,128)(2,1)S(1)}, u32[]{:S(2)}, u32[]{:S(2)}) async-start(bf16[64,32,128]{2,1,0:T(8,128)(2,1)} %shard_map.78), calls=%async_computation.2 | async-start | bytes 1048576 | tf_op jit(solution)/shard_map/all_to_all | solution.py:140
  59.9 0.0 copy-done.4
  59.9 0.0 copy-done.1
  59.9 0.0 copy-done.3
  59.9 2.6 %shard_map.75 = (bf16[16,128,128]{2,1,0:T(8,128)(2,1)S(1)}, f32[128,2048]{1,0:T(8,128)S(1)}) custom-call(bf16[128,2048]{1,0:T(8,128)(2,1)S(1)} %copy-done.4, bf16[128,2048]{1,0:T(8,128)(2,1)S(1)} %copy-done.1, bf16[128,2048]{1,0:T(8,128)(2,1)S(1)} %copy-done.3), custom_call_target="tpu_custom_call" | custom-call | flops 134217728 | bytes 3145728 | tf_op jit(solution)/shard_map/pallas_call | solution.py:35
  62.5 0.0 copy-start.10
  62.5 0.8 copy-done.10
  63.3 8.8 %all-to-all-done.2 = bf16[64,32,128]{2,1,0:T(8,128)(2,1)S(1)} async-done(((bf16[64,32,128]{2,1,0:T(8,128)(2,1)}), bf16[64,32,128]{2,1,0:T(8,128)(2,1)S(1)}, u32[]{:S(2)}, u32[]{:S(2)}) %all-to-all-start.2) | async-done | bytes 524320 | tf_op jit(solution)/shard_map/all_to_all | solution.py:140
  72.1 0.0 copy-start.9
  72.1 1.0 copy-done.9
  73.1 1.1 shard_map.79
  74.2 0.0 copy-start.12
  74.2 0.8 copy-done.12
  75.0 0.0 copy-start.14
  75.0 0.8 copy-done.14
  75.8 16.7 %all_to_all.31.parts_ref = bf16[64,32,128]{2,1,0:T(8,128)(2,1)S(1)} all-to-all(bf16[64,32,128]{2,1,0:T(8,128)(2,1)S(1)} %bitcast.9), channel_id=1, replica_groups=mesh['ctx'=64,'head'=8] {'ctx':(8)8,'head'}, dimensions={0} | all-to-all | bytes 1048576 | tf_op jit(solution)/shard_map/all_to_all | solution.py:131
  92.5 0.1 shard_map.81
  92.6 14.3 %all_to_all.32.totals_ref = bf16[8,32,128]{2,1,0:T(8,128)(2,1)S(1)} all-to-all(bf16[8,32,128]{2,1,0:T(8,128)(2,1)S(1)} %shard_map.81), channel_id=1, replica_groups=mesh['ctx'=64,'head'=8] {'ctx':(1)8}, dimensions={0} | all-to-all | bytes 131072 | tf_op jit(solution)/shard_map/all_to_all | solution.py:133
  106.9 0.9 shard_map.82
  107.8 0.0 copy-start.11
  107.8 7.0 %all-to-all-start.5 = ((bf16[64,32,128]{2,1,0:T(8,128)(2,1)}), bf16[64,32,128]{2,1,0:T(8,128)(2,1)S(1)}, u32[]{:S(2)}, u32[]{:S(2)}) async-start(bf16[64,32,128]{2,1,0:T(8,128)(2,1)} %shard_map.82), calls=%async_computation.5 | async-start | bytes 1048576 | tf_op jit(solution)/shard_map/all_to_all | solution.py:140
  114.8 0.0 copy-done.11
  114.8 0.0 copy-start.13
  114.8 1.0 copy-done.13
  115.8 0.0 copy-start.15
  115.8 1.0 copy-done.15
  116.9 3.5 %shard_map.80 = (bf16[128,2048]{1,0:T(8,128)(2,1)}, f32[128,2048]{1,0:T(8,128)S(1)}, f32[128,2048]{1,0:T(8,128)S(1)}, bf16[128,2048]{1,0:T(8,128)(2,1)}) custom-call(bf16[128,2048]{1,0:T(8,128)(2,1)S(1)} %copy-done.4, bf16[128,2048]{1,0:T(8,128)(2,1)S(1)} %copy-done.1, bf16[128,2048]{1,0:T(8,128)(2,1)S(1)} %copy-done.3, bf16[128,2048]{1,0:T(8,128)(2,1)S(1)} %copy-done.15, ...), custom_call_target="tpu_custom_call" | custom-call | flops 335544320 | bytes 6815744 | tf_op jit(solution)/shard_map/pallas_call | solution.py:35
  120.4 0.0 copy-start.5
  120.4 1.0 copy-done.5
  121.4 0.0 copy-start.7
  121.4 1.0 copy-done.7
  122.4 4.6 %all-to-all-done.5 = bf16[64,32,128]{2,1,0:T(8,128)(2,1)S(1)} async-done(((bf16[64,32,128]{2,1,0:T(8,128)(2,1)}), bf16[64,32,128]{2,1,0:T(8,128)(2,1)S(1)}, u32[]{:S(2)}, u32[]{:S(2)}) %all-to-all-start.5) | async-done | bytes 524320 | tf_op jit(solution)/shard_map/all_to_all | solution.py:140
  127.0 0.0 copy-start.6
  127.0 1.2 copy-done.6
  128.2 0.0 copy-start.8
  128.2 1.2 copy-done.8
  129.4 1.6 %shard_map.83 = (bf16[128,2048]{1,0:T(8,128)(2,1)}, bf16[128,2048]{1,0:T(8,128)(2,1)}) custom-call(bf16[128,2048]{1,0:T(8,128)(2,1)S(1)} %copy-done.1, bf16[128,2048]{1,0:T(8,128)(2,1)S(1)} %copy-done.3, f32[128,2048]{1,0:T(8,128)S(1)} %copy-done.6, f32[128,2048]{1,0:T(8,128)S(1)} %copy-done.8, bf16[16,128,128]{2,1,0:T(8,128)(2,1)S(1)} %bitcast.7), custom_call_target="tpu_custom_call" | custom-call | flops 134217728 | bytes 4718592 | tf_op jit(solution)/shard_map/pallas_call | solution.py:35
Async XLA Ops:
  0.6 1.0 copy-start
  1.7 1.0 copy-start.2
  26.2 25.9 %all-to-all-start.1 = ((bf16[8,32,128]{2,1,0:T(8,128)(2,1)}), bf16[8,32,128]{2,1,0:T(8,128)(2,1)S(1)}, u32[]{:S(2)}, u32[]{:S(2)}) async-start(bf16[8,32,128]{2,1,0:T(8,128)(2,1)} %shard_map.77), calls=%async_computation.1 | async-start | bytes 131072 | tf_op jit(solution)/shard_map/all_to_all | solution.py:133
  52.1 7.9 %copy-start.4 = (bf16[128,2048]{1,0:T(8,128)(2,1)S(1)}, bf16[128,2048]{1,0:T(8,128)(2,1)}, u32[]{:S(2)}) copy-start(bf16[128,2048]{1,0:T(8,128)(2,1)} %q_ref.5) | copy-start | bytes 1572868
  52.9 7.0 %copy-start.1 = (bf16[128,2048]{1,0:T(8,128)(2,1)S(1)}, bf16[128,2048]{1,0:T(8,128)(2,1)}, u32[]{:S(2)}) copy-start(bf16[128,2048]{1,0:T(8,128)(2,1)} %k_ref.7) | copy-start | bytes 1572868
  53.0 7.0 %copy-start.3 = (bf16[128,2048]{1,0:T(8,128)(2,1)S(1)}, bf16[128,2048]{1,0:T(8,128)(2,1)}, u32[]{:S(2)}) copy-start(bf16[128,2048]{1,0:T(8,128)(2,1)} %v_ref.7) | copy-start | bytes 1572868
  53.0 19.1 %all-to-all-start.2 = ((bf16[64,32,128]{2,1,0:T(8,128)(2,1)}), bf16[64,32,128]{2,1,0:T(8,128)(2,1)S(1)}, u32[]{:S(2)}, u32[]{:S(2)}) async-start(bf16[64,32,128]{2,1,0:T(8,128)(2,1)} %shard_map.78), calls=%async_computation.2 | async-start | bytes 1048576 | tf_op jit(solution)/shard_map/all_to_all | solution.py:140
  62.5 0.8 copy-start.10
  72.1 1.0 copy-start.9
  74.2 0.8 copy-start.12
  75.0 0.8 copy-start.14
  107.8 7.0 %copy-start.11 = (bf16[16,128,128]{2,1,0:T(8,128)(2,1)S(1)}, bf16[16,128,128]{2,1,0:T(8,128)(2,1)}, u32[]{:S(2)}) copy-start(bf16[16,128,128]{2,1,0:T(8,128)(2,1)} %copy-done.10) | copy-start | bytes 1572868
  107.8 19.2 %all-to-all-start.5 = ((bf16[64,32,128]{2,1,0:T(8,128)(2,1)}), bf16[64,32,128]{2,1,0:T(8,128)(2,1)S(1)}, u32[]{:S(2)}, u32[]{:S(2)}) async-start(bf16[64,32,128]{2,1,0:T(8,128)(2,1)} %shard_map.82), calls=%async_computation.5 | async-start | bytes 1048576 | tf_op jit(solution)/shard_map/all_to_all | solution.py:140
  114.8 1.0 copy-start.13
  115.8 1.0 copy-start.15
  120.4 1.0 copy-start.5
  121.4 1.0 copy-start.7
  127.0 1.2 copy-start.6
  128.2 1.2 copy-start.8

commit v3 on v2

v3 whole, which is shorter than its diff:
```python
import functools

import jax
import jax.numpy as jnp
from jax import lax
from jax.experimental import pallas as pl
from jax.experimental.pallas import tpu as pltpu
from jax.sharding import Mesh, PartitionSpec as P

HEAD_DIM = 128
GROUP = 512
MIB = 1024 * 1024
LARGE = 56 * MIB
STATE_LIMIT = 53 * MIB
MIXED_LIMIT = 52 * MIB
LAST_LIMIT = 52 * MIB
SMALL = 16 * MIB
f32 = jnp.float32
bf16 = jnp.bfloat16


def dot_nn(a, b):
    return lax.dot_general(a, b, (((1,), (0,)), ((), ())), preferred_element_type=f32)


def dot_nt(a, b):
    return lax.dot_general(a, b, (((1,), (1,)), ((), ())), preferred_element_type=f32)


def dot_tn(a, b):
    return lax.dot_general(a, b, (((0,), (0,)), ((), ())), preferred_element_type=f32)


def shape(*dims, dtype=bf16):
    return jax.ShapeDtypeStruct(dims, dtype)


def call(kernel, out_shape, operands, limit, flops=0, far=(), far_out=(), smem=(), scratch=()):
    def space(i, kept):
        return pl.BlockSpec(memory_space=pltpu.HBM if i in kept else pltpu.VMEM)

    in_specs = [
        pl.BlockSpec(memory_space=pltpu.SMEM) if i in smem else space(i, far)
        for i in range(len(operands))
    ]
    out_specs = tuple(space(i, far_out) for i in range(len(out_shape)))
    moved = sum(x.size * x.dtype.itemsize for x in tuple(operands) + out_shape)
    return pl.pallas_call(
        kernel,
        out_shape=out_shape,
        in_specs=in_specs,
        out_specs=out_specs,
        scratch_shapes=scratch,
        compiler_params=pltpu.CompilerParams(vmem_limit_bytes=limit),
        cost_estimate=pl.CostEstimate(flops=flops, bytes_accessed=moved, transcendentals=0),
    )(*operands)


def copies_of(pairs, sems, first=0):
    return [
        pltpu.make_async_copy(src, dst, sems.at[first + i]) for i, (src, dst) in enumerate(pairs)
    ]


def start_all(copies):
    for copy in copies:
        copy.start()


def wait_all(copies):
    for copy in copies:
        copy.wait()


def cut(ref, g):
    return ref.at[:, pl.ds(g * GROUP, GROUP)]


def grouped(pairs, sems):
    count = pairs[0][0].shape[1] // GROUP
    return [
        copies_of([(cut(src, g), cut(dst, g)) for src, dst in pairs], sems, g * len(pairs))
        for g in range(count)
    ]


def group_heads(g):
    heads = range(g * GROUP // HEAD_DIM, (g + 1) * GROUP // HEAD_DIM)
    return [(h, slice(h * HEAD_DIM, (h + 1) * HEAD_DIM)) for h in heads]


def half(ref, which):
    count = ref.shape[-1] // 2
    return ref.at[:, pl.ds(pl.multiple_of(which * count, count), count)]


def causal(count):
    rows = lax.broadcasted_iota(jnp.int32, (count, count), 0)
    cols = lax.broadcasted_iota(jnp.int32, (count, count), 1)
    return rows >= cols


def state_kernel(k_far, v_far, out_ref, k_ref, v_ref, sems):
    pairs, rows, _ = out_ref.shape
    cuts = HEAD_DIM // rows
    heads = pairs // cuts // 2
    copies = grouped([(k_far, k_ref), (v_far, v_ref)], sems)
    for group in copies:
        start_all(group)
    for g, group in enumerate(copies):
        wait_all(group)
        for h, cols in group_heads(g):
            state = dot_tn(k_ref[:, cols], v_ref[:, cols]).astype(bf16)
            for q in range(cuts):
                place = 2 * ((h % heads) * cuts + q) + h // heads
                out_ref[place] = state[q * rows : (q + 1) * rows]


def total_kernel(parts_ref, *refs):
    out_ref = refs[-1]
    total = parts_ref[0].astype(f32)
    for j in range(1, parts_ref.shape[0]):
        total = total + parts_ref[j].astype(f32)
    total = total.astype(bf16)
    for j in range(out_ref.shape[0]):
        out_ref[j] = total


def outer_sum(reverse, place, totals_ref):
    acc = jnp.zeros(totals_ref.shape[1:], f32)
    for b in range(totals_ref.shape[0]):
        wanted = b > place if reverse else b < place
        acc = acc + jnp.where(wanted, totals_ref[b].astype(f32), 0.0)
    return acc


def prior_kernel(place_ref, parts_ref, totals_ref, token_ref, out_ref):
    acc = outer_sum(False, place_ref[0], totals_ref)
    for r in range(out_ref.shape[0]):
        out_ref[r] = acc.astype(bf16)
        acc = acc + parts_ref[2 * r].astype(f32) + parts_ref[2 * r + 1].astype(f32)


def later_kernel(place_ref, parts_ref, totals_ref, token_ref, out_ref):
    acc = outer_sum(True, place_ref[0], totals_ref)
    for r in reversed(range(parts_ref.shape[0])):
        out_ref[2 * r] = acc.astype(bf16)
        out_ref[2 * r + 1] = acc.astype(bf16)
        acc = acc + parts_ref[r].astype(f32)


def pack_kernel(core_ref, q_far, k_far, v_far, g_far, out_ref, token_ref, sems):
    other = 1 - core_ref[0]
    rows = (q_far, k_far, v_far, g_far)
    copies = copies_of([(half(src, other), out_ref.at[i]) for i, src in enumerate(rows)], sems)
    start_all(copies)
    token_ref[...] = jnp.zeros_like(token_ref)
    wait_all(copies)


def local_kernel(
    core_ref, q_far, k_far, v_far, g_far, recv_far,
    inner_ref, qg_ref, kv_ref, token_ref, sems,
):
    core = core_ref[0]
    count = q_far.shape[0]
    mine = pl.ds(pl.multiple_of(core * count, count), count)
    theirs = pl.ds(pl.multiple_of((1 - core) * count, count), count)
    q_ref, k_ref, v_ref = qg_ref.at[0], kv_ref.at[0], kv_ref.at[1]
    near = (q_ref, k_ref, v_ref, qg_ref.at[1])
    copies = copies_of(
        [(half(src, core), dst.at[mine]) for src, dst in zip((q_far, k_far, v_far, g_far), near)]
        + [(recv_far.at[i], dst.at[theirs]) for i, dst in enumerate(near)],
        sems,
    )
    start_all(copies)
    token_ref[...] = jnp.zeros_like(token_ref)
    wait_all(copies)
    mask = causal(2 * count)
    for g in range(q_ref.shape[1] // GROUP):
        for h, cols in group_heads(g):
            scores = dot_nt(q_ref[:, cols], k_ref[:, cols])
            local = jnp.where(mask, scores, 0.0).astype(bf16)
            inner_ref[:, cols] = dot_nn(local, v_ref[:, cols])


def whole_state(ref, h):
    cuts = HEAD_DIM // ref.shape[1]
    return jnp.concatenate([ref[h * cuts + q] for q in range(cuts)], axis=0)


def normed_parts(mixed, grad):
    scale = lax.rsqrt(jnp.mean(mixed * mixed, axis=-1, keepdims=True) + 1e-06)
    inner_mean = jnp.mean(grad * mixed, axis=-1, keepdims=True)
    dy = (scale * grad - mixed * (scale * scale * scale * inner_mean)).astype(bf16)
    return scale, dy


def mixed_kernel(qg_far, inner_ref, prior_ref, state_ref, qg_ref, sems):
    rows = state_ref.shape[1]
    cuts = HEAD_DIM // rows
    q_ref, g_ref = qg_ref.at[0], qg_ref.at[1]
    copies = grouped([(qg_far.at[i], qg_ref.at[i]) for i in range(2)], sems)
    for group in copies:
        start_all(group)
    for g, group in enumerate(copies):
        wait_all(group)
        for h, cols in group_heads(g):
            query = q_ref[:, cols]
            mixed = inner_ref[:, cols] + dot_nn(query, whole_state(prior_ref, h))
            _, dy = normed_parts(mixed, g_ref[:, cols].astype(f32))
            state = dot_tn(query, dy).astype(bf16)
            for q in range(cuts):
                state_ref[h * cuts + q] = state[q * rows : (q + 1) * rows]


def side_kernel(
    core_ref, qg_far, kv_far, inner_far, prior_far, own_ref, send_ref, token_ref,
    qg_ref, kv_ref, inner_ref, prior_ref, tile_ref, sems, prior_sem,
):
    core = core_ref[0]
    count = own_ref.shape[1]
    q_ref, g_ref, k_ref, v_ref = qg_ref.at[0], qg_ref.at[1], kv_ref.at[0], kv_ref.at[1]
    copies = grouped(
        [(qg_far.at[i], qg_ref.at[i]) for i in range(2)]
        + [(kv_far.at[i], kv_ref.at[i]) for i in range(2)]
        + [(inner_far, inner_ref)],
        sems,
    )
    prior_copy = copies_of([(prior_far, prior_ref)], prior_sem)
    start_all(prior_copy)
    for group in copies:
        start_all(group)
    token_ref[...] = jnp.zeros_like(token_ref)
    mask = causal(2 * count)
    wait_all(prior_copy)
    for g, group in enumerate(copies):
        wait_all(group)
        for h, cols in group_heads(g):
            query, key, value = q_ref[:, cols], k_ref[:, cols], v_ref[:, cols]
            prior = whole_state(prior_ref, h)
            local = jnp.where(mask, dot_nt(query, key), 0.0).astype(bf16)
            mixed = inner_ref[:, cols] + dot_nn(query, prior)
            scale, dy = normed_parts(mixed, g_ref[:, cols].astype(f32))
            dlocal = jnp.where(mask, dot_nt(dy, value), 0.0).astype(bf16)
            tile_ref[0, :, cols] = (mixed * scale).astype(bf16)
            tile_ref[1, :, cols] = (dot_nn(dlocal, key) + dot_nt(dy, prior)).astype(bf16)
            tile_ref[2, :, cols] = dot_tn(dlocal, query).astype(bf16)
            tile_ref[3, :, cols] = dot_tn(local, dy).astype(bf16)
    mine = pl.ds(pl.multiple_of(core * count, count), count)
    theirs = pl.ds(pl.multiple_of((1 - core) * count, count), count)
    for i in range(own_ref.shape[0]):
        own_ref[i] = tile_ref[i, mine]
        send_ref[i] = tile_ref[i, theirs]


def finish_kernel(core_ref, own_far, recv_far, attended_ref, gq_ref, side_ref, sems):
    core = core_ref[0]
    outs = (attended_ref, gq_ref, side_ref.at[0], side_ref.at[1])
    copies = copies_of(
        [(own_far.at[i], half(dst, core)) for i, dst in enumerate(outs)]
        + [(recv_far.at[i], half(dst, 1 - core)) for i, dst in enumerate(outs)],
        sems,
    )
    start_all(copies)
    wait_all(copies)


def last_kernel(
    k_ref, v_ref, side_far, later_ref, out_k_far, out_v_far,
    side_ref, out_k_ref, out_v_ref, sems, out_sems,
):
    cuts = HEAD_DIM // later_ref.shape[1]
    heads = later_ref.shape[0] // cuts // 2
    copies = grouped([(side_far.at[i], side_ref.at[i]) for i in range(2)], sems)
    out_copies = grouped([(out_k_ref, out_k_far), (out_v_ref, out_v_far)], out_sems)
    for group in copies:
        start_all(group)
    for g, group in enumerate(out_copies):
        wait_all(copies[g])
        for h, cols in group_heads(g):
            places = [2 * ((h % heads) * cuts + q) + h // heads for q in range(cuts)]
            later = jnp.concatenate([later_ref[i] for i in places], axis=0)
            gk = side_ref[0, :, cols].astype(f32) + dot_nt(v_ref[:, cols], later)
            gv = side_ref[1, :, cols].astype(f32) + dot_nn(k_ref[:, cols], later)
            out_k_ref[:, cols] = gk.astype(bf16)
            out_v_ref[:, cols] = gv.astype(bf16)
        start_all(group)
    for group in out_copies:
        wait_all(group)


def per_device(query, keys, values, grads):
    tokens, width = query.shape
    part = width // 2
    pairs = lax.axis_size("pair")
    blocks = lax.axis_size("outer")
    both = ("pair", "core")
    slice_rows = part // pairs
    groups = width // GROUP
    part_groups = part // GROUP
    unit = 2 * tokens * width * HEAD_DIM
    core = lax.axis_index("core").astype(jnp.int32).reshape(1)
    place = lax.axis_index("outer").astype(jnp.int32).reshape(1)
    swap = [(0, 1), (1, 0)]

    def vmem(*dims, dtype=bf16):
        return pltpu.VMEM(dims, dtype)

    def sems(count):
        return pltpu.SemaphoreType.DMA((count,))

    pair_rows = vmem(2, 2 * tokens, part)
    pair_rows_f32 = vmem(2 * tokens, part, dtype=f32)
    rows = vmem(tokens, width)
    totals_shape = (shape(blocks, slice_rows, HEAD_DIM),)
    half_states = shape(pairs, slice_rows, HEAD_DIM)
    states = shape(2 * pairs, slice_rows, HEAD_DIM)
    pair_tiles = shape(2, 2 * tokens, part)

    out = shape(tokens, width)
    token = shape(8, 128, dtype=f32)
    (kv,) = call(
        state_kernel, (states,), (keys, values), STATE_LIMIT, unit,
        far=(0, 1), scratch=(rows, rows, sems(2 * groups)),
    )
    kv_parts = lax.all_to_all(kv, both, 0, 0, tiled=True)
    send, packed = call(
        pack_kernel, (shape(4, tokens, part), token), (core, query, keys, values, grads), LARGE,
        far=(1, 2, 3, 4), smem=(0,), scratch=(sems(4),),
    )
    recv = lax.ppermute(send, "core", swap)
    (sent,) = call(total_kernel, totals_shape, (kv_parts, packed), SMALL, far=(1,))
    kv_totals = lax.all_to_all(sent, "outer", 0, 0, tiled=True)
    inner, qg, kv_pair, ready = call(
        local_kernel,
        (shape(2 * tokens, part, dtype=f32), pair_tiles, pair_tiles, token),
        (core, query, keys, values, grads, recv),
        LARGE, 4 * unit,
        far=(1, 2, 3, 4, 5), smem=(0,), scratch=(sems(8),),
    )
    (running,) = call(
        prior_kernel, (half_states,), (place, kv_parts, kv_totals, ready), SMALL,
        far=(3,), smem=(0,),
    )
    prior = lax.all_to_all(running, "pair", 0, 0, tiled=True)
    (gq_state,) = call(
        mixed_kernel, (half_states,), (qg, inner, prior), MIXED_LIMIT, 2 * unit,
        far=(0,), scratch=(pair_rows, sems(2 * part_groups)),
    )
    gq_parts = lax.all_to_all(gq_state, "pair", 0, 0, tiled=True)
    own, send, done = call(
        side_kernel, (shape(4, tokens, part), shape(4, tokens, part), token),
        (core, qg, kv_pair, inner, prior), LARGE, 10 * unit,
        far=(1, 2, 3, 4), smem=(0,),
        scratch=(
            pair_rows, pair_rows, pair_rows_f32, vmem(pairs, slice_rows, HEAD_DIM), vmem(4, 2 * tokens, part),
            sems(5 * part_groups), sems(1),
        ),
    )
    (sent,) = call(total_kernel, totals_shape, (gq_parts,), SMALL)
    gq_totals = lax.all_to_all(sent, "outer", 0, 0, tiled=True)
    recv = lax.ppermute(send, "core", swap)
    attended, grad_query, sides = call(
        finish_kernel, (out, out, shape(2, tokens, width)), (core, own, recv), LARGE,
        far=(1, 2), smem=(0,), scratch=(sems(8),),
    )
    (running,) = call(
        later_kernel, (states,), (place, gq_parts, gq_totals, done), SMALL,
        far=(3,), smem=(0,),
    )
    later = lax.all_to_all(running, both, 0, 0, tiled=True)
    grad_key, grad_value = call(
        last_kernel, (out, out), (keys, values, sides, later), LAST_LIMIT, 2 * unit,
        far=(2,), far_out=(0, 1),
        scratch=(vmem(2, tokens, width), rows, rows, sems(2 * groups), sems(2 * groups)),
    )
    return attended, grad_query, grad_key, grad_value


def solution(mesh):
    split = Mesh(mesh.devices.reshape(-1, 32, 2), ("outer", "pair", "core"))
    placed = P(("outer", "pair", "core"), None)
    return jax.shard_map(
        per_device,
        mesh=split,
        in_specs=(placed,) * 4,
        out_specs=(placed,) * 4,
        check_vma=False,
    )
```

time: 132 us -> 124 us (0.939)
  blocking collectives: 53.4 us -> 22.8 us
  starting transfers between devices: 27.8 us -> 43.4 us
  Pallas kernels: 11.7 us -> 26.7 us
  local copies, waits for them, and re-layouts: 12 us -> 4.03 us
    all_to_all x3 -> x2, blocking collectives: 53.4 us -> 22.8 us  [the longest x1 11.5 us: per_device(): prior = lax.all_to_all(running, 'pair', 0, 0, tiled=True)]
    pallas_call x9 -> x11, Pallas kernels: 11.7 us -> 26.7 us  [call(): pl.pallas_call(kernel, out_shape=out_shape, in_specs=in_specs, out_specs=...]
    all_to_all x3 -> x4, starting transfers between devices: 27.8 us -> 38.6 us  [the longest x1 13.2 us: per_device(): kv_totals = lax.all_to_all(sent, 'outer', 0, 0, tiled=True)]
    unnamed x32 -> x20, local copies, waits for them, and re-layouts: 12 us -> 4.03 us
    ppermute x0 -> x2, starting transfers between devices: none -> 4.84 us  [per_device(): recv = lax.ppermute(send, 'core', swap)]
    ppermute x0 -> x2, waiting for transfers between devices: none -> 2.27 us  [per_device(): recv = lax.ppermute(send, 'core', swap)]
    all_to_all x3 -> x4, waiting for transfers between devices: 25.4 us -> 23.4 us  [the longest x1 7.57 us: per_device(): kv_parts = lax.all_to_all(kv, both, 0, 0, tiled=True)]
  transfers between devices with their start and end apart: 3 -> 6, of which waited for: 3 -> 5; matrix products, arithmetic and copies ran while one was open for 0% -> 0% of each run, Pallas kernels for 5% -> 14%
where the time goes in v3:
time: 124 us; the launch traced here: 123 us
  starting transfers between devices  43.4 us (35%)
  Pallas kernels  26.7 us (22%)
  waiting for transfers between devices  25.7 us (21%)
  blocking collectives  22.8 us (18%)
  local copies, waits for them, and re-layouts  4.03 us (3%)
    pallas_call x11, Pallas kernels, call(): pl.pallas_call(kernel, out_shape=out_shape, in_specs=in_specs, out_specs=...  26.7 us
    all_to_all x1, starting transfers between devices, per_device(): kv_totals = lax.all_to_all(sent, 'outer', 0, 0, tiled=True)  13.2 us
    all_to_all x1, blocking collectives, per_device(): prior = lax.all_to_all(running, 'pair', 0, 0, tiled=True)  11.5 us
    all_to_all x1, blocking collectives, per_device(): gq_parts = lax.all_to_all(gq_state, 'pair', 0, 0, tiled=True)  11.3 us
    all_to_all x1, starting transfers between devices, per_device(): kv_parts = lax.all_to_all(kv, both, 0, 0, tiled=True)  11 us
    all_to_all x1, starting transfers between devices, per_device(): later = lax.all_to_all(running, both, 0, 0, tiled=True)  10 us
    all_to_all x1, waiting for transfers between devices, per_device(): kv_parts = lax.all_to_all(kv, both, 0, 0, tiled=True)  7.57 us
    all_to_all x1, waiting for transfers between devices, per_device(): kv_totals = lax.all_to_all(sent, 'outer', 0, 0, tiled=True)  7.54 us
  transfers between devices with their start and end apart: 6, of which 5 were waited for; matrix products, arithmetic and copies ran while one was open for 0% of the time, Pallas kernels for 14%

profile of v3, /device:TPU:1, one launch (start us, length us, event | category | flops | bytes accessed | tf_op | source)
XLA Modules:
  0.0 123.4 jit_solution(1903240230935329432)
XLA Ops:
  0.6 2.7 %shard_map.77 = bf16[64,32,128]{2,1,0:T(8,128)(2,1)} custom-call(bf16[128,2048]{1,0:T(8,128)(2,1)} %k_ref.1, bf16[128,2048]{1,0:T(8,128)(2,1)} %v_ref.1), custom_call_target="tpu_custom_call" | custom-call | flops 67108864 | bytes 1572864 | tf_op jit(solution)/shard_map/pallas_call | solution.py:48
  3.3 11.0 %all-to-all-start = ((bf16[64,32,128]{2,1,0:T(8,128)(2,1)}), bf16[64,32,128]{2,1,0:T(8,128)(2,1)S(1)}, u32[]{:S(2)}, u32[]{:S(2)}) async-start(bf16[64,32,128]{2,1,0:T(8,128)(2,1)} %shard_map.77), calls=%async_computation | async-start | bytes 1048576 | tf_op jit(solution)/shard_map/all_to_all | solution.py:327
  14.3 2.2 %shard_map.75 = (bf16[4,128,1024]{2,1,0:T(8,128)(2,1)}, f32[8,128]{1,0:T(8,128)}) custom-call(s32[1]{0:T(128)} %bitcast.core_ref, bf16[128,2048]{1,0:T(8,128)(2,1)} %q_far.3, bf16[128,2048]{1,0:T(8,128)(2,1)} %k_ref.1, bf16[128,2048]{1,0:T(8,128)(2,1)} %v_ref.1, bf16[128,2048]{1,0:T(8,128)(2,1)} %g_far.3), custom_call_target="tpu_custom_call" | custom-call | bytes 3149828 | tf_op jit(solution)/shard_map/pallas_call | solution.py:48
  16.5 2.5 %collective-permute-start = (bf16[4,128,1024]{2,1,0:T(8,128)(2,1)}, bf16[4,128,1024]{2,1,0:T(8,128)(2,1)S(1)}, u32[]{:S(2)}, u32[]{:S(2)}) collective-permute-start(bf16[4,128,1024]{2,1,0:T(8,128)(2,1)} %get-tuple-element.18), channel_id=1, source_target_pairs={{0,1},{1,0},{2,3},{3,2},{4,5},{5,4},{6,7},{7,6},{8,9},{9,8},{10,11... | collective-permute-start | bytes 3145736 | tf_op jit(solution)/shard_map/ppermute | solution.py:332
  19.0 7.6 %all-to-all-done.parts_ref = bf16[64,32,128]{2,1,0:T(8,128)(2,1)S(1)} async-done(((bf16[64,32,128]{2,1,0:T(8,128)(2,1)}), bf16[64,32,128]{2,1,0:T(8,128)(2,1)S(1)}, u32[]{:S(2)}, u32[]{:S(2)}) %all-to-all-start) | async-done | bytes 524320 | tf_op jit(solution)/shard_map/all_to_all | solution.py:327
  26.6 0.0 copy-start.6
  26.6 0.7 copy-done.6
  27.3 0.7 shard_map.78
  28.0 13.2 %all-to-all-start.1 = ((bf16[8,32,128]{2,1,0:T(8,128)(2,1)}), bf16[8,32,128]{2,1,0:T(8,128)(2,1)S(1)}, u32[]{:S(2)}, u32[]{:S(2)}) async-start(bf16[8,32,128]{2,1,0:T(8,128)(2,1)} %shard_map.78), calls=%async_computation.1 | async-start | bytes 131072 | tf_op jit(solution)/shard_map/all_to_all | solution.py:334
  41.2 0.0 collective-permute-done.recv_far
  41.2 0.0 copy-start.8
  41.2 1.0 copy-done.8
  42.2 3.5 %shard_map.76 = (f32[256,1024]{1,0:T(8,128)}, bf16[2,256,1024]{2,1,0:T(8,128)(2,1)}, bf16[2,256,1024]{2,1,0:T(8,128)(2,1)}, f32[8,128]{1,0:T(8,128)}) custom-call(s32[1]{0:T(128)} %bitcast.core_ref, bf16[128,2048]{1,0:T(8,128)(2,1)} %q_far.3, bf16[128,2048]{1,0:T(8,128)(2,1)} %k_ref.1, bf16[128,2048]{1,0:T(8,128)(2,1)} %v_ref.1, bf16[128,2048]{1,0:T(8,128)(2,1)} %g_far.3, ...), custom_call_target="tpu_custom_call" | custom-call | flops 268435456 | bytes 6295556 | tf_op jit(solution)/shard_map/pallas_call | solution.py:48
  45.7 0.0 copy-start.2
  45.7 7.5 %all-to-all-done.1.totals_ref = bf16[8,32,128]{2,1,0:T(8,128)(2,1)S(1)} async-done(((bf16[8,32,128]{2,1,0:T(8,128)(2,1)}), bf16[8,32,128]{2,1,0:T(8,128)(2,1)S(1)}, u32[]{:S(2)}, u32[]{:S(2)}) %all-to-all-start.1) | async-done | bytes 65568 | tf_op jit(solution)/shard_map/all_to_all | solution.py:334
  53.2 0.0 copy-start.5
  53.2 0.7 copy-done.5
  53.9 0.1 shard_map.79
  54.0 11.5 %all_to_all.30.prior_far.prior_ref = bf16[32,32,128]{2,1,0:T(8,128)(2,1)S(1)} all-to-all(bf16[32,32,128]{2,1,0:T(8,128)(2,1)S(1)} %shard_map.79), channel_id=1, replica_groups=mesh['outer'=8,'pair'=32,'core'=2] {'pair'}, dimensions={0} | all-to-all | bytes 524288 | tf_op jit(solution)/shard_map/all_to_all | solution.py:346
  65.5 0.0 copy-start.3
  65.5 0.0 copy-done.2
  65.5 2.7 %shard_map.82 = bf16[32,32,128]{2,1,0:T(8,128)(2,1)S(1)} custom-call(bf16[2,256,1024]{2,1,0:T(8,128)(2,1)S(1)} %copy-done.2, f32[256,1024]{1,0:T(8,128)} %get-tuple-element.21.inner_far.inner_ref, bf16[32,32,128]{2,1,0:T(8,128)(2,1)S(1)} %all_to_all.30.prior_far.prior_ref), custom_call_target="tpu_custom_call" | custom-call | flops 134217728 | bytes 2621440 | tf_op jit(solution)/shard_map/pallas_call | solution.py:48
  68.2 0.0 copy-done.3
  68.3 11.3 %all_to_all.31.parts_ref = bf16[32,32,128]{2,1,0:T(8,128)(2,1)S(1)} all-to-all(bf16[32,32,128]{2,1,0:T(8,128)(2,1)S(1)} %shard_map.82), channel_id=1, replica_groups=mesh['outer'=8,'pair'=32,'core'=2] {'pair'}, dimensions={0} | all-to-all | bytes 524288 | tf_op jit(solution)/shard_map/all_to_all | solution.py:351
  79.5 0.7 shard_map.83
  80.2 4.4 %all-to-all-start.4 = ((bf16[8,32,128]{2,1,0:T(8,128)(2,1)}), bf16[8,32,128]{2,1,0:T(8,128)(2,1)S(1)}, u32[]{:S(2)}, u32[]{:S(2)}) async-start(bf16[8,32,128]{2,1,0:T(8,128)(2,1)} %shard_map.83), calls=%async_computation.4 | async-start | bytes 131072 | tf_op jit(solution)/shard_map/all_to_all | solution.py:362
  84.6 7.4 %shard_map.80 = (bf16[4,128,1024]{2,1,0:T(8,128)(2,1)}, bf16[4,128,1024]{2,1,0:T(8,128)(2,1)}, f32[8,128]{1,0:T(8,128)}) custom-call(s32[1]{0:T(128)} %bitcast.core_ref, bf16[2,256,1024]{2,1,0:T(8,128)(2,1)} %get-tuple-element.19.qg_far, bf16[2,256,1024]{2,1,0:T(8,128)(2,1)} %get-tuple-element.20.kv_far, f32[256,1024]{1,0:T(8,128)} %get-tuple-element.21.inner_far.inner_ref, ...), custom_call_target="tpu_custom_call" | custom-call | flops 671088640 | bytes 5509124 | tf_op jit(solution)/shard_map/pallas_call | solution.py:48
  92.1 4.8 %all-to-all-done.4.totals_ref = bf16[8,32,128]{2,1,0:T(8,128)(2,1)S(1)} async-done(((bf16[8,32,128]{2,1,0:T(8,128)(2,1)}), bf16[8,32,128]{2,1,0:T(8,128)(2,1)S(1)}, u32[]{:S(2)}, u32[]{:S(2)}) %all-to-all-start.4) | async-done | bytes 65568 | tf_op jit(solution)/shard_map/all_to_all | solution.py:362
  96.8 0.0 copy-start.4
  96.8 0.7 copy-done.4
  97.5 0.0 copy-start.9
  97.5 0.8 shard_map.84
  98.4 10.0 %all-to-all-start.5 = ((bf16[64,32,128]{2,1,0:T(8,128)(2,1)}), bf16[64,32,128]{2,1,0:T(8,128)(2,1)S(1)}, u32[]{:S(2)}, u32[]{:S(2)}) async-start(bf16[64,32,128]{2,1,0:T(8,128)(2,1)} %shard_map.84), calls=%async_computation.5 | async-start | bytes 1048576 | tf_op jit(solution)/shard_map/all_to_all | solution.py:372
  108.4 0.0 copy-done.9
  108.4 2.4 %collective-permute-start.1 = (bf16[4,128,1024]{2,1,0:T(8,128)(2,1)S(1)}, bf16[4,128,1024]{2,1,0:T(8,128)(2,1)S(1)}, u32[]{:S(2)}, u32[]{:S(2)}) collective-permute-start(bf16[4,128,1024]{2,1,0:T(8,128)(2,1)S(1)} %copy-done.9), channel_id=1, source_target_pairs={{0,1},{1,0},{2,3},{3,2},{4,5},{5,4},{6,7},{7,6},{8,9},{9,8},{10,11... | collective-permute-start | bytes 3145736 | tf_op jit(solution)/shard_map/ppermute | solution.py:363
  110.8 2.3 %collective-permute-done.1.recv_far = bf16[4,128,1024]{2,1,0:T(8,128)(2,1)S(1)} collective-permute-done((bf16[4,128,1024]{2,1,0:T(8,128)(2,1)S(1)}, bf16[4,128,1024]{2,1,0:T(8,128)(2,1)S(1)}, u32[]{:S(2)}, u32[]{:S(2)}) %collective-permute-start.1) | collective-permute-done | bytes 1048608 | tf_op jit(solution)/shard_map/ppermute | solution.py:363
  113.1 0.0 copy-start.7
  113.1 1.0 copy-done.7
  114.0 0.0 copy-start
  114.0 0.0 copy-start.1
  114.0 3.0 %shard_map.81 = (bf16[128,2048]{1,0:T(8,128)(2,1)}, bf16[128,2048]{1,0:T(8,128)(2,1)}, bf16[2,128,2048]{2,1,0:T(8,128)(2,1)}) custom-call(s32[1]{0:T(128)} %bitcast.core_ref, bf16[4,128,1024]{2,1,0:T(8,128)(2,1)} %get-tuple-element.24.own_far, bf16[4,128,1024]{2,1,0:T(8,128)(2,1)} %copy-done.7), custom_call_target="tpu_custom_call" | custom-call | bytes 4194308 | tf_op jit(solution)/shard_map/pallas_call | solution.py:48
  117.0 3.6 %all-to-all-done.5.later_ref = bf16[64,32,128]{2,1,0:T(8,128)(2,1)S(1)} async-done(((bf16[64,32,128]{2,1,0:T(8,128)(2,1)}), bf16[64,32,128]{2,1,0:T(8,128)(2,1)S(1)}, u32[]{:S(2)}, u32[]{:S(2)}) %all-to-all-start.5) | async-done | bytes 524320 | tf_op jit(solution)/shard_map/all_to_all | solution.py:372
  120.6 0.0 copy-done
  120.6 0.0 copy-done.1
  120.6 2.8 %shard_map.85 = (bf16[128,2048]{1,0:T(8,128)(2,1)}, bf16[128,2048]{1,0:T(8,128)(2,1)}) custom-call(bf16[128,2048]{1,0:T(8,128)(2,1)S(1)} %copy-done, bf16[128,2048]{1,0:T(8,128)(2,1)S(1)} %copy-done.1, bf16[2,128,2048]{2,1,0:T(8,128)(2,1)} %get-tuple-element.28.side_far, bf16[64,32,128]{2,1,0:T(8,128)(2,1)S(1)} %all-to-all-done.5.later_ref), custom_call_target="tpu_custom_call" | custom-call | flops 134217728 | bytes 3670016 | tf_op jit(solution)/shard_map/pallas_call | solution.py:48
Async XLA Ops:
  3.3 23.3 %all-to-all-start = ((bf16[64,32,128]{2,1,0:T(8,128)(2,1)}), bf16[64,32,128]{2,1,0:T(8,128)(2,1)S(1)}, u32[]{:S(2)}, u32[]{:S(2)}) async-start(bf16[64,32,128]{2,1,0:T(8,128)(2,1)} %shard_map.77), calls=%async_computation | async-start | bytes 1048576 | tf_op jit(solution)/shard_map/all_to_all | solution.py:327
  16.5 24.7 %collective-permute-start = (bf16[4,128,1024]{2,1,0:T(8,128)(2,1)}, bf16[4,128,1024]{2,1,0:T(8,128)(2,1)S(1)}, u32[]{:S(2)}, u32[]{:S(2)}) collective-permute-start(bf16[4,128,1024]{2,1,0:T(8,128)(2,1)} %get-tuple-element.18), channel_id=1, source_target_pairs={{0,1},{1,0},{2,3},{3,2},{4,5},{5,4},{6,7},{7,6},{8,9},{9,8},{10,11... | collective-permute-start | bytes 3145736 | tf_op jit(solution)/shard_map/ppermute | solution.py:332
  26.6 0.7 copy-start.6
  28.0 25.2 %all-to-all-start.1 = ((bf16[8,32,128]{2,1,0:T(8,128)(2,1)}), bf16[8,32,128]{2,1,0:T(8,128)(2,1)S(1)}, u32[]{:S(2)}, u32[]{:S(2)}) async-start(bf16[8,32,128]{2,1,0:T(8,128)(2,1)} %shard_map.78), calls=%async_computation.1 | async-start | bytes 131072 | tf_op jit(solution)/shard_map/all_to_all | solution.py:334
  41.2 1.0 copy-start.8
  45.7 19.8 %copy-start.2 = (bf16[2,256,1024]{2,1,0:T(8,128)(2,1)S(1)}, bf16[2,256,1024]{2,1,0:T(8,128)(2,1)}, u32[]{:S(2)}) copy-start(bf16[2,256,1024]{2,1,0:T(8,128)(2,1)} %get-tuple-element.19.qg_far) | copy-start | bytes 3145732
  53.2 0.7 copy-start.5
  65.5 2.7 %copy-start.3 = (bf16[32,32,128]{2,1,0:T(8,128)(2,1)}, bf16[32,32,128]{2,1,0:T(8,128)(2,1)S(1)}, u32[]{:S(2)}) copy-start(bf16[32,32,128]{2,1,0:T(8,128)(2,1)S(1)} %all_to_all.30.prior_far.prior_ref) | copy-start | bytes 786436
  80.2 16.6 %all-to-all-start.4 = ((bf16[8,32,128]{2,1,0:T(8,128)(2,1)}), bf16[8,32,128]{2,1,0:T(8,128)(2,1)S(1)}, u32[]{:S(2)}, u32[]{:S(2)}) async-start(bf16[8,32,128]{2,1,0:T(8,128)(2,1)} %shard_map.83), calls=%async_computation.4 | async-start | bytes 131072 | tf_op jit(solution)/shard_map/all_to_all | solution.py:362
  96.8 0.7 copy-start.4
  97.5 10.9 %copy-start.9 = (bf16[4,128,1024]{2,1,0:T(8,128)(2,1)S(1)}, bf16[4,128,1024]{2,1,0:T(8,128)(2,1)}, u32[]{:S(2)}) copy-start(bf16[4,128,1024]{2,1,0:T(8,128)(2,1)} %get-tuple-element.25) | copy-start | bytes 3145732
  98.4 22.2 %all-to-all-start.5 = ((bf16[64,32,128]{2,1,0:T(8,128)(2,1)}), bf16[64,32,128]{2,1,0:T(8,128)(2,1)S(1)}, u32[]{:S(2)}, u32[]{:S(2)}) async-start(bf16[64,32,128]{2,1,0:T(8,128)(2,1)} %shard_map.84), calls=%async_computation.5 | async-start | bytes 1048576 | tf_op jit(solution)/shard_map/all_to_all | solution.py:372
  108.4 4.6 %collective-permute-start.1 = (bf16[4,128,1024]{2,1,0:T(8,128)(2,1)S(1)}, bf16[4,128,1024]{2,1,0:T(8,128)(2,1)S(1)}, u32[]{:S(2)}, u32[]{:S(2)}) collective-permute-start(bf16[4,128,1024]{2,1,0:T(8,128)(2,1)S(1)} %copy-done.9), channel_id=1, source_target_pairs={{0,1},{1,0},{2,3},{3,2},{4,5},{5,4},{6,7},{7,6},{8,9},{9,8},{10,11... | collective-permute-start | bytes 3145736 | tf_op jit(solution)/shard_map/ppermute | solution.py:363
  113.1 1.0 copy-start.7
  114.0 6.6 %copy-start = (bf16[128,2048]{1,0:T(8,128)(2,1)S(1)}, bf16[128,2048]{1,0:T(8,128)(2,1)}, u32[]{:S(2)}) copy-start(bf16[128,2048]{1,0:T(8,128)(2,1)} %k_ref.1) | copy-start | bytes 1572868
  114.0 6.6 %copy-start.1 = (bf16[128,2048]{1,0:T(8,128)(2,1)S(1)}, bf16[128,2048]{1,0:T(8,128)(2,1)}, u32[]{:S(2)}) copy-start(bf16[128,2048]{1,0:T(8,128)(2,1)} %v_ref.1) | copy-start | bytes 1572868

commit v4 on v3

v4 whole, which is shorter than its diff:
```python
import functools

import jax
import jax.numpy as jnp
from jax import lax
from jax.experimental import pallas as pl
from jax.experimental.pallas import tpu as pltpu
from jax.sharding import Mesh, PartitionSpec as P

HEAD_DIM = 128
GROUP = 512
MIB = 1024 * 1024
LIMITS = {
    "total": 53 * MIB,
    "prior": 53 * MIB,
    "later": 53 * MIB,
    "mixed": 51 * MIB,
    "finish": 48 * MIB,
    "last": 50 * MIB,
    "local": 56 * MIB,
    "side": 56 * MIB,
    "state": 53 * MIB,
    "pack": 56 * MIB,
}
f32 = jnp.float32
bf16 = jnp.bfloat16
OUTER_TURN = 4
INNER_TURN = 20
PAIR_TURN = INNER_TURN // 2


def dot_nn(a, b):
    return lax.dot_general(a, b, (((1,), (0,)), ((), ())), preferred_element_type=f32)


def dot_nt(a, b):
    return lax.dot_general(a, b, (((1,), (1,)), ((), ())), preferred_element_type=f32)


def dot_tn(a, b):
    return lax.dot_general(a, b, (((0,), (0,)), ((), ())), preferred_element_type=f32)


def shape(*dims, dtype=bf16):
    return jax.ShapeDtypeStruct(dims, dtype)


def call(kernel, out_shape, operands, limit, flops=0, far=(), far_out=(), smem=(), scratch=()):
    def space(i, kept):
        return pl.BlockSpec(memory_space=pltpu.HBM if i in kept else pltpu.VMEM)

    in_specs = [
        pl.BlockSpec(memory_space=pltpu.SMEM) if i in smem else space(i, far)
        for i in range(len(operands))
    ]
    out_specs = tuple(space(i, far_out) for i in range(len(out_shape)))
    moved = sum(x.size * x.dtype.itemsize for x in tuple(operands) + out_shape)
    return pl.pallas_call(
        kernel,
        out_shape=out_shape,
        in_specs=in_specs,
        out_specs=out_specs,
        scratch_shapes=scratch,
        compiler_params=pltpu.CompilerParams(vmem_limit_bytes=limit),
        cost_estimate=pl.CostEstimate(flops=flops, bytes_accessed=moved, transcendentals=0),
    )(*operands)


def copies_of(pairs, sems, first=0):
    return [
        pltpu.make_async_copy(src, dst, sems.at[first + i]) for i, (src, dst) in enumerate(pairs)
    ]


def start_all(copies):
    for copy in copies:
        copy.start()


def wait_all(copies):
    for copy in copies:
        copy.wait()


def cut(ref, g):
    return ref.at[:, pl.ds(g * GROUP, GROUP)]


def grouped(pairs, sems):
    count = pairs[0][0].shape[1] // GROUP
    return [
        copies_of([(cut(src, g), cut(dst, g)) for src, dst in pairs], sems, g * len(pairs))
        for g in range(count)
    ]


def group_heads(g):
    heads = range(g * GROUP // HEAD_DIM, (g + 1) * GROUP // HEAD_DIM)
    return [(h, slice(h * HEAD_DIM, (h + 1) * HEAD_DIM)) for h in heads]


def half(ref, which):
    count = ref.shape[-1] // 2
    return ref.at[:, pl.ds(pl.multiple_of(which * count, count), count)]


def causal(count):
    rows = lax.broadcasted_iota(jnp.int32, (count, count), 0)
    cols = lax.broadcasted_iota(jnp.int32, (count, count), 1)
    return rows >= cols


def state_kernel(k_far, v_far, out_ref, k_ref, v_ref, sems):
    pairs, rows, _ = out_ref.shape
    cuts = HEAD_DIM // rows
    heads = pairs // cuts // 2
    copies = grouped([(k_far, k_ref), (v_far, v_ref)], sems)
    for group in copies:
        start_all(group)
    for g, group in enumerate(copies):
        wait_all(group)
        for h, cols in group_heads(g):
            state = dot_tn(k_ref[:, cols], v_ref[:, cols]).astype(bf16)
            for q in range(cuts):
                place = 2 * ((h % heads) * cuts + q) + h // heads
                out_ref[place ^ INNER_TURN] = state[q * rows : (q + 1) * rows]


def total_kernel(parts_ref, *refs):
    out_ref = refs[-1]
    total = parts_ref[0].astype(f32)
    for j in range(1, parts_ref.shape[0]):
        total = total + parts_ref[j].astype(f32)
    total = total.astype(bf16)
    for j in range(out_ref.shape[0]):
        out_ref[j] = total


def outer_sum(reverse, place, totals_ref):
    acc = jnp.zeros(totals_ref.shape[1:], f32)
    for b in range(totals_ref.shape[0]):
        wanted = b > place if reverse else b < place
        acc = acc + jnp.where(wanted, totals_ref[b ^ OUTER_TURN].astype(f32), 0.0)
    return acc


def prior_kernel(place_ref, parts_ref, totals_ref, after_ref, out_ref):
    acc = outer_sum(False, place_ref[0], totals_ref)
    for r in range(out_ref.shape[0]):
        out_ref[r ^ PAIR_TURN] = acc.astype(bf16)
        for i in (2 * r, 2 * r + 1):
            acc = acc + parts_ref[i ^ INNER_TURN].astype(f32)


def later_kernel(place_ref, parts_ref, totals_ref, after_ref, out_ref):
    acc = outer_sum(True, place_ref[0], totals_ref)
    for r in reversed(range(parts_ref.shape[0])):
        for i in (2 * r, 2 * r + 1):
            out_ref[i ^ INNER_TURN] = acc.astype(bf16)
        acc = acc + parts_ref[r ^ PAIR_TURN].astype(f32)


def pack_kernel(core_ref, q_far, k_far, v_far, g_far, out_ref, sems):
    other = 1 - core_ref[0]
    rows = (q_far, k_far, v_far, g_far)
    copies = copies_of([(half(src, other), out_ref.at[i]) for i, src in enumerate(rows)], sems)
    start_all(copies)
    wait_all(copies)


def local_kernel(
    core_ref, q_far, k_far, v_far, g_far, recv_far,
    inner_ref, qg_ref, kv_ref, sems,
):
    core = core_ref[0]
    count = q_far.shape[0]
    mine = pl.ds(pl.multiple_of(core * count, count), count)
    theirs = pl.ds(pl.multiple_of((1 - core) * count, count), count)
    q_ref, k_ref, v_ref = qg_ref.at[0], kv_ref.at[0], kv_ref.at[1]
    near = (q_ref, k_ref, v_ref, qg_ref.at[1])
    copies = copies_of(
        [(half(src, core), dst.at[mine]) for src, dst in zip((q_far, k_far, v_far, g_far), near)]
        + [(recv_far.at[i], dst.at[theirs]) for i, dst in enumerate(near)],
        sems,
    )
    start_all(copies)
    wait_all(copies)
    mask = causal(2 * count)
    for g in range(q_ref.shape[1] // GROUP):
        for h, cols in group_heads(g):
            scores = dot_nt(q_ref[:, cols], k_ref[:, cols])
            local = jnp.where(mask, scores, 0.0).astype(bf16)
            inner_ref[:, cols] = dot_nn(local, v_ref[:, cols])


def whole_state(ref, h):
    cuts = HEAD_DIM // ref.shape[1]
    return jnp.concatenate([ref[(h * cuts + q) ^ PAIR_TURN] for q in range(cuts)], axis=0)


def normed_parts(mixed, grad):
    scale = lax.rsqrt(jnp.mean(mixed * mixed, axis=-1, keepdims=True) + 1e-06)
    inner_mean = jnp.mean(grad * mixed, axis=-1, keepdims=True)
    dy = (scale * grad - mixed * (scale * scale * scale * inner_mean)).astype(bf16)
    return scale, dy


def mixed_kernel(qg_ref, inner_far, prior_ref, state_ref, inner_ref, sems):
    rows = state_ref.shape[1]
    cuts = HEAD_DIM // rows
    q_ref, g_ref = qg_ref.at[0], qg_ref.at[1]
    copies = grouped([(inner_far, inner_ref)], sems)
    for group in copies:
        start_all(group)
    for g, group in enumerate(copies):
        wait_all(group)
        for h, cols in group_heads(g):
            query = q_ref[:, cols]
            mixed = inner_ref[:, cols] + dot_nn(query, whole_state(prior_ref, h))
            _, dy = normed_parts(mixed, g_ref[:, cols].astype(f32))
            state = dot_tn(query, dy).astype(bf16)
            for q in range(cuts):
                state_ref[(h * cuts + q) ^ PAIR_TURN] = state[q * rows : (q + 1) * rows]


def side_kernel(
    first, core_ref, qg_far, kv_far, inner_far, prior_far, own_ref, send_ref,
    qg_ref, kv_ref, inner_ref, prior_ref, tile_ref, sems, prior_sem,
):
    core = core_ref[0]
    count = own_ref.shape[1]
    q_ref, g_ref, k_ref, v_ref = qg_ref.at[0], qg_ref.at[1], kv_ref.at[0], kv_ref.at[1]
    mine_cols = pl.ds(first * HEAD_DIM, inner_ref.shape[1])
    copies = grouped(
        [(qg_far.at[i, :, mine_cols], qg_ref.at[i]) for i in range(2)]
        + [(kv_far.at[i, :, mine_cols], kv_ref.at[i]) for i in range(2)]
        + [(inner_far.at[:, mine_cols], inner_ref)],
        sems,
    )
    prior_copy = copies_of([(prior_far, prior_ref)], prior_sem)
    start_all(prior_copy)
    for group in copies:
        start_all(group)
    mask = causal(2 * count)
    wait_all(prior_copy)
    for g, group in enumerate(copies):
        wait_all(group)
        for h, cols in group_heads(g):
            query, key, value = q_ref[:, cols], k_ref[:, cols], v_ref[:, cols]
            prior = whole_state(prior_ref, first + h)
            local = jnp.where(mask, dot_nt(query, key), 0.0).astype(bf16)
            mixed = inner_ref[:, cols] + dot_nn(query, prior)
            scale, dy = normed_parts(mixed, g_ref[:, cols].astype(f32))
            dlocal = jnp.where(mask, dot_nt(dy, value), 0.0).astype(bf16)
            tile_ref[0, :, cols] = (mixed * scale).astype(bf16)
            tile_ref[1, :, cols] = (dot_nn(dlocal, key) + dot_nt(dy, prior)).astype(bf16)
            tile_ref[2, :, cols] = dot_tn(dlocal, query).astype(bf16)
            tile_ref[3, :, cols] = dot_tn(local, dy).astype(bf16)
    mine = pl.ds(pl.multiple_of(core * count, count), count)
    theirs = pl.ds(pl.multiple_of((1 - core) * count, count), count)
    for i in range(own_ref.shape[0]):
        own_ref[i] = tile_ref[i, mine]
        send_ref[i] = tile_ref[i, theirs]


def swapped_copies(core, first, outs, own_a, own_b, recv_a, recv_b, sems):
    pairs = []
    for j, (own, recv) in enumerate(((own_a, recv_a), (own_b, recv_b))):
        for i, dst in enumerate(outs):
            quarter = dst.shape[1] // 4
            for src, which in ((own, core), (recv, 1 - core)):
                start = pl.multiple_of((2 * which + j) * quarter, quarter)
                pairs.append((src.at[first + i], dst.at[:, pl.ds(start, quarter)]))
    return copies_of(pairs, sems)


def finish_kernel(core_ref, own_a, own_b, recv_a, recv_b, attended_ref, gq_ref, sems):
    outs = (attended_ref, gq_ref)
    copies = swapped_copies(core_ref[0], 0, outs, own_a, own_b, recv_a, recv_b, sems)
    start_all(copies)
    wait_all(copies)


def last_kernel(
    core_ref, k_ref, v_ref, own_a, own_b, recv_a, recv_b, later_ref, out_k_far, out_v_far,
    gk_ref, gv_ref, out_k_ref, out_v_ref, sems, out_sems,
):
    cuts = HEAD_DIM // later_ref.shape[1]
    heads = later_ref.shape[0] // cuts // 2
    sides = (gk_ref, gv_ref)
    copies = swapped_copies(core_ref[0], 2, sides, own_a, own_b, recv_a, recv_b, sems)
    out_copies = grouped([(out_k_ref, out_k_far), (out_v_ref, out_v_far)], out_sems)
    start_all(copies)
    wait_all(copies)
    for g, group in enumerate(out_copies):
        for h, cols in group_heads(g):
            places = [2 * ((h % heads) * cuts + q) + h // heads for q in range(cuts)]
            later = jnp.concatenate([later_ref[i ^ INNER_TURN] for i in places], axis=0)
            gk = gk_ref[:, cols].astype(f32) + dot_nt(v_ref[:, cols], later)
            gv = gv_ref[:, cols].astype(f32) + dot_nn(k_ref[:, cols], later)
            out_k_ref[:, cols] = gk.astype(bf16)
            out_v_ref[:, cols] = gv.astype(bf16)
        start_all(group)
    for group in out_copies:
        wait_all(group)


def exchange(blocks, axis, groups):
    return lax.all_to_all(blocks, axis, 0, 0, tiled=True, axis_index_groups=groups)


def per_device(query, keys, values, grads):
    tokens, width = query.shape
    part = width // 2
    pairs = lax.axis_size("inner") // 2
    blocks = lax.axis_size("outer")
    slice_rows = part // pairs
    groups = width // GROUP
    part_groups = part // GROUP
    unit = 2 * tokens * width * HEAD_DIM
    core = (lax.axis_index("inner").astype(jnp.int32) % 2).reshape(1)
    place = lax.axis_index("outer").astype(jnp.int32).reshape(1)
    swap = [(i, i ^ 1) for i in range(2 * pairs)]
    outer_groups = [[b ^ OUTER_TURN for b in range(blocks)]]
    inner_groups = [[i ^ INNER_TURN for i in range(2 * pairs)]]
    pair_groups = [[2 * (r ^ PAIR_TURN) + c for r in range(pairs)] for c in range(2)]

    def vmem(*dims, dtype=bf16):
        return pltpu.VMEM(dims, dtype)

    def sems(count):
        return pltpu.SemaphoreType.DMA((count,))

    pair_rows = vmem(2, 2 * tokens, part)
    pair_rows_f32 = vmem(2 * tokens, part, dtype=f32)
    rows = vmem(tokens, width)
    totals_shape = (shape(blocks, slice_rows, HEAD_DIM),)
    half_states = shape(pairs, slice_rows, HEAD_DIM)
    states = shape(2 * pairs, slice_rows, HEAD_DIM)
    pair_tiles = shape(2, 2 * tokens, part)

    out = shape(tokens, width)
    (kv,) = call(
        state_kernel, (states,), (keys, values), LIMITS["state"], unit,
        far=(0, 1), scratch=(rows, rows, sems(2 * groups)),
    )
    kv_parts = exchange(kv, "inner", inner_groups)
    (send,) = call(
        pack_kernel, (shape(4, tokens, part),), (core, query, keys, values, grads), LIMITS["pack"],
        far=(1, 2, 3, 4), smem=(0,), scratch=(sems(4),),
    )
    recv = lax.ppermute(send, "inner", swap)
    (sent,) = call(total_kernel, totals_shape, (kv_parts, send), LIMITS["total"], far=(1,))
    kv_totals = exchange(sent, "outer", outer_groups)
    inner, qg, kv_pair = call(
        local_kernel,
        (shape(2 * tokens, part, dtype=f32), pair_tiles, pair_tiles),
        (core, query, keys, values, grads, recv),
        LIMITS["local"], 4 * unit,
        far=(1, 2, 3, 4, 5), smem=(0,), scratch=(sems(8),),
    )
    (running,) = call(
        prior_kernel, (half_states,), (place, kv_parts, kv_totals, qg), LIMITS["prior"],
        far=(3,), smem=(0,),
    )
    prior = exchange(running, "inner", pair_groups)
    (gq_state,) = call(
        mixed_kernel, (half_states,), (qg, inner, prior), LIMITS["mixed"], 2 * unit,
        far=(1,), scratch=(pair_rows_f32, sems(part_groups)),
    )
    gq_parts = exchange(gq_state, "inner", pair_groups)
    piece = GROUP
    quarter = shape(4, tokens, piece)

    def side(first):
        return call(
            functools.partial(side_kernel, first), (quarter, quarter),
            (core, qg, kv_pair, inner, prior), LIMITS["side"], 5 * unit,
            far=(1, 2, 3, 4), smem=(0,),
            scratch=(
                vmem(2, 2 * tokens, piece), vmem(2, 2 * tokens, piece),
                vmem(2 * tokens, piece, dtype=f32), vmem(pairs, slice_rows, HEAD_DIM),
                vmem(4, 2 * tokens, piece), sems(5), sems(1),
            ),
        )

    own_a, send_a = side(0)
    own_b, send_b = side(piece // HEAD_DIM)
    (sent,) = call(total_kernel, totals_shape, (gq_parts, own_a), LIMITS["total"], far=(1,))
    gq_totals = exchange(sent, "outer", outer_groups)
    recv_a = lax.ppermute(send_a, "inner", swap)
    recv_b = lax.ppermute(send_b, "inner", swap)
    swapped = (own_a, own_b, recv_a, recv_b)
    attended, grad_query = call(
        finish_kernel, (out, out), (core,) + swapped, LIMITS["finish"],
        far=(1, 2, 3, 4), smem=(0,), scratch=(sems(8),),
    )
    (running,) = call(
        later_kernel, (states,), (place, gq_parts, gq_totals, own_b), LIMITS["later"],
        far=(3,), smem=(0,),
    )
    later = exchange(running, "inner", inner_groups)
    grad_key, grad_value = call(
        last_kernel, (out, out), (core, keys, values) + swapped + (later,), LIMITS["last"], 2 * unit,
        far=(3, 4, 5, 6), far_out=(0, 1), smem=(0,),
        scratch=(rows,) * 4 + (sems(8), sems(2 * groups)),
    )
    return attended, grad_query, grad_key, grad_value


def solution(mesh):
    split = Mesh(mesh.devices.reshape(-1, 64), ("outer", "inner"))
    placed = P(("outer", "inner"), None)
    return jax.shard_map(
        per_device,
        mesh=split,
        in_specs=(placed,) * 4,
        out_specs=(placed,) * 4,
        check_vma=False,
    )
```

time: 124 us -> 113 us (0.911)
  starting transfers between devices: 43.4 us -> 67.1 us
  waiting for transfers between devices: 25.7 us -> 5.24 us
  blocking collectives: 22.8 us -> 11.4 us
  local copies, waits for them, and re-layouts: 4.03 us -> 2.03 us
    all_to_all x4 -> x5, starting transfers between devices: 38.6 us -> 60.4 us  [exchange(): lax.all_to_all(blocks, axis, 0, 0, tiled=True, axis_index_groups=groups)]
    all_to_all x4 -> x5, waiting for transfers between devices: 23.4 us -> 3.3 us  [exchange(): lax.all_to_all(blocks, axis, 0, 0, tiled=True, axis_index_groups=groups)]
    all_to_all x2 -> x1, blocking collectives: 22.8 us -> 11.4 us  [exchange(): lax.all_to_all(blocks, axis, 0, 0, tiled=True, axis_index_groups=groups)]
    unnamed x20 -> x18, local copies, waits for them, and re-layouts: 4.03 us -> 2.03 us
    ppermute x2 -> x3, starting transfers between devices: 4.84 us -> 6.73 us  [the longest x1 2.27 us: per_device(): recv = lax.ppermute(send, 'inner', swap)]
    pallas_call x11 -> x12, Pallas kernels: 26.7 us -> 25.9 us  [call(): pl.pallas_call(kernel, out_shape=out_shape, in_specs=in_specs, out_specs=...]
  transfers between devices with their start and end apart: 6 -> 8, of which waited for: 5 -> 3; matrix products, arithmetic and copies ran while one was open for 0% -> 0% of each run, Pallas kernels for 14% -> 15%
where the time goes in v4:
time: 113 us; the launch traced here: 112 us
  starting transfers between devices  67.1 us (59%)
  Pallas kernels  25.9 us (23%)
  blocking collectives  11.4 us (10%)
  waiting for transfers between devices  5.24 us (5%)
  local copies, waits for them, and re-layouts  2.03 us (2%)
    all_to_all x5, starting transfers between devices, exchange(): lax.all_to_all(blocks, axis, 0, 0, tiled=True, axis_index_groups=groups)  60.4 us
    pallas_call x12, Pallas kernels, call(): pl.pallas_call(kernel, out_shape=out_shape, in_specs=in_specs, out_specs=...  25.9 us
    all_to_all x1, blocking collectives, exchange(): lax.all_to_all(blocks, axis, 0, 0, tiled=True, axis_index_groups=groups)  11.4 us
    all_to_all x5, waiting for transfers between devices, exchange(): lax.all_to_all(blocks, axis, 0, 0, tiled=True, axis_index_groups=groups)  3.3 us
    ppermute x1, starting transfers between devices, per_device(): recv = lax.ppermute(send, 'inner', swap)  2.27 us
    ppermute x1, starting transfers between devices, per_device(): recv_a = lax.ppermute(send_a, 'inner', swap)  2.27 us
  transfers between devices with their start and end apart: 8, of which 3 were waited for; matrix products, arithmetic and copies ran while one was open for 0% of the time, Pallas kernels for 15%

profile of v4, /device:TPU:1, one launch (start us, length us, event | category | flops | bytes accessed | tf_op | source)
XLA Modules:
  0.0 112.5 jit_solution(10306104807784156709)
XLA Ops:
  0.6 2.7 %shard_map.77 = bf16[64,32,128]{2,1,0:T(8,128)(2,1)} custom-call(bf16[128,2048]{1,0:T(8,128)(2,1)} %k_ref.1, bf16[128,2048]{1,0:T(8,128)(2,1)} %v_ref.1), custom_call_target="tpu_custom_call" | custom-call | flops 67108864 | bytes 1572864 | tf_op jit(solution)/shard_map/pallas_call | solution.py:58
  3.3 14.3 %all-to-all-start = ((bf16[64,32,128]{2,1,0:T(8,128)(2,1)}), bf16[64,32,128]{2,1,0:T(8,128)(2,1)S(1)}, u32[]{:S(2)}, u32[]{:S(2)}) async-start(bf16[64,32,128]{2,1,0:T(8,128)(2,1)} %shard_map.77), calls=%async_computation | async-start | bytes 1048576 | tf_op jit(solution)/shard_map/all_to_all | solution.py:309
  17.7 2.2 %shard_map.75.refs_0_ = bf16[4,128,1024]{2,1,0:T(8,128)(2,1)} custom-call(s32[1]{0:T(128)} %bitcast.core_ref, bf16[128,2048]{1,0:T(8,128)(2,1)} %q_far.3, bf16[128,2048]{1,0:T(8,128)(2,1)} %k_ref.1, bf16[128,2048]{1,0:T(8,128)(2,1)} %v_ref.1, bf16[128,2048]{1,0:T(8,128)(2,1)} %g_far.3), custom_call_target="tpu_custom_call" | custom-call | bytes 3145732 | tf_op jit(solution)/shard_map/pallas_call | solution.py:58
  19.9 2.3 %collective-permute-start = (bf16[4,128,1024]{2,1,0:T(8,128)(2,1)}, bf16[4,128,1024]{2,1,0:T(8,128)(2,1)S(1)}, u32[]{:S(2)}, u32[]{:S(2)}) collective-permute-start(bf16[4,128,1024]{2,1,0:T(8,128)(2,1)} %shard_map.75.refs_0_), channel_id=1, source_target_pairs={{0,1},{1,0},{2,3},{3,2},{4,5},{5,4},{6,7},{7,6},{8,9},{9,8},{10,11... | collective-permute-start | bytes 3145736 | tf_op jit(solution)/shard_map/ppermute | solution.py:352
  22.2 3.2 %all-to-all-done.parts_ref = bf16[64,32,128]{2,1,0:T(8,128)(2,1)S(1)} async-done(((bf16[64,32,128]{2,1,0:T(8,128)(2,1)}), bf16[64,32,128]{2,1,0:T(8,128)(2,1)S(1)}, u32[]{:S(2)}, u32[]{:S(2)}) %all-to-all-start) | async-done | bytes 524320 | tf_op jit(solution)/shard_map/all_to_all | solution.py:309
  25.4 0.7 shard_map.78
  26.2 14.5 %all-to-all-start.1 = ((bf16[8,32,128]{2,1,0:T(8,128)(2,1)}), bf16[8,32,128]{2,1,0:T(8,128)(2,1)S(1)}, u32[]{:S(2)}, u32[]{:S(2)}) async-start(bf16[8,32,128]{2,1,0:T(8,128)(2,1)} %shard_map.78), calls=%async_computation.1 | async-start | bytes 131072 | tf_op jit(solution)/shard_map/all_to_all | solution.py:309
  40.7 0.0 collective-permute-done.recv_far
  40.7 0.0 copy-start.8
  40.7 1.0 copy-done.8
  41.7 3.5 %shard_map.76 = (f32[256,1024]{1,0:T(8,128)}, bf16[2,256,1024]{2,1,0:T(8,128)(2,1)}, bf16[2,256,1024]{2,1,0:T(8,128)(2,1)}) custom-call(s32[1]{0:T(128)} %bitcast.core_ref, bf16[128,2048]{1,0:T(8,128)(2,1)} %q_far.3, bf16[128,2048]{1,0:T(8,128)(2,1)} %k_ref.1, bf16[128,2048]{1,0:T(8,128)(2,1)} %v_ref.1, bf16[128,2048]{1,0:T(8,128)(2,1)} %g_far.3, ...), custom_call_target="tpu_custom_call" | custom-call | flops 268435456 | bytes 6291460 | tf_op jit(solution)/shard_map/pallas_call | solution.py:58
  45.2 0.0 all-to-all-done.1.totals_ref
  45.2 0.0 copy-start
  45.2 0.0 copy-start.1
  45.2 0.1 shard_map.79
  45.3 11.4 %all_to_all.30.prior_far.prior_ref = bf16[32,32,128]{2,1,0:T(8,128)(2,1)S(1)} all-to-all(bf16[32,32,128]{2,1,0:T(8,128)(2,1)S(1)} %shard_map.79), channel_id=1, replica_groups={{20,22,16,18,28,30,24,26,4,6,0,2,12,14,8,10,52,54,48,50,60,62,56,58,36,..., dimensions={0} | all-to-all | bytes 524288 | tf_op jit(solution)/shard_map/all_to_all | solution.py:309
  56.7 0.0 copy-start.7
  56.7 0.0 copy-done
  56.7 0.0 copy-done.1
  56.7 2.2 %shard_map.83 = bf16[32,32,128]{2,1,0:T(8,128)(2,1)} custom-call(bf16[2,256,1024]{2,1,0:T(8,128)(2,1)S(1)} %copy-done, f32[256,1024]{1,0:T(8,128)S(1)} %copy-done.1, bf16[32,32,128]{2,1,0:T(8,128)(2,1)S(1)} %all_to_all.30.prior_far.prior_ref), custom_call_target="tpu_custom_call" | custom-call | flops 134217728 | bytes 2621440 | tf_op jit(solution)/shard_map/pallas_call | solution.py:58
  58.9 0.0 copy-done.7
  58.9 7.4 %all-to-all-start.3 = ((bf16[32,32,128]{2,1,0:T(8,128)(2,1)}), bf16[32,32,128]{2,1,0:T(8,128)(2,1)S(1)}, u32[]{:S(2)}, u32[]{:S(2)}) async-start(bf16[32,32,128]{2,1,0:T(8,128)(2,1)} %shard_map.83), calls=%async_computation.3 | async-start | bytes 524288 | tf_op jit(solution)/shard_map/all_to_all | solution.py:309
  66.3 4.6 %shard_map.80 = (bf16[4,128,512]{2,1,0:T(8,128)(2,1)}, bf16[4,128,512]{2,1,0:T(8,128)(2,1)}) custom-call(s32[1]{0:T(128)} %bitcast.core_ref, bf16[2,256,1024]{2,1,0:T(8,128)(2,1)} %get-tuple-element.15.after_ref.qg_far.qg_ref, bf16[2,256,1024]{2,1,0:T(8,128)(2,1)} %get-tuple-element.16.kv_far, f32[256,1024]{1,0:T(8,128)} %get-tuple-element.17.inner_far, ...), custom_call_target="tpu_custom_call" | custom-call | flops 335544320 | bytes 4456452 | tf_op jit(solution)/shard_map/pallas_call | solution.py:58
  70.9 0.0 all-to-all-done.3.parts_ref
  70.9 0.0 copy-start.5
  70.9 1.0 copy-done.5
  72.0 0.7 shard_map.84
  72.6 11.5 %all-to-all-start.4 = ((bf16[8,32,128]{2,1,0:T(8,128)(2,1)}), bf16[8,32,128]{2,1,0:T(8,128)(2,1)S(1)}, u32[]{:S(2)}, u32[]{:S(2)}) async-start(bf16[8,32,128]{2,1,0:T(8,128)(2,1)} %shard_map.84), calls=%async_computation.4 | async-start | bytes 131072 | tf_op jit(solution)/shard_map/all_to_all | solution.py:309
  84.1 4.6 %shard_map.81 = (bf16[4,128,512]{2,1,0:T(8,128)(2,1)}, bf16[4,128,512]{2,1,0:T(8,128)(2,1)}) custom-call(s32[1]{0:T(128)} %bitcast.core_ref, bf16[2,256,1024]{2,1,0:T(8,128)(2,1)} %get-tuple-element.15.after_ref.qg_far.qg_ref, bf16[2,256,1024]{2,1,0:T(8,128)(2,1)} %get-tuple-element.16.kv_far, f32[256,1024]{1,0:T(8,128)} %get-tuple-element.17.inner_far, ...), custom_call_target="tpu_custom_call" | custom-call | flops 335544320 | bytes 4456452 | tf_op jit(solution)/shard_map/pallas_call | solution.py:58
  88.7 0.0 all-to-all-done.4.totals_ref
  88.7 0.9 shard_map.85
  89.5 0.0 copy-start.4
  89.5 0.0 copy-start.6
  89.5 12.6 %all-to-all-start.5 = ((bf16[64,32,128]{2,1,0:T(8,128)(2,1)}), bf16[64,32,128]{2,1,0:T(8,128)(2,1)}, u32[]{:S(2)}, u32[]{:S(2)}) async-start(bf16[64,32,128]{2,1,0:T(8,128)(2,1)} %shard_map.85), calls=%async_computation.5 | async-start | bytes 1048576 | tf_op jit(solution)/shard_map/all_to_all | solution.py:309
  102.2 2.3 %collective-permute-start.1 = (bf16[4,128,512]{2,1,0:T(8,128)(2,1)}, bf16[4,128,512]{2,1,0:T(8,128)(2,1)S(1)}, u32[]{:S(2)}, u32[]{:S(2)}) collective-permute-start(bf16[4,128,512]{2,1,0:T(8,128)(2,1)} %get-tuple-element.20), channel_id=1, source_target_pairs={{0,1},{1,0},{2,3},{3,2},{4,5},{5,4},{6,7},{7,6},{8,9},{9,8},{10,11... | collective-permute-start | bytes 1572872 | tf_op jit(solution)/shard_map/ppermute | solution.py:391
  104.5 0.0 copy-start.2
  104.5 0.0 copy-start.3
  104.5 2.2 %collective-permute-start.2 = (bf16[4,128,512]{2,1,0:T(8,128)(2,1)}, bf16[4,128,512]{2,1,0:T(8,128)(2,1)S(1)}, u32[]{:S(2)}, u32[]{:S(2)}) collective-permute-start(bf16[4,128,512]{2,1,0:T(8,128)(2,1)} %get-tuple-element.21), channel_id=1, source_target_pairs={{0,1},{1,0},{2,3},{3,2},{4,5},{5,4},{6,7},{7,6},{8,9},{9,8},{10,11... | collective-permute-start | bytes 1572872 | tf_op jit(solution)/shard_map/ppermute | solution.py:392
  106.7 0.0 collective-permute-done.1.recv_a
  106.7 1.9 %collective-permute-done.2.recv_b = bf16[4,128,512]{2,1,0:T(8,128)(2,1)S(1)} collective-permute-done((bf16[4,128,512]{2,1,0:T(8,128)(2,1)}, bf16[4,128,512]{2,1,0:T(8,128)(2,1)S(1)}, u32[]{:S(2)}, u32[]{:S(2)}) %collective-permute-start.2) | collective-permute-done | bytes 524320 | tf_op jit(solution)/shard_map/ppermute | solution.py:392
  108.6 0.0 copy-done.4
  108.6 0.0 copy-done.6
  108.6 1.2 %shard_map.82 = (bf16[128,2048]{1,0:T(8,128)(2,1)}, bf16[128,2048]{1,0:T(8,128)(2,1)}) custom-call(s32[1]{0:T(128)} %bitcast.core_ref, bf16[4,128,512]{2,1,0:T(8,128)(2,1)S(1)} %copy-done.6, bf16[4,128,512]{2,1,0:T(8,128)(2,1)S(1)} %copy-done.4, bf16[4,128,512]{2,1,0:T(8,128)(2,1)S(1)} %collective-permute-done.1.recv_a, ...), custom_call_target="tpu_custom_call" | custom-call | bytes 3145732 | tf_op jit(solution)/shard_map/pallas_call | solution.py:58
  109.8 0.1 all-to-all-done.5.later_ref
  109.9 0.0 copy-done.2
  109.9 0.0 copy-done.3
  109.9 2.6 %shard_map.86 = (bf16[128,2048]{1,0:T(8,128)(2,1)}, bf16[128,2048]{1,0:T(8,128)(2,1)}) custom-call(s32[1]{0:T(128)} %bitcast.core_ref, bf16[128,2048]{1,0:T(8,128)(2,1)S(1)} %copy-done.2, bf16[128,2048]{1,0:T(8,128)(2,1)S(1)} %copy-done.3, bf16[4,128,512]{2,1,0:T(8,128)(2,1)S(1)} %copy-done.6, bf16[4,128,512]{2,1,0:T(8,128)(2,1)S(1)} %copy-done.4, ...), custom_call_target="tpu_custom_call" | custom-call | flops 134217728 | bytes 4718596 | tf_op jit(solution)/shard_map/pallas_call | solution.py:58
Async XLA Ops:
  3.3 22.1 %all-to-all-start = ((bf16[64,32,128]{2,1,0:T(8,128)(2,1)}), bf16[64,32,128]{2,1,0:T(8,128)(2,1)S(1)}, u32[]{:S(2)}, u32[]{:S(2)}) async-start(bf16[64,32,128]{2,1,0:T(8,128)(2,1)} %shard_map.77), calls=%async_computation | async-start | bytes 1048576 | tf_op jit(solution)/shard_map/all_to_all | solution.py:309
  19.9 20.8 %collective-permute-start = (bf16[4,128,1024]{2,1,0:T(8,128)(2,1)}, bf16[4,128,1024]{2,1,0:T(8,128)(2,1)S(1)}, u32[]{:S(2)}, u32[]{:S(2)}) collective-permute-start(bf16[4,128,1024]{2,1,0:T(8,128)(2,1)} %shard_map.75.refs_0_), channel_id=1, source_target_pairs={{0,1},{1,0},{2,3},{3,2},{4,5},{5,4},{6,7},{7,6},{8,9},{9,8},{10,11... | collective-permute-start | bytes 3145736 | tf_op jit(solution)/shard_map/ppermute | solution.py:352
  26.2 19.0 %all-to-all-start.1 = ((bf16[8,32,128]{2,1,0:T(8,128)(2,1)}), bf16[8,32,128]{2,1,0:T(8,128)(2,1)S(1)}, u32[]{:S(2)}, u32[]{:S(2)}) async-start(bf16[8,32,128]{2,1,0:T(8,128)(2,1)} %shard_map.78), calls=%async_computation.1 | async-start | bytes 131072 | tf_op jit(solution)/shard_map/all_to_all | solution.py:309
  40.7 1.0 copy-start.8
  45.2 11.5 %copy-start = (bf16[2,256,1024]{2,1,0:T(8,128)(2,1)S(1)}, bf16[2,256,1024]{2,1,0:T(8,128)(2,1)}, u32[]{:S(2)}) copy-start(bf16[2,256,1024]{2,1,0:T(8,128)(2,1)} %get-tuple-element.15.after_ref.qg_far.qg_ref) | copy-start | bytes 3145732
  45.2 11.5 %copy-start.1 = (f32[256,1024]{1,0:T(8,128)S(1)}, f32[256,1024]{1,0:T(8,128)}, u32[]{:S(2)}) copy-start(f32[256,1024]{1,0:T(8,128)} %get-tuple-element.17.inner_far) | copy-start | bytes 3145732
  56.7 2.2 %copy-start.7 = (bf16[32,32,128]{2,1,0:T(8,128)(2,1)}, bf16[32,32,128]{2,1,0:T(8,128)(2,1)S(1)}, u32[]{:S(2)}) copy-start(bf16[32,32,128]{2,1,0:T(8,128)(2,1)S(1)} %all_to_all.30.prior_far.prior_ref) | copy-start | bytes 786436
  58.9 12.0 %all-to-all-start.3 = ((bf16[32,32,128]{2,1,0:T(8,128)(2,1)}), bf16[32,32,128]{2,1,0:T(8,128)(2,1)S(1)}, u32[]{:S(2)}, u32[]{:S(2)}) async-start(bf16[32,32,128]{2,1,0:T(8,128)(2,1)} %shard_map.83), calls=%async_computation.3 | async-start | bytes 524288 | tf_op jit(solution)/shard_map/all_to_all | solution.py:309
  70.9 1.0 copy-start.5
  72.6 16.0 %all-to-all-start.4 = ((bf16[8,32,128]{2,1,0:T(8,128)(2,1)}), bf16[8,32,128]{2,1,0:T(8,128)(2,1)S(1)}, u32[]{:S(2)}, u32[]{:S(2)}) async-start(bf16[8,32,128]{2,1,0:T(8,128)(2,1)} %shard_map.84), calls=%async_computation.4 | async-start | bytes 131072 | tf_op jit(solution)/shard_map/all_to_all | solution.py:309
  89.5 19.1 %copy-start.4 = (bf16[4,128,512]{2,1,0:T(8,128)(2,1)S(1)}, bf16[4,128,512]{2,1,0:T(8,128)(2,1)}, u32[]{:S(2)}) copy-start(bf16[4,128,512]{2,1,0:T(8,128)(2,1)} %get-tuple-element.19.own_b.after_ref) | copy-start | bytes 1572868
  89.5 19.1 %copy-start.6 = (bf16[4,128,512]{2,1,0:T(8,128)(2,1)S(1)}, bf16[4,128,512]{2,1,0:T(8,128)(2,1)}, u32[]{:S(2)}) copy-start(bf16[4,128,512]{2,1,0:T(8,128)(2,1)} %get-tuple-element.18.own_a.refs_0_) | copy-start | bytes 1572868
  89.5 20.3 %all-to-all-start.5 = ((bf16[64,32,128]{2,1,0:T(8,128)(2,1)}), bf16[64,32,128]{2,1,0:T(8,128)(2,1)}, u32[]{:S(2)}, u32[]{:S(2)}) async-start(bf16[64,32,128]{2,1,0:T(8,128)(2,1)} %shard_map.85), calls=%async_computation.5 | async-start | bytes 1048576 | tf_op jit(solution)/shard_map/all_to_all | solution.py:309
  102.2 4.5 %collective-permute-start.1 = (bf16[4,128,512]{2,1,0:T(8,128)(2,1)}, bf16[4,128,512]{2,1,0:T(8,128)(2,1)S(1)}, u32[]{:S(2)}, u32[]{:S(2)}) collective-permute-start(bf16[4,128,512]{2,1,0:T(8,128)(2,1)} %get-tuple-element.20), channel_id=1, source_target_pairs={{0,1},{1,0},{2,3},{3,2},{4,5},{5,4},{6,7},{7,6},{8,9},{9,8},{10,11... | collective-permute-start | bytes 1572872 | tf_op jit(solution)/shard_map/ppermute | solution.py:391
  104.5 5.4 %copy-start.2 = (bf16[128,2048]{1,0:T(8,128)(2,1)S(1)}, bf16[128,2048]{1,0:T(8,128)(2,1)}, u32[]{:S(2)}) copy-start(bf16[128,2048]{1,0:T(8,128)(2,1)} %k_ref.1) | copy-start | bytes 1572868
  104.5 5.4 %copy-start.3 = (bf16[128,2048]{1,0:T(8,128)(2,1)S(1)}, bf16[128,2048]{1,0:T(8,128)(2,1)}, u32[]{:S(2)}) copy-start(bf16[128,2048]{1,0:T(8,128)(2,1)} %v_ref.1) | copy-start | bytes 1572868
  104.5 4.1 %collective-permute-start.2 = (bf16[4,128,512]{2,1,0:T(8,128)(2,1)}, bf16[4,128,512]{2,1,0:T(8,128)(2,1)S(1)}, u32[]{:S(2)}, u32[]{:S(2)}) collective-permute-start(bf16[4,128,512]{2,1,0:T(8,128)(2,1)} %get-tuple-element.21), channel_id=1, source_target_pairs={{0,1},{1,0},{2,3},{3,2},{4,5},{5,4},{6,7},{7,6},{8,9},{9,8},{10,11... | collective-permute-start | bytes 1572872 | tf_op jit(solution)/shard_map/ppermute | solution.py:392

commit v5 on v4

v5 whole, which is shorter than its diff:
```python
import functools

import jax
import jax.numpy as jnp
from jax import lax
from jax.experimental import pallas as pl
from jax.experimental.pallas import tpu as pltpu
from jax.sharding import Mesh, PartitionSpec as P

HEAD_DIM = 128
GROUP = 512
MIB = 1024 * 1024
LIMITS = {
    "state": 53 * MIB,
    "pack": 56 * MIB,
    "total": 53 * MIB,
    "local": 51 * MIB,
    "prior": 53 * MIB,
    "mixed": 51 * MIB,
    "side": 56 * MIB,
    "later": 53 * MIB,
    "finish": 48 * MIB,
    "last": 50 * MIB,
}
OUTER_TURN = 4
INNER_TURN = 20
PAIR_TURN = INNER_TURN // 2
f32 = jnp.float32
bf16 = jnp.bfloat16


def dot_nn(a, b):
    return lax.dot_general(a, b, (((1,), (0,)), ((), ())), preferred_element_type=f32)


def dot_nt(a, b):
    return lax.dot_general(a, b, (((1,), (1,)), ((), ())), preferred_element_type=f32)


def dot_tn(a, b):
    return lax.dot_general(a, b, (((0,), (0,)), ((), ())), preferred_element_type=f32)


def shape(*dims, dtype=bf16):
    return jax.ShapeDtypeStruct(dims, dtype)


def call(kernel, out_shape, operands, limit, flops=0, far=(), far_out=(), smem=(), scratch=()):
    def space(i, kept):
        return pl.BlockSpec(memory_space=pltpu.HBM if i in kept else pltpu.VMEM)

    in_specs = [
        pl.BlockSpec(memory_space=pltpu.SMEM) if i in smem else space(i, far)
        for i in range(len(operands))
    ]
    out_specs = tuple(space(i, far_out) for i in range(len(out_shape)))
    moved = sum(x.size * x.dtype.itemsize for x in tuple(operands) + out_shape)
    return pl.pallas_call(
        kernel,
        out_shape=out_shape,
        in_specs=in_specs,
        out_specs=out_specs,
        scratch_shapes=scratch,
        compiler_params=pltpu.CompilerParams(vmem_limit_bytes=limit),
        cost_estimate=pl.CostEstimate(flops=flops, bytes_accessed=moved, transcendentals=0),
    )(*operands)


def copies_of(pairs, sems, first=0):
    return [
        pltpu.make_async_copy(src, dst, sems.at[first + i]) for i, (src, dst) in enumerate(pairs)
    ]


def start_all(copies):
    for copy in copies:
        copy.start()


def wait_all(copies):
    for copy in copies:
        copy.wait()


def columns(g, width=GROUP):
    return pl.ds(g * width, width)


def heads_of(g, width=GROUP):
    heads = range(g * width // HEAD_DIM, (g + 1) * width // HEAD_DIM)
    return [(h, slice(h * HEAD_DIM, (h + 1) * HEAD_DIM)) for h in heads]


def half(ref, which):
    count = ref.shape[-1] // 2
    return ref.at[:, pl.ds(pl.multiple_of(which * count, count), count)]


def rows_of(core, count):
    return pl.ds(pl.multiple_of(core * count, count), count)


def at_or_after(count, turned=False):
    rows = lax.broadcasted_iota(jnp.int32, (count, count), 0)
    cols = lax.broadcasted_iota(jnp.int32, (count, count), 1)
    return cols >= rows if turned else rows >= cols


def state_kernel(k_far, v_far, out_far, k_ref, v_ref, out_ref, sems, out_sems):
    pairs, _, rows, _ = out_far.shape
    cuts = HEAD_DIM // rows
    heads = pairs // cuts
    count = k_far.shape[1] // GROUP
    copies = [
        copies_of(
            [(src.at[:, columns(g)], dst.at[:, columns(g)]) for src, dst in ((k_far, k_ref), (v_far, v_ref))],
            sems, 2 * g,
        )
        for g in range(count)
    ]
    for group in copies:
        start_all(group)
    out_copies = []
    for g, group in enumerate(copies):
        wait_all(group)
        for h, cols in heads_of(g):
            state = dot_tn(k_ref[:, cols], v_ref[:, cols]).astype(bf16)
            for q in range(cuts):
                r = (h % heads) * cuts + q
                out_ref[r ^ PAIR_TURN, h // heads] = state[q * rows : (q + 1) * rows]
        block = pl.ds((g % 2) * (pairs // 2), pairs // 2)
        out_copies += copies_of(
            [(out_ref.at[block, g // 2], out_far.at[block, g // 2])], out_sems, g
        )
        out_copies[-1].start()
    wait_all(out_copies)


def total_kernel(parts_ref, after_far, out_ref):
    total = parts_ref[0].astype(f32)
    for j in range(1, parts_ref.shape[0]):
        total = total + parts_ref[j].astype(f32)
    total = total.astype(bf16)
    for j in range(out_ref.shape[0]):
        out_ref[j] = total


def outer_sum(reverse, place, totals_ref):
    acc = jnp.zeros(totals_ref.shape[1:], f32)
    for b in range(totals_ref.shape[0]):
        wanted = b > place if reverse else b < place
        acc = acc + jnp.where(wanted, totals_ref[b ^ OUTER_TURN].astype(f32), 0.0)
    return acc


def prior_kernel(place_ref, parts_ref, totals_ref, after_far, out_ref):
    acc = outer_sum(False, place_ref[0], totals_ref)
    for r in range(out_ref.shape[0]):
        out_ref[r ^ PAIR_TURN] = acc.astype(bf16)
        for i in (2 * r, 2 * r + 1):
            acc = acc + parts_ref[i ^ INNER_TURN].astype(f32)


def later_kernel(place_ref, parts_ref, totals_ref, out_far, out_ref, out_sems):
    acc = outer_sum(True, place_ref[0], totals_ref)
    pairs = parts_ref.shape[0]
    step = pairs // 4
    out_copies = []
    for r in reversed(range(pairs)):
        for c in range(2):
            out_ref[r ^ PAIR_TURN, c] = acc.astype(bf16)
        acc = acc + parts_ref[r ^ PAIR_TURN].astype(f32)
        if r % step == 0:
            block = pl.ds((r ^ PAIR_TURN) // step * step, step)
            out_copies += copies_of([(out_ref.at[block], out_far.at[block])], out_sems, r // step)
            out_copies[-1].start()
    wait_all(out_copies)


def pack_kernel(core_ref, q_far, k_far, v_far, g_far, out_ref, sems):
    other = 1 - core_ref[0]
    rows = (q_far, k_far, v_far, g_far)
    copies = copies_of([(half(src, other), out_ref.at[i]) for i, src in enumerate(rows)], sems)
    start_all(copies)
    wait_all(copies)


def local_kernel(
    core_ref, q_far, k_far, v_far, g_far, recv_far, inner_far, qg_far, kv_far,
    inner_ref, qg_ref, kv_ref, sems, out_sems,
):
    core = core_ref[0]
    count = q_far.shape[0]
    part = inner_far.shape[1]
    mine, theirs = rows_of(core, count), rows_of(1 - core, count)
    q_ref, k_ref, v_ref = qg_ref.at[0], kv_ref.at[0], kv_ref.at[1]
    near = (q_ref, k_ref, v_ref, qg_ref.at[1])
    copies = []
    for g in range(part // GROUP):
        own = pl.ds(pl.multiple_of(core * part + g * GROUP, GROUP), GROUP)
        pairs = [
            (src.at[:, own], dst.at[mine, columns(g)])
            for src, dst in zip((q_far, k_far, v_far, g_far), near)
        ]
        pairs += [(recv_far.at[i, :, columns(g)], dst.at[theirs, columns(g)]) for i, dst in enumerate(near)]
        copies.append(copies_of(pairs, sems, 8 * g))
    for group in copies:
        start_all(group)
    mask = at_or_after(2 * count)
    out_copies = []
    for g, group in enumerate(copies):
        wait_all(group)
        rows = copies_of(
            [(ref.at[:, :, columns(g)], far.at[:, :, columns(g)]) for ref, far in ((qg_ref, qg_far), (kv_ref, kv_far))],
            out_sems, 3 * g,
        )
        start_all(rows)
        heads = heads_of(g)
        scores = [dot_nt(q_ref[:, cols], k_ref[:, cols]) for _, cols in heads]
        local = [jnp.where(mask, x, 0.0).astype(bf16) for x in scores]
        for (_, cols), x in zip(heads, local):
            inner_ref[:, cols] = dot_nn(x, v_ref[:, cols])
        mixed = copies_of([(inner_ref.at[:, columns(g)], inner_far.at[:, columns(g)])], out_sems, 3 * g + 2)
        start_all(mixed)
        out_copies += rows + mixed
    wait_all(out_copies)


def whole_state(ref, h):
    cuts = HEAD_DIM // ref.shape[1]
    return jnp.concatenate([ref[(h * cuts + q) ^ PAIR_TURN] for q in range(cuts)], axis=0)


def normed_parts(mixed, grad):
    scale = lax.rsqrt(jnp.mean(mixed * mixed, axis=-1, keepdims=True) + 1e-06)
    inner_mean = jnp.mean(grad * mixed, axis=-1, keepdims=True)
    dy = (scale * grad - mixed * (scale * scale * scale * inner_mean)).astype(bf16)
    return scale, dy


def mixed_kernel(qg_ref, inner_far, prior_ref, state_far, inner_ref, state_ref, sems, out_sems):
    pairs, rows, _ = state_ref.shape
    cuts = HEAD_DIM // rows
    q_ref, g_ref = qg_ref.at[0], qg_ref.at[1]
    count = q_ref.shape[1] // GROUP
    copies = copies_of([(inner_far.at[:, columns(g)], inner_ref.at[:, columns(g)]) for g in range(count)], sems)
    start_all(copies)
    out_copies = []
    for g, copy in enumerate(copies):
        copy.wait()
        for h, cols in heads_of(g):
            query = q_ref[:, cols]
            mixed = inner_ref[:, cols] + dot_nn(query, whole_state(prior_ref, h))
            _, dy = normed_parts(mixed, g_ref[:, cols].astype(f32))
            state = dot_tn(query, dy).astype(bf16)
            for q in range(cuts):
                state_ref[(h * cuts + q) ^ PAIR_TURN] = state[q * rows : (q + 1) * rows]
        block = pl.ds(g * (pairs // count), pairs // count)
        out_copies += copies_of([(state_ref.at[block], state_far.at[block])], out_sems, g)
        out_copies[-1].start()
    wait_all(out_copies)


def side_kernel(
    core_ref, qg_far, kv_far, inner_far, prior_far, own_far, send_far,
    qg_ref, kv_ref, inner_ref, prior_ref, tile_ref, sems, prior_sem, out_sems,
):
    core = core_ref[0]
    count = own_far.shape[1]
    q_ref, g_ref, k_ref, v_ref = qg_ref.at[0], qg_ref.at[1], kv_ref.at[0], kv_ref.at[1]
    prior_copy = copies_of([(prior_far, prior_ref)], prior_sem)
    start_all(prior_copy)
    copies = [
        copies_of(
            [
                (qg_far.at[:, :, columns(g)], qg_ref.at[:, :, columns(g)]),
                (inner_far.at[:, columns(g)], inner_ref.at[:, columns(g)]),
                (kv_far.at[:, :, columns(g)], kv_ref.at[:, :, columns(g)]),
            ],
            sems, 3 * g,
        )
        for g in range(inner_ref.shape[1] // GROUP)
    ]
    for group in copies:
        start_all(group)
    mask = at_or_after(2 * count)
    turned = at_or_after(2 * count, True)
    mine, theirs = rows_of(core, count), rows_of(1 - core, count)
    wait_all(prior_copy)
    out_copies = []
    for g, group in enumerate(copies):
        wait_all(group)
        heads = heads_of(g)
        queries = [q_ref[:, cols] for _, cols in heads]
        key_rows = [k_ref[:, cols] for _, cols in heads]
        value_rows = [v_ref[:, cols] for _, cols in heads]
        priors = [whole_state(prior_ref, h) for h, _ in heads]
        mixed = [inner_ref[:, cols] + dot_nn(q, p) for (_, cols), q, p in zip(heads, queries, priors)]
        local_t = [
            jnp.where(turned, dot_nt(k, q), 0.0).astype(bf16) for k, q in zip(key_rows, queries)
        ]
        normed = [normed_parts(x, g_ref[:, cols].astype(f32)) for x, (_, cols) in zip(mixed, heads)]
        dlocal = [
            jnp.where(mask, dot_nt(dy, v), 0.0).astype(bf16) for (_, dy), v in zip(normed, value_rows)
        ]
        dlocal_t = [
            jnp.where(turned, dot_nt(v, dy), 0.0).astype(bf16) for (_, dy), v in zip(normed, value_rows)
        ]
        for i, (_, cols) in enumerate(heads):
            scale, dy = normed[i]
            tile_ref[0, :, cols] = (mixed[i] * scale).astype(bf16)
            tile_ref[1, :, cols] = (dot_nn(dlocal[i], key_rows[i]) + dot_nt(dy, priors[i])).astype(bf16)
            tile_ref[2, :, cols] = dot_nn(dlocal_t[i], queries[i]).astype(bf16)
            tile_ref[3, :, cols] = dot_nn(local_t[i], dy).astype(bf16)
        group_out = copies_of(
            [
                (tile_ref.at[:, mine, columns(g)], own_far.at[:, :, columns(g)]),
                (tile_ref.at[:, theirs, columns(g)], send_far.at[:, :, columns(g)]),
            ],
            out_sems, 2 * g,
        )
        start_all(group_out)
        out_copies += group_out
    wait_all(out_copies)


def swapped_copies(core, first, outs, own_far, recv_far, sems):
    pairs = [(own_far.at[first + i], half(dst, core)) for i, dst in enumerate(outs)]
    pairs += [(recv_far.at[first + i], half(dst, 1 - core)) for i, dst in enumerate(outs)]
    return copies_of(pairs, sems)


def finish_kernel(core_ref, own_far, recv_far, attended_ref, gq_ref, sems):
    copies = swapped_copies(core_ref[0], 0, (attended_ref, gq_ref), own_far, recv_far, sems)
    start_all(copies)
    wait_all(copies)


def last_kernel(
    core_ref, k_ref, v_ref, own_far, recv_far, later_far, out_k_far, out_v_far,
    gk_ref, gv_ref, later_ref, out_k_ref, out_v_ref, sems, later_sem, out_sems,
):
    cuts = HEAD_DIM // later_far.shape[1]
    heads = later_far.shape[0] // cuts // 2
    copies = copies_of([(later_far, later_ref)], later_sem)
    copies += swapped_copies(core_ref[0], 2, (gk_ref, gv_ref), own_far, recv_far, sems)
    start_all(copies)
    wait_all(copies)
    out_copies = []
    for g in range(k_ref.shape[1] // GROUP):
        for h, cols in heads_of(g):
            places = [2 * ((h % heads) * cuts + q) + h // heads for q in range(cuts)]
            later = jnp.concatenate([later_ref[i ^ INNER_TURN] for i in places], axis=0)
            gk = gk_ref[:, cols].astype(f32) + dot_nt(v_ref[:, cols], later)
            gv = gv_ref[:, cols].astype(f32) + dot_nn(k_ref[:, cols], later)
            out_k_ref[:, cols] = gk.astype(bf16)
            out_v_ref[:, cols] = gv.astype(bf16)
        group = copies_of(
            [
                (near.at[:, columns(g)], far.at[:, columns(g)])
                for near, far in ((out_k_ref, out_k_far), (out_v_ref, out_v_far))
            ],
            out_sems, 2 * g,
        )
        start_all(group)
        out_copies += group
    wait_all(out_copies)


def exchange(blocks, axis, groups):
    return lax.all_to_all(blocks, axis, 0, 0, tiled=True, axis_index_groups=groups)


def per_device(query, keys, values, grads):
    tokens, width = query.shape
    part = width // 2
    pairs = lax.axis_size("inner") // 2
    blocks = lax.axis_size("outer")
    slice_rows = part // pairs
    groups = width // GROUP
    part_groups = part // GROUP
    unit = 2 * tokens * width * HEAD_DIM
    core = (lax.axis_index("inner").astype(jnp.int32) % 2).reshape(1)
    place = lax.axis_index("outer").astype(jnp.int32).reshape(1)
    swap = [(i, i ^ 1) for i in range(2 * pairs)]
    outer_groups = [[b ^ OUTER_TURN for b in range(blocks)]]
    inner_groups = [[i ^ INNER_TURN for i in range(2 * pairs)]]
    pair_groups = [[2 * (r ^ PAIR_TURN) + c for r in range(pairs)] for c in range(2)]

    def vmem(*dims, dtype=bf16):
        return pltpu.VMEM(dims, dtype)

    def sems(count):
        return pltpu.SemaphoreType.DMA((count,))

    rows = vmem(tokens, width)
    totals_shape = (shape(blocks, slice_rows, HEAD_DIM),)
    half_states = shape(pairs, slice_rows, HEAD_DIM)
    states = shape(pairs, 2, slice_rows, HEAD_DIM)
    pair_tiles = shape(2, 2 * tokens, part)
    inner_shape = shape(2 * tokens, part, dtype=f32)
    out = shape(tokens, width)

    (kv,) = call(
        state_kernel, (states,), (keys, values), LIMITS["state"], unit,
        far=(0, 1), far_out=(0,),
        scratch=(rows, rows, vmem(*states.shape), sems(2 * groups), sems(groups)),
    )
    kv_parts = exchange(kv.reshape(-1, slice_rows, HEAD_DIM), "inner", inner_groups)
    (send,) = call(
        pack_kernel, (shape(4, tokens, part),), (core, query, keys, values, grads), LIMITS["pack"],
        far=(1, 2, 3, 4), smem=(0,), scratch=(sems(4),),
    )
    recv = lax.ppermute(send, "inner", swap)
    (sent,) = call(total_kernel, totals_shape, (kv_parts, send), LIMITS["total"], far=(1,))
    kv_totals = exchange(sent, "outer", outer_groups)
    inner, qg, kv_pair = call(
        local_kernel, (inner_shape, pair_tiles, pair_tiles),
        (core, query, keys, values, grads, recv), LIMITS["local"], 4 * unit,
        far=(1, 2, 3, 4, 5), far_out=(0, 1, 2), smem=(0,),
        scratch=(
            vmem(2 * tokens, part, dtype=f32), vmem(*pair_tiles.shape), vmem(*pair_tiles.shape),
            sems(8 * part_groups), sems(3 * part_groups),
        ),
    )
    (running,) = call(
        prior_kernel, (half_states,), (place, kv_parts, kv_totals, qg), LIMITS["prior"],
        far=(3,), smem=(0,),
    )
    prior = exchange(running, "inner", pair_groups)
    (gq_state,) = call(
        mixed_kernel, (half_states,), (qg, inner, prior), LIMITS["mixed"], 2 * unit,
        far=(1,), far_out=(0,),
        scratch=(
            vmem(2 * tokens, part, dtype=f32), vmem(*half_states.shape),
            sems(part_groups), sems(part_groups),
        ),
    )
    gq_parts = exchange(gq_state, "inner", pair_groups)
    swapped = shape(4, tokens, part)
    own, send = call(
        side_kernel, (swapped, swapped), (core, qg, kv_pair, inner, prior), LIMITS["side"], 10 * unit,
        far=(1, 2, 3, 4), far_out=(0, 1), smem=(0,),
        scratch=(
            vmem(*pair_tiles.shape), vmem(*pair_tiles.shape), vmem(2 * tokens, part, dtype=f32),
            vmem(*half_states.shape), vmem(4, 2 * tokens, part),
            sems(3 * part_groups), sems(1), sems(2 * part_groups),
        ),
    )
    (sent,) = call(total_kernel, totals_shape, (gq_parts, own), LIMITS["total"], far=(1,))
    gq_totals = exchange(sent, "outer", outer_groups)
    (running,) = call(
        later_kernel, (states,), (place, gq_parts, gq_totals), LIMITS["later"],
        far_out=(0,), smem=(0,), scratch=(vmem(*states.shape), sems(4)),
    )
    later = exchange(running.reshape(-1, slice_rows, HEAD_DIM), "inner", inner_groups)
    recv = lax.ppermute(send, "inner", swap)
    attended, grad_query = call(
        finish_kernel, (out, out), (core, own, recv), LIMITS["finish"],
        far=(1, 2), smem=(0,), scratch=(sems(4),),
    )
    grad_key, grad_value = call(
        last_kernel, (out, out), (core, keys, values, own, recv, later), LIMITS["last"], 2 * unit,
        far=(3, 4, 5), far_out=(0, 1), smem=(0,),
        scratch=(rows, rows, vmem(*later.shape), rows, rows, sems(4), sems(1), sems(2 * groups)),
    )
    return attended, grad_query, grad_key, grad_value


def solution(mesh):
    split = Mesh(mesh.devices.reshape(-1, 64), ("outer", "inner"))
    placed = P(("outer", "inner"), None)
    return jax.shard_map(
        per_device,
        mesh=split,
        in_specs=(placed,) * 4,
        out_specs=(placed,) * 4,
        check_vma=False,
    )
```

time: 113 us -> 110 us (0.973)
  blocking collectives: 11.4 us -> 26.2 us
  starting transfers between devices: 67.1 us -> 54 us
  Pallas kernels: 25.9 us -> 20.8 us
  waiting for transfers between devices: 5.24 us -> 7.36 us
  local copies, waits for them, and re-layouts: 2.03 us -> 0.04 us
    all_to_all x1 -> x2, blocking collectives: 11.4 us -> 26.2 us  [exchange(): lax.all_to_all(blocks, axis, 0, 0, tiled=True, axis_index_groups=groups)]
    all_to_all x5 -> x4, starting transfers between devices: 60.4 us -> 49.4 us  [exchange(): lax.all_to_all(blocks, axis, 0, 0, tiled=True, axis_index_groups=groups)]
    pallas_call x12 -> x11, Pallas kernels: 25.9 us -> 20.8 us  [call(): pl.pallas_call(kernel, out_shape=out_shape, in_specs=in_specs, out_specs=...]
    ppermute x2 -> x0, starting transfers between devices: 4.46 us -> none  [the longest x1 2.27 us: per_device(): recv_a = lax.ppermute(send_a, 'inner', swap)]
    ppermute x1 -> x2, waiting for transfers between devices: 0.01 us -> 2.49 us  [per_device(): recv = lax.ppermute(send, 'inner', swap)]
    ppermute x1 -> x2, starting transfers between devices: 2.27 us -> 4.67 us  [per_device(): recv = lax.ppermute(send, 'inner', swap)]
    unnamed x18 -> x16, local copies, waits for them, and re-layouts: 2.03 us -> 0.04 us
    ppermute x2 -> x0, waiting for transfers between devices: 1.94 us -> none  [the longest x1 1.94 us: per_device(): recv_b = lax.ppermute(send_b, 'inner', swap)]
  transfers between devices with their start and end apart: 8 -> 6, of which waited for: 3 -> 3; matrix products, arithmetic and copies ran while one was open for 0% -> 0% of each run, Pallas kernels for 15% -> 12%
where the time goes in v5:
time: 110 us; the launch traced here: 109 us
  starting transfers between devices  54 us (49%)
  blocking collectives  26.2 us (24%)
  Pallas kernels  20.8 us (19%)
  waiting for transfers between devices  7.36 us (7%)
    all_to_all x4, starting transfers between devices, exchange(): lax.all_to_all(blocks, axis, 0, 0, tiled=True, axis_index_groups=groups)  49.4 us
    all_to_all x2, blocking collectives, exchange(): lax.all_to_all(blocks, axis, 0, 0, tiled=True, axis_index_groups=groups)  26.2 us
    pallas_call x11, Pallas kernels, call(): pl.pallas_call(kernel, out_shape=out_shape, in_specs=in_specs, out_specs=...  20.8 us
    all_to_all x4, waiting for transfers between devices, exchange(): lax.all_to_all(blocks, axis, 0, 0, tiled=True, axis_index_groups=groups)  4.87 us
    ppermute x2, starting transfers between devices, per_device(): recv = lax.ppermute(send, 'inner', swap)  4.67 us
    ppermute x2, waiting for transfers between devices, per_device(): recv = lax.ppermute(send, 'inner', swap)  2.49 us
  transfers between devices with their start and end apart: 6, of which 3 were waited for; matrix products, arithmetic and copies ran while one was open for 0% of the time, Pallas kernels for 12%

profile of v5, /device:TPU:1, one launch (start us, length us, event | category | flops | bytes accessed | tf_op | source)
XLA Modules:
  0.0 109.3 jit_solution(5860704788718411362)
XLA Ops:
  0.6 2.6 %shard_map.77 = bf16[32,2,32,128]{3,2,1,0:T(8,128)(2,1)} custom-call(bf16[128,2048]{1,0:T(8,128)(2,1)} %k_ref.1, bf16[128,2048]{1,0:T(8,128)(2,1)} %v_ref.1), custom_call_target="tpu_custom_call" | custom-call | flops 67108864 | bytes 1572864 | tf_op jit(solution)/shard_map/pallas_call | solution.py:58
  3.2 14.3 %all-to-all-start = ((bf16[64,32,128]{2,1,0:T(8,128)(2,1)}), bf16[64,32,128]{2,1,0:T(8,128)(2,1)S(1)}, u32[]{:S(2)}, u32[]{:S(2)}) async-start(bf16[64,32,128]{2,1,0:T(8,128)(2,1)} %bitcast.2), calls=%async_computation | async-start | bytes 1048576 | tf_op jit(solution)/shard_map/all_to_all | solution.py:371
  17.6 0.0 copy-start.7
  17.6 2.3 %shard_map.75.after_far = bf16[4,128,1024]{2,1,0:T(8,128)(2,1)} custom-call(s32[1]{0:T(128)} %bitcast.core_ref, bf16[128,2048]{1,0:T(8,128)(2,1)} %q_far.3, bf16[128,2048]{1,0:T(8,128)(2,1)} %k_ref.1, bf16[128,2048]{1,0:T(8,128)(2,1)} %v_ref.1, bf16[128,2048]{1,0:T(8,128)(2,1)} %g_far.3), custom_call_target="tpu_custom_call" | custom-call | bytes 3145732 | tf_op jit(solution)/shard_map/pallas_call | solution.py:58
  19.9 0.0 copy-start.2
  19.9 0.0 copy-start.3
  19.9 0.0 copy-start.6
  19.9 2.4 %collective-permute-start = (bf16[4,128,1024]{2,1,0:T(8,128)(2,1)}, bf16[4,128,1024]{2,1,0:T(8,128)(2,1)}, u32[]{:S(2)}, u32[]{:S(2)}) collective-permute-start(bf16[4,128,1024]{2,1,0:T(8,128)(2,1)} %shard_map.75.after_far), channel_id=1, source_target_pairs={{0,1},{1,0},{2,3},{3,2},{4,5},{5,4},{6,7},{7,6},{8,9},{9,8},{10,11... | collective-permute-start | bytes 3145736 | tf_op jit(solution)/shard_map/ppermute | solution.py:414
  22.3 3.0 %all-to-all-done.parts_ref = bf16[64,32,128]{2,1,0:T(8,128)(2,1)S(1)} async-done(((bf16[64,32,128]{2,1,0:T(8,128)(2,1)}), bf16[64,32,128]{2,1,0:T(8,128)(2,1)S(1)}, u32[]{:S(2)}, u32[]{:S(2)}) %all-to-all-start) | async-done | bytes 524320 | tf_op jit(solution)/shard_map/all_to_all | solution.py:371
  25.3 0.7 shard_map.78
  26.1 14.5 %all-to-all-start.1 = ((bf16[8,32,128]{2,1,0:T(8,128)(2,1)}), bf16[8,32,128]{2,1,0:T(8,128)(2,1)S(1)}, u32[]{:S(2)}, u32[]{:S(2)}) async-start(bf16[8,32,128]{2,1,0:T(8,128)(2,1)} %shard_map.78), calls=%async_computation.1 | async-start | bytes 131072 | tf_op jit(solution)/shard_map/all_to_all | solution.py:371
  40.6 0.0 collective-permute-done.recv_far
  40.6 0.0 copy-done.7
  40.6 0.0 copy-done.2
  40.6 0.0 copy-done.3
  40.6 0.0 copy-done.6
  40.6 3.2 %shard_map.76 = (f32[256,1024]{1,0:T(8,128)}, bf16[2,256,1024]{2,1,0:T(8,128)(2,1)}, bf16[2,256,1024]{2,1,0:T(8,128)(2,1)}) custom-call(s32[1]{0:T(128)} %bitcast.core_ref, bf16[128,2048]{1,0:T(8,128)(2,1)S(1)} %copy-done.6, bf16[128,2048]{1,0:T(8,128)(2,1)S(1)} %copy-done.2, bf16[128,2048]{1,0:T(8,128)(2,1)S(1)} %copy-done.3, ...), custom_call_target="tpu_custom_call" | custom-call | flops 268435456 | bytes 6291460 | tf_op jit(solution)/shard_map/pallas_call | solution.py:58
  43.8 0.0 all-to-all-done.1.totals_ref
  43.8 0.0 copy-start
  43.9 0.0 copy-start.4
  43.9 0.1 shard_map.79
  44.0 11.7 %all_to_all.30.prior_far.prior_ref = bf16[32,32,128]{2,1,0:T(8,128)(2,1)S(1)} all-to-all(bf16[32,32,128]{2,1,0:T(8,128)(2,1)S(1)} %shard_map.79), channel_id=1, replica_groups={{20,22,16,18,28,30,24,26,4,6,0,2,12,14,8,10,52,54,48,50,60,62,56,58,36,..., dimensions={0} | all-to-all | bytes 524288 | tf_op jit(solution)/shard_map/all_to_all | solution.py:371
  55.7 0.0 copy-start.5
  55.7 0.0 copy-done
  55.7 0.0 copy-done.4
  55.7 2.1 %shard_map.82 = bf16[32,32,128]{2,1,0:T(8,128)(2,1)} custom-call(bf16[2,256,1024]{2,1,0:T(8,128)(2,1)S(1)} %copy-done, f32[256,1024]{1,0:T(8,128)S(1)} %copy-done.4, bf16[32,32,128]{2,1,0:T(8,128)(2,1)S(1)} %all_to_all.30.prior_far.prior_ref), custom_call_target="tpu_custom_call" | custom-call | flops 134217728 | bytes 2621440 | tf_op jit(solution)/shard_map/pallas_call | solution.py:58
  57.9 0.0 copy-done.5
  57.9 7.4 %all-to-all-start.3 = ((bf16[32,32,128]{2,1,0:T(8,128)(2,1)}), bf16[32,32,128]{2,1,0:T(8,128)(2,1)S(1)}, u32[]{:S(2)}, u32[]{:S(2)}) async-start(bf16[32,32,128]{2,1,0:T(8,128)(2,1)} %shard_map.82), calls=%async_computation.3 | async-start | bytes 524288 | tf_op jit(solution)/shard_map/all_to_all | solution.py:371
  65.3 5.4 %shard_map.80 = (bf16[4,128,1024]{2,1,0:T(8,128)(2,1)}, bf16[4,128,1024]{2,1,0:T(8,128)(2,1)}) custom-call(s32[1]{0:T(128)} %bitcast.core_ref, bf16[2,256,1024]{2,1,0:T(8,128)(2,1)} %get-tuple-element.13.after_far.qg_far.qg_ref, bf16[2,256,1024]{2,1,0:T(8,128)(2,1)} %get-tuple-element.14.kv_far, f32[256,1024]{1,0:T(8,128)} %get-tuple-element.15.inner_far, ...), custom_call_target="tpu_custom_call" | custom-call | flops 671088640 | bytes 5505028 | tf_op jit(solution)/shard_map/pallas_call | solution.py:58
  70.7 0.0 all-to-all-done.3.parts_ref
  70.8 0.0 copy-start.1
  70.8 14.4 %all_to_all.31.totals_ref = bf16[8,32,128]{2,1,0:T(8,128)(2,1)S(1)} all-to-all(bf16[8,32,128]{2,1,0:T(8,128)(2,1)S(1)} %shard_map.83), channel_id=1, replica_groups={{256,320,384,448,0,64,128,192},{257,321,385,449,1,65,129,193},{258,322,..., dimensions={0} | all-to-all | bytes 131072 | tf_op jit(solution)/shard_map/all_to_all | solution.py:371
  85.2 0.8 shard_map.84
  86.0 13.1 %all-to-all-start.5 = ((bf16[64,32,128]{2,1,0:T(8,128)(2,1)}), bf16[64,32,128]{2,1,0:T(8,128)(2,1)}, u32[]{:S(2)}, u32[]{:S(2)}) async-start(bf16[64,32,128]{2,1,0:T(8,128)(2,1)} %bitcast.3), calls=%async_computation.5 | async-start | bytes 1048576 | tf_op jit(solution)/shard_map/all_to_all | solution.py:371
  99.1 2.3 %collective-permute-start.1 = (bf16[4,128,1024]{2,1,0:T(8,128)(2,1)}, bf16[4,128,1024]{2,1,0:T(8,128)(2,1)S(1)}, u32[]{:S(2)}, u32[]{:S(2)}) collective-permute-start(bf16[4,128,1024]{2,1,0:T(8,128)(2,1)} %get-tuple-element.17), channel_id=1, source_target_pairs={{0,1},{1,0},{2,3},{3,2},{4,5},{5,4},{6,7},{7,6},{8,9},{9,8},{10,11... | collective-permute-start | bytes 3145736 | tf_op jit(solution)/shard_map/ppermute | solution.py:457
  101.4 2.5 %collective-permute-done.1.recv_far = bf16[4,128,1024]{2,1,0:T(8,128)(2,1)S(1)} collective-permute-done((bf16[4,128,1024]{2,1,0:T(8,128)(2,1)}, bf16[4,128,1024]{2,1,0:T(8,128)(2,1)S(1)}, u32[]{:S(2)}, u32[]{:S(2)}) %collective-permute-start.1) | collective-permute-done | bytes 1048608 | tf_op jit(solution)/shard_map/ppermute | solution.py:457
  103.9 0.0 copy-done.1
  103.9 1.1 shard_map.81
  105.0 1.8 %all-to-all-done.5.later_far = bf16[64,32,128]{2,1,0:T(8,128)(2,1)} async-done(((bf16[64,32,128]{2,1,0:T(8,128)(2,1)}), bf16[64,32,128]{2,1,0:T(8,128)(2,1)}, u32[]{:S(2)}, u32[]{:S(2)}) %all-to-all-start.5) | async-done | bytes 524320 | tf_op jit(solution)/shard_map/all_to_all | solution.py:371
  106.8 2.4 %shard_map.85 = (bf16[128,2048]{1,0:T(8,128)(2,1)}, bf16[128,2048]{1,0:T(8,128)(2,1)}) custom-call(s32[1]{0:T(128)} %bitcast.core_ref, bf16[128,2048]{1,0:T(8,128)(2,1)S(1)} %copy-done.2, bf16[128,2048]{1,0:T(8,128)(2,1)S(1)} %copy-done.3, bf16[4,128,1024]{2,1,0:T(8,128)(2,1)S(1)} %copy-done.1, bf16[4,128,1024]{2,1,0:T(8,128)(2,1)S(1)} %collective-permute-done.1.recv_far, ...), custom_call_target="tpu_custom_call" | custom-call | flops 134217728 | bytes 4718596 | tf_op jit(solution)/shard_map/pallas_call | solution.py:58
  (1 shorter events, 0.0 us)
Async XLA Ops:
  3.2 22.1 %all-to-all-start = ((bf16[64,32,128]{2,1,0:T(8,128)(2,1)}), bf16[64,32,128]{2,1,0:T(8,128)(2,1)S(1)}, u32[]{:S(2)}, u32[]{:S(2)}) async-start(bf16[64,32,128]{2,1,0:T(8,128)(2,1)} %bitcast.2), calls=%async_computation | async-start | bytes 1048576 | tf_op jit(solution)/shard_map/all_to_all | solution.py:371
  17.6 23.0 %copy-start.7 = (bf16[128,2048]{1,0:T(8,128)(2,1)S(1)}, bf16[128,2048]{1,0:T(8,128)(2,1)}, u32[]{:S(2)}) copy-start(bf16[128,2048]{1,0:T(8,128)(2,1)} %g_far.3) | copy-start | bytes 1572868
  19.9 20.7 %copy-start.2 = (bf16[128,2048]{1,0:T(8,128)(2,1)S(1)}, bf16[128,2048]{1,0:T(8,128)(2,1)}, u32[]{:S(2)}) copy-start(bf16[128,2048]{1,0:T(8,128)(2,1)} %k_ref.1) | copy-start | bytes 1572868
  19.9 20.7 %copy-start.3 = (bf16[128,2048]{1,0:T(8,128)(2,1)S(1)}, bf16[128,2048]{1,0:T(8,128)(2,1)}, u32[]{:S(2)}) copy-start(bf16[128,2048]{1,0:T(8,128)(2,1)} %v_ref.1) | copy-start | bytes 1572868
  19.9 20.7 %copy-start.6 = (bf16[128,2048]{1,0:T(8,128)(2,1)S(1)}, bf16[128,2048]{1,0:T(8,128)(2,1)}, u32[]{:S(2)}) copy-start(bf16[128,2048]{1,0:T(8,128)(2,1)} %q_far.3) | copy-start | bytes 1572868
  19.9 20.7 %collective-permute-start = (bf16[4,128,1024]{2,1,0:T(8,128)(2,1)}, bf16[4,128,1024]{2,1,0:T(8,128)(2,1)}, u32[]{:S(2)}, u32[]{:S(2)}) collective-permute-start(bf16[4,128,1024]{2,1,0:T(8,128)(2,1)} %shard_map.75.after_far), channel_id=1, source_target_pairs={{0,1},{1,0},{2,3},{3,2},{4,5},{5,4},{6,7},{7,6},{8,9},{9,8},{10,11... | collective-permute-start | bytes 3145736 | tf_op jit(solution)/shard_map/ppermute | solution.py:414
  26.1 17.8 %all-to-all-start.1 = ((bf16[8,32,128]{2,1,0:T(8,128)(2,1)}), bf16[8,32,128]{2,1,0:T(8,128)(2,1)S(1)}, u32[]{:S(2)}, u32[]{:S(2)}) async-start(bf16[8,32,128]{2,1,0:T(8,128)(2,1)} %shard_map.78), calls=%async_computation.1 | async-start | bytes 131072 | tf_op jit(solution)/shard_map/all_to_all | solution.py:371
  43.8 11.9 %copy-start = (bf16[2,256,1024]{2,1,0:T(8,128)(2,1)S(1)}, bf16[2,256,1024]{2,1,0:T(8,128)(2,1)}, u32[]{:S(2)}) copy-start(bf16[2,256,1024]{2,1,0:T(8,128)(2,1)} %get-tuple-element.13.after_far.qg_far.qg_ref) | copy-start | bytes 3145732
  43.9 11.9 %copy-start.4 = (f32[256,1024]{1,0:T(8,128)S(1)}, f32[256,1024]{1,0:T(8,128)}, u32[]{:S(2)}) copy-start(f32[256,1024]{1,0:T(8,128)} %get-tuple-element.15.inner_far) | copy-start | bytes 3145732
  55.7 2.1 %copy-start.5 = (bf16[32,32,128]{2,1,0:T(8,128)(2,1)}, bf16[32,32,128]{2,1,0:T(8,128)(2,1)S(1)}, u32[]{:S(2)}) copy-start(bf16[32,32,128]{2,1,0:T(8,128)(2,1)S(1)} %all_to_all.30.prior_far.prior_ref) | copy-start | bytes 786436
  57.9 12.8 %all-to-all-start.3 = ((bf16[32,32,128]{2,1,0:T(8,128)(2,1)}), bf16[32,32,128]{2,1,0:T(8,128)(2,1)S(1)}, u32[]{:S(2)}, u32[]{:S(2)}) async-start(bf16[32,32,128]{2,1,0:T(8,128)(2,1)} %shard_map.82), calls=%async_computation.3 | async-start | bytes 524288 | tf_op jit(solution)/shard_map/all_to_all | solution.py:371
  70.8 33.2 %copy-start.1 = (bf16[4,128,1024]{2,1,0:T(8,128)(2,1)S(1)}, bf16[4,128,1024]{2,1,0:T(8,128)(2,1)}, u32[]{:S(2)}) copy-start(bf16[4,128,1024]{2,1,0:T(8,128)(2,1)} %get-tuple-element.16.own_far.after_far) | copy-start | bytes 3145732
  86.0 20.8 %all-to-all-start.5 = ((bf16[64,32,128]{2,1,0:T(8,128)(2,1)}), bf16[64,32,128]{2,1,0:T(8,128)(2,1)}, u32[]{:S(2)}, u32[]{:S(2)}) async-start(bf16[64,32,128]{2,1,0:T(8,128)(2,1)} %bitcast.3), calls=%async_computation.5 | async-start | bytes 1048576 | tf_op jit(solution)/shard_map/all_to_all | solution.py:371
  99.1 4.8 %collective-permute-start.1 = (bf16[4,128,1024]{2,1,0:T(8,128)(2,1)}, bf16[4,128,1024]{2,1,0:T(8,128)(2,1)S(1)}, u32[]{:S(2)}, u32[]{:S(2)}) collective-permute-start(bf16[4,128,1024]{2,1,0:T(8,128)(2,1)} %get-tuple-element.17), channel_id=1, source_target_pairs={{0,1},{1,0},{2,3},{3,2},{4,5},{5,4},{6,7},{7,6},{8,9},{9,8},{10,11... | collective-permute-start | bytes 3145736 | tf_op jit(solution)/shard_map/ppermute | solution.py:457

commit v6 on v5

--- a/solution.py
+++ b/solution.py
@@ -16,15 +16,15 @@
     "total": 53 * MIB,
     "local": 51 * MIB,
     "prior": 53 * MIB,
-    "mixed": 51 * MIB,
+    "mixed": 50 * MIB,
     "side": 56 * MIB,
     "later": 53 * MIB,
     "finish": 48 * MIB,
     "last": 50 * MIB,
 }
 OUTER_TURN = 4
-INNER_TURN = 20
-PAIR_TURN = INNER_TURN // 2
+INNER_TURN = 53
+PAIR_TURN, CORE_TURN = INNER_TURN // 2, INNER_TURN % 2
 f32 = jnp.float32
 bf16 = jnp.bfloat16
 
@@ -100,6 +100,10 @@
     return pl.ds(pl.multiple_of(core * count, count), count)
 
 
+def turned_block(g, size):
+    return pl.ds((g * size) ^ (PAIR_TURN // size * size), size)
+
+
 def at_or_after(count, turned=False):
     rows = lax.broadcasted_iota(jnp.int32, (count, count), 0)
     cols = lax.broadcasted_iota(jnp.int32, (count, count), 1)
@@ -127,10 +131,10 @@
             state = dot_tn(k_ref[:, cols], v_ref[:, cols]).astype(bf16)
             for q in range(cuts):
                 r = (h % heads) * cuts + q
-                out_ref[r ^ PAIR_TURN, h // heads] = state[q * rows : (q + 1) * rows]
-        block = pl.ds((g % 2) * (pairs // 2), pairs // 2)
+                out_ref[r ^ PAIR_TURN, h // heads ^ CORE_TURN] = state[q * rows : (q + 1) * rows]
+        block, core = turned_block(g % 2, pairs // 2), g // 2 ^ CORE_TURN
         out_copies += copies_of(
-            [(out_ref.at[block, g // 2], out_far.at[block, g // 2])], out_sems, g
+            [(out_ref.at[block, core], out_far.at[block, core])], out_sems, g
         )
         out_copies[-1].start()
     wait_all(out_copies)
@@ -238,16 +242,13 @@
     return scale, dy
 
 
-def mixed_kernel(qg_ref, inner_far, prior_ref, state_far, inner_ref, state_ref, sems, out_sems):
+def mixed_kernel(qg_ref, inner_ref, prior_ref, state_far, state_ref, out_sems):
     pairs, rows, _ = state_ref.shape
     cuts = HEAD_DIM // rows
     q_ref, g_ref = qg_ref.at[0], qg_ref.at[1]
     count = q_ref.shape[1] // GROUP
-    copies = copies_of([(inner_far.at[:, columns(g)], inner_ref.at[:, columns(g)]) for g in range(count)], sems)
-    start_all(copies)
-    out_copies = []
-    for g, copy in enumerate(copies):
-        copy.wait()
+    out_copies = []
+    for g in range(count):
         for h, cols in heads_of(g):
             query = q_ref[:, cols]
             mixed = inner_ref[:, cols] + dot_nn(query, whole_state(prior_ref, h))
@@ -255,7 +256,7 @@
             state = dot_tn(query, dy).astype(bf16)
             for q in range(cuts):
                 state_ref[(h * cuts + q) ^ PAIR_TURN] = state[q * rows : (q + 1) * rows]
-        block = pl.ds(g * (pairs // count), pairs // count)
+        block = turned_block(g, pairs // count)
         out_copies += copies_of([(state_ref.at[block], state_far.at[block])], out_sems, g)
         out_copies[-1].start()
     wait_all(out_copies)
@@ -306,21 +307,24 @@
         dlocal_t = [
             jnp.where(turned, dot_nt(v, dy), 0.0).astype(bf16) for (_, dy), v in zip(normed, value_rows)
         ]
-        for i, (_, cols) in enumerate(heads):
-            scale, dy = normed[i]
-            tile_ref[0, :, cols] = (mixed[i] * scale).astype(bf16)
-            tile_ref[1, :, cols] = (dot_nn(dlocal[i], key_rows[i]) + dot_nt(dy, priors[i])).astype(bf16)
-            tile_ref[2, :, cols] = dot_nn(dlocal_t[i], queries[i]).astype(bf16)
-            tile_ref[3, :, cols] = dot_nn(local_t[i], dy).astype(bf16)
-        group_out = copies_of(
-            [
-                (tile_ref.at[:, mine, columns(g)], own_far.at[:, :, columns(g)]),
-                (tile_ref.at[:, theirs, columns(g)], send_far.at[:, :, columns(g)]),
-            ],
-            out_sems, 2 * g,
-        )
-        start_all(group_out)
-        out_copies += group_out
+        results = (
+            lambda i: mixed[i] * normed[i][0],
+            lambda i: dot_nn(dlocal[i], key_rows[i]) + dot_nt(normed[i][1], priors[i]),
+            lambda i: dot_nn(dlocal_t[i], queries[i]),
+            lambda i: dot_nn(local_t[i], normed[i][1]),
+        )
+        for slot, result in enumerate(results):
+            for i, (_, cols) in enumerate(heads):
+                tile_ref[slot, :, cols] = result(i).astype(bf16)
+            slot_out = copies_of(
+                [
+                    (tile_ref.at[slot, mine, columns(g)], own_far.at[slot, :, columns(g)]),
+                    (tile_ref.at[slot, theirs, columns(g)], send_far.at[slot, :, columns(g)]),
+                ],
+                out_sems, 2 * (len(results) * g + slot),
+            )
+            start_all(slot_out)
+            out_copies += slot_out
     wait_all(out_copies)
 
 
@@ -430,11 +434,7 @@
     prior = exchange(running, "inner", pair_groups)
     (gq_state,) = call(
         mixed_kernel, (half_states,), (qg, inner, prior), LIMITS["mixed"], 2 * unit,
-        far=(1,), far_out=(0,),
-        scratch=(
-            vmem(2 * tokens, part, dtype=f32), vmem(*half_states.shape),
-            sems(part_groups), sems(part_groups),
-        ),
+        far_out=(0,), scratch=(vmem(*half_states.shape), sems(part_groups)),
     )
     gq_parts = exchange(gq_state, "inner", pair_groups)
     swapped = shape(4, tokens, part)
@@ -444,7 +444,7 @@
         scratch=(
             vmem(*pair_tiles.shape), vmem(*pair_tiles.shape), vmem(2 * tokens, part, dtype=f32),
             vmem(*half_states.shape), vmem(4, 2 * tokens, part),
-            sems(3 * part_groups), sems(1), sems(2 * part_groups),
+            sems(3 * part_groups), sems(1), sems(8 * part_groups),
         ),
     )
     (sent,) = call(total_kernel, totals_shape, (gq_parts, own), LIMITS["total"], far=(1,))

time: 110 us -> 108 us (0.982)
  waiting for transfers between devices: 7.36 us -> 5.5 us
    all_to_all x4, waiting for transfers between devices: 4.87 us -> 3.03 us  [exchange(): lax.all_to_all(blocks, axis, 0, 0, tiled=True, axis_index_groups=groups)]
  transfers between devices with their start and end apart: 6 -> 6, of which waited for: 3 -> 4; matrix products, arithmetic and copies ran while one was open for 0% -> 0% of each run, Pallas kernels for 12% -> 12%
where the time goes in v6:
time: 108 us; the launch traced here: 107 us
  starting transfers between devices  54.7 us (51%)
  blocking collectives  26.1 us (24%)
  Pallas kernels  20.2 us (19%)
  waiting for transfers between devices  5.5 us (5%)
    all_to_all x4, starting transfers between devices, exchange(): lax.all_to_all(blocks, axis, 0, 0, tiled=True, axis_index_groups=groups)  49.9 us
    all_to_all x2, blocking collectives, exchange(): lax.all_to_all(blocks, axis, 0, 0, tiled=True, axis_index_groups=groups)  26.1 us
    pallas_call x11, Pallas kernels, call(): pl.pallas_call(kernel, out_shape=out_shape, in_specs=in_specs, out_specs=...  20.2 us
    ppermute x2, starting transfers between devices, per_device(): recv = lax.ppermute(send, 'inner', swap)  4.81 us
    all_to_all x4, waiting for transfers between devices, exchange(): lax.all_to_all(blocks, axis, 0, 0, tiled=True, axis_index_groups=groups)  3.03 us
    ppermute x2, waiting for transfers between devices, per_device(): recv = lax.ppermute(send, 'inner', swap)  2.48 us
  transfers between devices with their start and end apart: 6, of which 4 were waited for; matrix products, arithmetic and copies ran while one was open for 0% of the time, Pallas kernels for 12%

profile of v6, /device:TPU:1, one launch (start us, length us, event | category | flops | bytes accessed | tf_op | source)
XLA Modules:
  0.0 107.4 jit_solution(16546110439865705067)
XLA Ops:
  0.6 2.6 %shard_map.77 = bf16[32,2,32,128]{3,2,1,0:T(8,128)(2,1)} custom-call(bf16[128,2048]{1,0:T(8,128)(2,1)} %k_ref.1, bf16[128,2048]{1,0:T(8,128)(2,1)} %v_ref.1), custom_call_target="tpu_custom_call" | custom-call | flops 67108864 | bytes 1572864 | tf_op jit(solution)/shard_map/pallas_call | solution.py:58
  3.2 15.1 %all-to-all-start = ((bf16[64,32,128]{2,1,0:T(8,128)(2,1)}), bf16[64,32,128]{2,1,0:T(8,128)(2,1)S(1)}, u32[]{:S(2)}, u32[]{:S(2)}) async-start(bf16[64,32,128]{2,1,0:T(8,128)(2,1)} %bitcast.2), calls=%async_computation | async-start | bytes 1048576 | tf_op jit(solution)/shard_map/all_to_all | solution.py:375
  18.4 0.0 copy-start.7
  18.4 2.3 %shard_map.75.after_far = bf16[4,128,1024]{2,1,0:T(8,128)(2,1)} custom-call(s32[1]{0:T(128)} %bitcast.core_ref, bf16[128,2048]{1,0:T(8,128)(2,1)} %q_far.3, bf16[128,2048]{1,0:T(8,128)(2,1)} %k_ref.1, bf16[128,2048]{1,0:T(8,128)(2,1)} %v_ref.1, bf16[128,2048]{1,0:T(8,128)(2,1)} %g_far.3), custom_call_target="tpu_custom_call" | custom-call | bytes 3145732 | tf_op jit(solution)/shard_map/pallas_call | solution.py:58
  20.7 0.0 copy-start.2
  20.7 0.0 copy-start.3
  20.7 0.0 copy-start.6
  20.7 2.5 %collective-permute-start = (bf16[4,128,1024]{2,1,0:T(8,128)(2,1)}, bf16[4,128,1024]{2,1,0:T(8,128)(2,1)}, u32[]{:S(2)}, u32[]{:S(2)}) collective-permute-start(bf16[4,128,1024]{2,1,0:T(8,128)(2,1)} %shard_map.75.after_far), channel_id=1, source_target_pairs={{0,1},{1,0},{2,3},{3,2},{4,5},{5,4},{6,7},{7,6},{8,9},{9,8},{10,11... | collective-permute-start | bytes 3145736 | tf_op jit(solution)/shard_map/ppermute | solution.py:418
  23.2 1.9 %all-to-all-done.parts_ref = bf16[64,32,128]{2,1,0:T(8,128)(2,1)S(1)} async-done(((bf16[64,32,128]{2,1,0:T(8,128)(2,1)}), bf16[64,32,128]{2,1,0:T(8,128)(2,1)S(1)}, u32[]{:S(2)}, u32[]{:S(2)}) %all-to-all-start) | async-done | bytes 524320 | tf_op jit(solution)/shard_map/all_to_all | solution.py:375
  25.0 0.7 shard_map.78
  25.8 14.1 %all-to-all-start.1 = ((bf16[8,32,128]{2,1,0:T(8,128)(2,1)}), bf16[8,32,128]{2,1,0:T(8,128)(2,1)S(1)}, u32[]{:S(2)}, u32[]{:S(2)}) async-start(bf16[8,32,128]{2,1,0:T(8,128)(2,1)} %shard_map.78), calls=%async_computation.1 | async-start | bytes 131072 | tf_op jit(solution)/shard_map/all_to_all | solution.py:375
  39.8 0.0 collective-permute-done.recv_far
  39.8 0.0 copy-done.7
  39.8 0.0 copy-done.2
  39.9 0.0 copy-done.3
  39.9 0.0 copy-done.6
  39.9 3.2 %shard_map.76 = (f32[256,1024]{1,0:T(8,128)}, bf16[2,256,1024]{2,1,0:T(8,128)(2,1)}, bf16[2,256,1024]{2,1,0:T(8,128)(2,1)}) custom-call(s32[1]{0:T(128)} %bitcast.core_ref, bf16[128,2048]{1,0:T(8,128)(2,1)S(1)} %copy-done.6, bf16[128,2048]{1,0:T(8,128)(2,1)S(1)} %copy-done.2, bf16[128,2048]{1,0:T(8,128)(2,1)S(1)} %copy-done.3, ...), custom_call_target="tpu_custom_call" | custom-call | flops 268435456 | bytes 6291460 | tf_op jit(solution)/shard_map/pallas_call | solution.py:58
  43.1 0.5 all-to-all-done.1.totals_ref
  43.6 0.0 copy-start
  43.6 0.0 copy-start.4
  43.6 0.1 shard_map.79
  43.7 12.0 %all_to_all.30.prior_far.prior_ref = bf16[32,32,128]{2,1,0:T(8,128)(2,1)S(1)} all-to-all(bf16[32,32,128]{2,1,0:T(8,128)(2,1)S(1)} %shard_map.79), channel_id=1, replica_groups={{52,54,48,50,60,62,56,58,36,38,32,34,44,46,40,42,20,22,16,18,28,30,24,2..., dimensions={0} | all-to-all | bytes 524288 | tf_op jit(solution)/shard_map/all_to_all | solution.py:375
  55.7 0.0 copy-start.5
  55.7 0.0 copy-done
  55.7 0.0 copy-done.4
  55.7 1.7 %shard_map.82 = bf16[32,32,128]{2,1,0:T(8,128)(2,1)} custom-call(bf16[2,256,1024]{2,1,0:T(8,128)(2,1)S(1)} %copy-done, f32[256,1024]{1,0:T(8,128)S(1)} %copy-done.4, bf16[32,32,128]{2,1,0:T(8,128)(2,1)S(1)} %all_to_all.30.prior_far.prior_ref), custom_call_target="tpu_custom_call" | custom-call | flops 134217728 | bytes 2621440 | tf_op jit(solution)/shard_map/pallas_call | solution.py:58
  57.4 0.0 copy-done.5
  57.4 8.5 %all-to-all-start.3 = ((bf16[32,32,128]{2,1,0:T(8,128)(2,1)}), bf16[32,32,128]{2,1,0:T(8,128)(2,1)S(1)}, u32[]{:S(2)}, u32[]{:S(2)}) async-start(bf16[32,32,128]{2,1,0:T(8,128)(2,1)} %shard_map.82), calls=%async_computation.3 | async-start | bytes 524288 | tf_op jit(solution)/shard_map/all_to_all | solution.py:375
  65.9 5.2 %shard_map.80 = (bf16[4,128,1024]{2,1,0:T(8,128)(2,1)}, bf16[4,128,1024]{2,1,0:T(8,128)(2,1)}) custom-call(s32[1]{0:T(128)} %bitcast.core_ref, bf16[2,256,1024]{2,1,0:T(8,128)(2,1)} %get-tuple-element.13.after_far.qg_far.qg_ref, bf16[2,256,1024]{2,1,0:T(8,128)(2,1)} %get-tuple-element.14.kv_far, f32[256,1024]{1,0:T(8,128)} %get-tuple-element.15.inner_far.inner_ref, ...), custom_call_target="tpu_custom_call" | custom-call | flops 671088640 | bytes 5505028 | tf_op jit(solution)/shard_map/pallas_call | solution.py:58
  71.1 0.0 all-to-all-done.3.parts_ref
  71.2 0.0 copy-start.1
  71.2 14.1 %all_to_all.31.totals_ref = bf16[8,32,128]{2,1,0:T(8,128)(2,1)S(1)} all-to-all(bf16[8,32,128]{2,1,0:T(8,128)(2,1)S(1)} %shard_map.83), channel_id=1, replica_groups={{256,320,384,448,0,64,128,192},{257,321,385,449,1,65,129,193},{258,322,..., dimensions={0} | all-to-all | bytes 131072 | tf_op jit(solution)/shard_map/all_to_all | solution.py:375
  85.3 0.8 shard_map.84
  86.1 12.2 %all-to-all-start.5 = ((bf16[64,32,128]{2,1,0:T(8,128)(2,1)}), bf16[64,32,128]{2,1,0:T(8,128)(2,1)}, u32[]{:S(2)}, u32[]{:S(2)}) async-start(bf16[64,32,128]{2,1,0:T(8,128)(2,1)} %bitcast.3), calls=%async_computation.5 | async-start | bytes 1048576 | tf_op jit(solution)/shard_map/all_to_all | solution.py:375
  98.3 2.3 %collective-permute-start.1 = (bf16[4,128,1024]{2,1,0:T(8,128)(2,1)}, bf16[4,128,1024]{2,1,0:T(8,128)(2,1)S(1)}, u32[]{:S(2)}, u32[]{:S(2)}) collective-permute-start(bf16[4,128,1024]{2,1,0:T(8,128)(2,1)} %get-tuple-element.17), channel_id=1, source_target_pairs={{0,1},{1,0},{2,3},{3,2},{4,5},{5,4},{6,7},{7,6},{8,9},{9,8},{10,11... | collective-permute-start | bytes 3145736 | tf_op jit(solution)/shard_map/ppermute | solution.py:457
  100.7 2.5 %collective-permute-done.1.recv_far = bf16[4,128,1024]{2,1,0:T(8,128)(2,1)S(1)} collective-permute-done((bf16[4,128,1024]{2,1,0:T(8,128)(2,1)}, bf16[4,128,1024]{2,1,0:T(8,128)(2,1)S(1)}, u32[]{:S(2)}, u32[]{:S(2)}) %collective-permute-start.1) | collective-permute-done | bytes 1048608 | tf_op jit(solution)/shard_map/ppermute | solution.py:457
  103.2 0.0 copy-done.1
  103.2 1.1 %shard_map.81 = (bf16[128,2048]{1,0:T(8,128)(2,1)}, bf16[128,2048]{1,0:T(8,128)(2,1)}) custom-call(s32[1]{0:T(128)} %bitcast.core_ref, bf16[4,128,1024]{2,1,0:T(8,128)(2,1)S(1)} %copy-done.1, bf16[4,128,1024]{2,1,0:T(8,128)(2,1)S(1)} %collective-permute-done.1.recv_far), custom_call_target="tpu_custom_call" | custom-call | bytes 3145732 | tf_op jit(solution)/shard_map/pallas_call | solution.py:58
  104.3 0.7 all-to-all-done.5.later_far
  104.9 2.4 %shard_map.85 = (bf16[128,2048]{1,0:T(8,128)(2,1)}, bf16[128,2048]{1,0:T(8,128)(2,1)}) custom-call(s32[1]{0:T(128)} %bitcast.core_ref, bf16[128,2048]{1,0:T(8,128)(2,1)S(1)} %copy-done.2, bf16[128,2048]{1,0:T(8,128)(2,1)S(1)} %copy-done.3, bf16[4,128,1024]{2,1,0:T(8,128)(2,1)S(1)} %copy-done.1, bf16[4,128,1024]{2,1,0:T(8,128)(2,1)S(1)} %collective-permute-done.1.recv_far, ...), custom_call_target="tpu_custom_call" | custom-call | flops 134217728 | bytes 4718596 | tf_op jit(solution)/shard_map/pallas_call | solution.py:58
  (1 shorter events, 0.0 us)
Async XLA Ops:
  3.2 21.8 %all-to-all-start = ((bf16[64,32,128]{2,1,0:T(8,128)(2,1)}), bf16[64,32,128]{2,1,0:T(8,128)(2,1)S(1)}, u32[]{:S(2)}, u32[]{:S(2)}) async-start(bf16[64,32,128]{2,1,0:T(8,128)(2,1)} %bitcast.2), calls=%async_computation | async-start | bytes 1048576 | tf_op jit(solution)/shard_map/all_to_all | solution.py:375
  18.4 21.5 %copy-start.7 = (bf16[128,2048]{1,0:T(8,128)(2,1)S(1)}, bf16[128,2048]{1,0:T(8,128)(2,1)}, u32[]{:S(2)}) copy-start(bf16[128,2048]{1,0:T(8,128)(2,1)} %g_far.3) | copy-start | bytes 1572868
  20.7 19.2 %copy-start.2 = (bf16[128,2048]{1,0:T(8,128)(2,1)S(1)}, bf16[128,2048]{1,0:T(8,128)(2,1)}, u32[]{:S(2)}) copy-start(bf16[128,2048]{1,0:T(8,128)(2,1)} %k_ref.1) | copy-start | bytes 1572868
  20.7 19.2 %copy-start.3 = (bf16[128,2048]{1,0:T(8,128)(2,1)S(1)}, bf16[128,2048]{1,0:T(8,128)(2,1)}, u32[]{:S(2)}) copy-start(bf16[128,2048]{1,0:T(8,128)(2,1)} %v_ref.1) | copy-start | bytes 1572868
  20.7 19.2 %copy-start.6 = (bf16[128,2048]{1,0:T(8,128)(2,1)S(1)}, bf16[128,2048]{1,0:T(8,128)(2,1)}, u32[]{:S(2)}) copy-start(bf16[128,2048]{1,0:T(8,128)(2,1)} %q_far.3) | copy-start | bytes 1572868
  20.7 19.1 %collective-permute-start = (bf16[4,128,1024]{2,1,0:T(8,128)(2,1)}, bf16[4,128,1024]{2,1,0:T(8,128)(2,1)}, u32[]{:S(2)}, u32[]{:S(2)}) collective-permute-start(bf16[4,128,1024]{2,1,0:T(8,128)(2,1)} %shard_map.75.after_far), channel_id=1, source_target_pairs={{0,1},{1,0},{2,3},{3,2},{4,5},{5,4},{6,7},{7,6},{8,9},{9,8},{10,11... | collective-permute-start | bytes 3145736 | tf_op jit(solution)/shard_map/ppermute | solution.py:418
  25.8 17.8 %all-to-all-start.1 = ((bf16[8,32,128]{2,1,0:T(8,128)(2,1)}), bf16[8,32,128]{2,1,0:T(8,128)(2,1)S(1)}, u32[]{:S(2)}, u32[]{:S(2)}) async-start(bf16[8,32,128]{2,1,0:T(8,128)(2,1)} %shard_map.78), calls=%async_computation.1 | async-start | bytes 131072 | tf_op jit(solution)/shard_map/all_to_all | solution.py:375
  43.6 12.1 %copy-start = (bf16[2,256,1024]{2,1,0:T(8,128)(2,1)S(1)}, bf16[2,256,1024]{2,1,0:T(8,128)(2,1)}, u32[]{:S(2)}) copy-start(bf16[2,256,1024]{2,1,0:T(8,128)(2,1)} %get-tuple-element.13.after_far.qg_far.qg_ref) | copy-start | bytes 3145732
  43.6 12.1 %copy-start.4 = (f32[256,1024]{1,0:T(8,128)S(1)}, f32[256,1024]{1,0:T(8,128)}, u32[]{:S(2)}) copy-start(f32[256,1024]{1,0:T(8,128)} %get-tuple-element.15.inner_far.inner_ref) | copy-start | bytes 3145732
  55.7 1.7 %copy-start.5 = (bf16[32,32,128]{2,1,0:T(8,128)(2,1)}, bf16[32,32,128]{2,1,0:T(8,128)(2,1)S(1)}, u32[]{:S(2)}) copy-start(bf16[32,32,128]{2,1,0:T(8,128)(2,1)S(1)} %all_to_all.30.prior_far.prior_ref) | copy-start | bytes 786436
  57.4 13.7 %all-to-all-start.3 = ((bf16[32,32,128]{2,1,0:T(8,128)(2,1)}), bf16[32,32,128]{2,1,0:T(8,128)(2,1)S(1)}, u32[]{:S(2)}, u32[]{:S(2)}) async-start(bf16[32,32,128]{2,1,0:T(8,128)(2,1)} %shard_map.82), calls=%async_computation.3 | async-start | bytes 524288 | tf_op jit(solution)/shard_map/all_to_all | solution.py:375
  71.2 32.0 %copy-start.1 = (bf16[4,128,1024]{2,1,0:T(8,128)(2,1)S(1)}, bf16[4,128,1024]{2,1,0:T(8,128)(2,1)}, u32[]{:S(2)}) copy-start(bf16[4,128,1024]{2,1,0:T(8,128)(2,1)} %get-tuple-element.16.own_far.after_far) | copy-start | bytes 3145732
  86.1 18.8 %all-to-all-start.5 = ((bf16[64,32,128]{2,1,0:T(8,128)(2,1)}), bf16[64,32,128]{2,1,0:T(8,128)(2,1)}, u32[]{:S(2)}, u32[]{:S(2)}) async-start(bf16[64,32,128]{2,1,0:T(8,128)(2,1)} %bitcast.3), calls=%async_computation.5 | async-start | bytes 1048576 | tf_op jit(solution)/shard_map/all_to_all | solution.py:375
  98.3 4.8 %collective-permute-start.1 = (bf16[4,128,1024]{2,1,0:T(8,128)(2,1)}, bf16[4,128,1024]{2,1,0:T(8,128)(2,1)S(1)}, u32[]{:S(2)}, u32[]{:S(2)}) collective-permute-start(bf16[4,128,1024]{2,1,0:T(8,128)(2,1)} %get-tuple-element.17), channel_id=1, source_target_pairs={{0,1},{1,0},{2,3},{3,2},{4,5},{5,4},{6,7},{7,6},{8,9},{9,8},{10,11... | collective-permute-start | bytes 3145736 | tf_op jit(solution)/shard_map/ppermute | solution.py:457

commit v7 on v6

--- a/solution.py
+++ b/solution.py
@@ -181,12 +181,16 @@
     wait_all(out_copies)
 
 
-def pack_kernel(core_ref, q_far, k_far, v_far, g_far, out_ref, sems):
+def pack_kernel(core_ref, q_far, k_far, v_far, g_far, out_far, near_ref, sems, out_sems):
     other = 1 - core_ref[0]
     rows = (q_far, k_far, v_far, g_far)
-    copies = copies_of([(half(src, other), out_ref.at[i]) for i, src in enumerate(rows)], sems)
+    copies = copies_of([(half(src, other), near_ref.at[i]) for i, src in enumerate(rows)], sems)
     start_all(copies)
-    wait_all(copies)
+    out_copies = copies_of([(near_ref.at[i], out_far.at[i]) for i in range(len(rows))], out_sems)
+    for copy, out_copy in zip(copies, out_copies):
+        copy.wait()
+        out_copy.start()
+    wait_all(out_copies)
 
 
 def local_kernel(
@@ -413,7 +417,8 @@
     kv_parts = exchange(kv.reshape(-1, slice_rows, HEAD_DIM), "inner", inner_groups)
     (send,) = call(
         pack_kernel, (shape(4, tokens, part),), (core, query, keys, values, grads), LIMITS["pack"],
-        far=(1, 2, 3, 4), smem=(0,), scratch=(sems(4),),
+        far=(1, 2, 3, 4), far_out=(0,), smem=(0,),
+        scratch=(vmem(4, tokens, part), sems(4), sems(4)),
     )
     recv = lax.ppermute(send, "inner", swap)
     (sent,) = call(total_kernel, totals_shape, (kv_parts, send), LIMITS["total"], far=(1,))

time: 108 us -> 108 us (level)
  transfers between devices with their start and end apart: 6 -> 6, of which waited for: 4 -> 4; matrix products, arithmetic and copies ran while one was open for 0% -> 0% of each run, Pallas kernels for 12% -> 11%
where the time goes in v7:
time: 108 us; the launch traced here: 107 us
  starting transfers between devices  54.7 us (51%)
  blocking collectives  26.1 us (24%)
  Pallas kernels  20 us (19%)
  waiting for transfers between devices  5.7 us (5%)
    all_to_all x4, starting transfers between devices, exchange(): lax.all_to_all(blocks, axis, 0, 0, tiled=True, axis_index_groups=groups)  49.9 us
    all_to_all x2, blocking collectives, exchange(): lax.all_to_all(blocks, axis, 0, 0, tiled=True, axis_index_groups=groups)  26.1 us
    pallas_call x11, Pallas kernels, call(): pl.pallas_call(kernel, out_shape=out_shape, in_specs=in_specs, out_specs=...  20 us
    ppermute x2, starting transfers between devices, per_device(): recv = lax.ppermute(send, 'inner', swap)  4.81 us
    all_to_all x4, waiting for transfers between devices, exchange(): lax.all_to_all(blocks, axis, 0, 0, tiled=True, axis_index_groups=groups)  3.23 us
    ppermute x2, waiting for transfers between devices, per_device(): recv = lax.ppermute(send, 'inner', swap)  2.48 us
  transfers between devices with their start and end apart: 6, of which 4 were waited for; matrix products, arithmetic and copies ran while one was open for 0% of the time, Pallas kernels for 11%

profile of v7, /device:TPU:1, one launch (start us, length us, event | category | flops | bytes accessed | tf_op | source)
XLA Modules:
  0.0 107.4 jit_solution(16809305758300318404)
XLA Ops:
  0.6 2.6 %shard_map.77 = bf16[32,2,32,128]{3,2,1,0:T(8,128)(2,1)} custom-call(bf16[128,2048]{1,0:T(8,128)(2,1)} %k_ref.1, bf16[128,2048]{1,0:T(8,128)(2,1)} %v_ref.1), custom_call_target="tpu_custom_call" | custom-call | flops 67108864 | bytes 1572864 | tf_op jit(solution)/shard_map/pallas_call | solution.py:58
  3.2 15.1 %all-to-all-start = ((bf16[64,32,128]{2,1,0:T(8,128)(2,1)}), bf16[64,32,128]{2,1,0:T(8,128)(2,1)S(1)}, u32[]{:S(2)}, u32[]{:S(2)}) async-start(bf16[64,32,128]{2,1,0:T(8,128)(2,1)} %bitcast.2), calls=%async_computation | async-start | bytes 1048576 | tf_op jit(solution)/shard_map/all_to_all | solution.py:379
  18.4 0.0 copy-start.7
  18.4 2.1 %shard_map.75.after_far = bf16[4,128,1024]{2,1,0:T(8,128)(2,1)} custom-call(s32[1]{0:T(128)} %bitcast.core_ref, bf16[128,2048]{1,0:T(8,128)(2,1)} %q_far.3, bf16[128,2048]{1,0:T(8,128)(2,1)} %k_ref.1, bf16[128,2048]{1,0:T(8,128)(2,1)} %v_ref.1, bf16[128,2048]{1,0:T(8,128)(2,1)} %g_far.3), custom_call_target="tpu_custom_call" | custom-call | bytes 3145732 | tf_op jit(solution)/shard_map/pallas_call | solution.py:58
  20.5 0.0 copy-start.2
  20.5 0.0 copy-start.3
  20.5 0.0 copy-start.6
  20.5 2.5 %collective-permute-start = (bf16[4,128,1024]{2,1,0:T(8,128)(2,1)}, bf16[4,128,1024]{2,1,0:T(8,128)(2,1)}, u32[]{:S(2)}, u32[]{:S(2)}) collective-permute-start(bf16[4,128,1024]{2,1,0:T(8,128)(2,1)} %shard_map.75.after_far), channel_id=1, source_target_pairs={{0,1},{1,0},{2,3},{3,2},{4,5},{5,4},{6,7},{7,6},{8,9},{9,8},{10,11... | collective-permute-start | bytes 3145736 | tf_op jit(solution)/shard_map/ppermute | solution.py:423
  23.0 2.1 %all-to-all-done.parts_ref = bf16[64,32,128]{2,1,0:T(8,128)(2,1)S(1)} async-done(((bf16[64,32,128]{2,1,0:T(8,128)(2,1)}), bf16[64,32,128]{2,1,0:T(8,128)(2,1)S(1)}, u32[]{:S(2)}, u32[]{:S(2)}) %all-to-all-start) | async-done | bytes 524320 | tf_op jit(solution)/shard_map/all_to_all | solution.py:379
  25.0 0.7 shard_map.78
  25.8 14.1 %all-to-all-start.1 = ((bf16[8,32,128]{2,1,0:T(8,128)(2,1)}), bf16[8,32,128]{2,1,0:T(8,128)(2,1)S(1)}, u32[]{:S(2)}, u32[]{:S(2)}) async-start(bf16[8,32,128]{2,1,0:T(8,128)(2,1)} %shard_map.78), calls=%async_computation.1 | async-start | bytes 131072 | tf_op jit(solution)/shard_map/all_to_all | solution.py:379
  39.8 0.0 collective-permute-done.recv_far
  39.8 0.0 copy-done.7
  39.8 0.0 copy-done.2
  39.9 0.0 copy-done.3
  39.9 0.0 copy-done.6
  39.9 3.2 %shard_map.76 = (f32[256,1024]{1,0:T(8,128)}, bf16[2,256,1024]{2,1,0:T(8,128)(2,1)}, bf16[2,256,1024]{2,1,0:T(8,128)(2,1)}) custom-call(s32[1]{0:T(128)} %bitcast.core_ref, bf16[128,2048]{1,0:T(8,128)(2,1)S(1)} %copy-done.6, bf16[128,2048]{1,0:T(8,128)(2,1)S(1)} %copy-done.2, bf16[128,2048]{1,0:T(8,128)(2,1)S(1)} %copy-done.3, ...), custom_call_target="tpu_custom_call" | custom-call | flops 268435456 | bytes 6291460 | tf_op jit(solution)/shard_map/pallas_call | solution.py:58
  43.1 0.5 all-to-all-done.1.totals_ref
  43.6 0.0 copy-start
  43.6 0.0 copy-start.4
  43.6 0.1 shard_map.79
  43.7 12.0 %all_to_all.30.prior_far.prior_ref = bf16[32,32,128]{2,1,0:T(8,128)(2,1)S(1)} all-to-all(bf16[32,32,128]{2,1,0:T(8,128)(2,1)S(1)} %shard_map.79), channel_id=1, replica_groups={{52,54,48,50,60,62,56,58,36,38,32,34,44,46,40,42,20,22,16,18,28,30,24,2..., dimensions={0} | all-to-all | bytes 524288 | tf_op jit(solution)/shard_map/all_to_all | solution.py:379
  55.7 0.0 copy-start.5
  55.7 0.0 copy-done
  55.7 0.0 copy-done.4
  55.7 1.7 %shard_map.82 = bf16[32,32,128]{2,1,0:T(8,128)(2,1)} custom-call(bf16[2,256,1024]{2,1,0:T(8,128)(2,1)S(1)} %copy-done, f32[256,1024]{1,0:T(8,128)S(1)} %copy-done.4, bf16[32,32,128]{2,1,0:T(8,128)(2,1)S(1)} %all_to_all.30.prior_far.prior_ref), custom_call_target="tpu_custom_call" | custom-call | flops 134217728 | bytes 2621440 | tf_op jit(solution)/shard_map/pallas_call | solution.py:58
  57.4 0.0 copy-done.5
  57.4 8.5 %all-to-all-start.3 = ((bf16[32,32,128]{2,1,0:T(8,128)(2,1)}), bf16[32,32,128]{2,1,0:T(8,128)(2,1)S(1)}, u32[]{:S(2)}, u32[]{:S(2)}) async-start(bf16[32,32,128]{2,1,0:T(8,128)(2,1)} %shard_map.82), calls=%async_computation.3 | async-start | bytes 524288 | tf_op jit(solution)/shard_map/all_to_all | solution.py:379
  65.9 5.2 %shard_map.80 = (bf16[4,128,1024]{2,1,0:T(8,128)(2,1)}, bf16[4,128,1024]{2,1,0:T(8,128)(2,1)}) custom-call(s32[1]{0:T(128)} %bitcast.core_ref, bf16[2,256,1024]{2,1,0:T(8,128)(2,1)} %get-tuple-element.13.after_far.qg_far.qg_ref, bf16[2,256,1024]{2,1,0:T(8,128)(2,1)} %get-tuple-element.14.kv_far, f32[256,1024]{1,0:T(8,128)} %get-tuple-element.15.inner_far.inner_ref, ...), custom_call_target="tpu_custom_call" | custom-call | flops 671088640 | bytes 5505028 | tf_op jit(solution)/shard_map/pallas_call | solution.py:58
  71.1 0.0 all-to-all-done.3.parts_ref
  71.2 0.0 copy-start.1
  71.2 14.1 %all_to_all.31.totals_ref = bf16[8,32,128]{2,1,0:T(8,128)(2,1)S(1)} all-to-all(bf16[8,32,128]{2,1,0:T(8,128)(2,1)S(1)} %shard_map.83), channel_id=1, replica_groups={{256,320,384,448,0,64,128,192},{257,321,385,449,1,65,129,193},{258,322,..., dimensions={0} | all-to-all | bytes 131072 | tf_op jit(solution)/shard_map/all_to_all | solution.py:379
  85.3 0.8 shard_map.84
  86.1 12.2 %all-to-all-start.5 = ((bf16[64,32,128]{2,1,0:T(8,128)(2,1)}), bf16[64,32,128]{2,1,0:T(8,128)(2,1)}, u32[]{:S(2)}, u32[]{:S(2)}) async-start(bf16[64,32,128]{2,1,0:T(8,128)(2,1)} %bitcast.3), calls=%async_computation.5 | async-start | bytes 1048576 | tf_op jit(solution)/shard_map/all_to_all | solution.py:379
  98.3 2.3 %collective-permute-start.1 = (bf16[4,128,1024]{2,1,0:T(8,128)(2,1)}, bf16[4,128,1024]{2,1,0:T(8,128)(2,1)S(1)}, u32[]{:S(2)}, u32[]{:S(2)}) collective-permute-start(bf16[4,128,1024]{2,1,0:T(8,128)(2,1)} %get-tuple-element.17), channel_id=1, source_target_pairs={{0,1},{1,0},{2,3},{3,2},{4,5},{5,4},{6,7},{7,6},{8,9},{9,8},{10,11... | collective-permute-start | bytes 3145736 | tf_op jit(solution)/shard_map/ppermute | solution.py:462
  100.7 2.5 %collective-permute-done.1.recv_far = bf16[4,128,1024]{2,1,0:T(8,128)(2,1)S(1)} collective-permute-done((bf16[4,128,1024]{2,1,0:T(8,128)(2,1)}, bf16[4,128,1024]{2,1,0:T(8,128)(2,1)S(1)}, u32[]{:S(2)}, u32[]{:S(2)}) %collective-permute-start.1) | collective-permute-done | bytes 1048608 | tf_op jit(solution)/shard_map/ppermute | solution.py:462
  103.2 0.0 copy-done.1
  103.2 1.1 %shard_map.81 = (bf16[128,2048]{1,0:T(8,128)(2,1)}, bf16[128,2048]{1,0:T(8,128)(2,1)}) custom-call(s32[1]{0:T(128)} %bitcast.core_ref, bf16[4,128,1024]{2,1,0:T(8,128)(2,1)S(1)} %copy-done.1, bf16[4,128,1024]{2,1,0:T(8,128)(2,1)S(1)} %collective-permute-done.1.recv_far), custom_call_target="tpu_custom_call" | custom-call | bytes 3145732 | tf_op jit(solution)/shard_map/pallas_call | solution.py:58
  104.3 0.7 all-to-all-done.5.later_far
  104.9 2.4 %shard_map.85 = (bf16[128,2048]{1,0:T(8,128)(2,1)}, bf16[128,2048]{1,0:T(8,128)(2,1)}) custom-call(s32[1]{0:T(128)} %bitcast.core_ref, bf16[128,2048]{1,0:T(8,128)(2,1)S(1)} %copy-done.2, bf16[128,2048]{1,0:T(8,128)(2,1)S(1)} %copy-done.3, bf16[4,128,1024]{2,1,0:T(8,128)(2,1)S(1)} %copy-done.1, bf16[4,128,1024]{2,1,0:T(8,128)(2,1)S(1)} %collective-permute-done.1.recv_far, ...), custom_call_target="tpu_custom_call" | custom-call | flops 134217728 | bytes 4718596 | tf_op jit(solution)/shard_map/pallas_call | solution.py:58
  (1 shorter events, 0.0 us)
Async XLA Ops:
  3.2 21.8 %all-to-all-start = ((bf16[64,32,128]{2,1,0:T(8,128)(2,1)}), bf16[64,32,128]{2,1,0:T(8,128)(2,1)S(1)}, u32[]{:S(2)}, u32[]{:S(2)}) async-start(bf16[64,32,128]{2,1,0:T(8,128)(2,1)} %bitcast.2), calls=%async_computation | async-start | bytes 1048576 | tf_op jit(solution)/shard_map/all_to_all | solution.py:379
  18.4 21.5 %copy-start.7 = (bf16[128,2048]{1,0:T(8,128)(2,1)S(1)}, bf16[128,2048]{1,0:T(8,128)(2,1)}, u32[]{:S(2)}) copy-start(bf16[128,2048]{1,0:T(8,128)(2,1)} %g_far.3) | copy-start | bytes 1572868
  20.5 19.4 %copy-start.2 = (bf16[128,2048]{1,0:T(8,128)(2,1)S(1)}, bf16[128,2048]{1,0:T(8,128)(2,1)}, u32[]{:S(2)}) copy-start(bf16[128,2048]{1,0:T(8,128)(2,1)} %k_ref.1) | copy-start | bytes 1572868
  20.5 19.4 %copy-start.3 = (bf16[128,2048]{1,0:T(8,128)(2,1)S(1)}, bf16[128,2048]{1,0:T(8,128)(2,1)}, u32[]{:S(2)}) copy-start(bf16[128,2048]{1,0:T(8,128)(2,1)} %v_ref.1) | copy-start | bytes 1572868
  20.5 19.4 %copy-start.6 = (bf16[128,2048]{1,0:T(8,128)(2,1)S(1)}, bf16[128,2048]{1,0:T(8,128)(2,1)}, u32[]{:S(2)}) copy-start(bf16[128,2048]{1,0:T(8,128)(2,1)} %q_far.3) | copy-start | bytes 1572868
  20.5 19.3 %collective-permute-start = (bf16[4,128,1024]{2,1,0:T(8,128)(2,1)}, bf16[4,128,1024]{2,1,0:T(8,128)(2,1)}, u32[]{:S(2)}, u32[]{:S(2)}) collective-permute-start(bf16[4,128,1024]{2,1,0:T(8,128)(2,1)} %shard_map.75.after_far), channel_id=1, source_target_pairs={{0,1},{1,0},{2,3},{3,2},{4,5},{5,4},{6,7},{7,6},{8,9},{9,8},{10,11... | collective-permute-start | bytes 3145736 | tf_op jit(solution)/shard_map/ppermute | solution.py:423
  25.8 17.8 %all-to-all-start.1 = ((bf16[8,32,128]{2,1,0:T(8,128)(2,1)}), bf16[8,32,128]{2,1,0:T(8,128)(2,1)S(1)}, u32[]{:S(2)}, u32[]{:S(2)}) async-start(bf16[8,32,128]{2,1,0:T(8,128)(2,1)} %shard_map.78), calls=%async_computation.1 | async-start | bytes 131072 | tf_op jit(solution)/shard_map/all_to_all | solution.py:379
  43.6 12.1 %copy-start = (bf16[2,256,1024]{2,1,0:T(8,128)(2,1)S(1)}, bf16[2,256,1024]{2,1,0:T(8,128)(2,1)}, u32[]{:S(2)}) copy-start(bf16[2,256,1024]{2,1,0:T(8,128)(2,1)} %get-tuple-element.13.after_far.qg_far.qg_ref) | copy-start | bytes 3145732
  43.6 12.1 %copy-start.4 = (f32[256,1024]{1,0:T(8,128)S(1)}, f32[256,1024]{1,0:T(8,128)}, u32[]{:S(2)}) copy-start(f32[256,1024]{1,0:T(8,128)} %get-tuple-element.15.inner_far.inner_ref) | copy-start | bytes 3145732
  55.7 1.7 %copy-start.5 = (bf16[32,32,128]{2,1,0:T(8,128)(2,1)}, bf16[32,32,128]{2,1,0:T(8,128)(2,1)S(1)}, u32[]{:S(2)}) copy-start(bf16[32,32,128]{2,1,0:T(8,128)(2,1)S(1)} %all_to_all.30.prior_far.prior_ref) | copy-start | bytes 786436
  57.4 13.7 %all-to-all-start.3 = ((bf16[32,32,128]{2,1,0:T(8,128)(2,1)}), bf16[32,32,128]{2,1,0:T(8,128)(2,1)S(1)}, u32[]{:S(2)}, u32[]{:S(2)}) async-start(bf16[32,32,128]{2,1,0:T(8,128)(2,1)} %shard_map.82), calls=%async_computation.3 | async-start | bytes 524288 | tf_op jit(solution)/shard_map/all_to_all | solution.py:379
  71.2 32.0 %copy-start.1 = (bf16[4,128,1024]{2,1,0:T(8,128)(2,1)S(1)}, bf16[4,128,1024]{2,1,0:T(8,128)(2,1)}, u32[]{:S(2)}) copy-start(bf16[4,128,1024]{2,1,0:T(8,128)(2,1)} %get-tuple-element.16.own_far.after_far) | copy-start | bytes 3145732
  86.1 18.8 %all-to-all-start.5 = ((bf16[64,32,128]{2,1,0:T(8,128)(2,1)}), bf16[64,32,128]{2,1,0:T(8,128)(2,1)}, u32[]{:S(2)}, u32[]{:S(2)}) async-start(bf16[64,32,128]{2,1,0:T(8,128)(2,1)} %bitcast.3), calls=%async_computation.5 | async-start | bytes 1048576 | tf_op jit(solution)/shard_map/all_to_all | solution.py:379
  98.3 4.8 %collective-permute-start.1 = (bf16[4,128,1024]{2,1,0:T(8,128)(2,1)}, bf16[4,128,1024]{2,1,0:T(8,128)(2,1)S(1)}, u32[]{:S(2)}, u32[]{:S(2)}) collective-permute-start(bf16[4,128,1024]{2,1,0:T(8,128)(2,1)} %get-tuple-element.17), channel_id=1, source_target_pairs={{0,1},{1,0},{2,3},{3,2},{4,5},{5,4},{6,7},{7,6},{8,9},{9,8},{10,11... | collective-permute-start | bytes 3145736 | tf_op jit(solution)/shard_map/ppermute | solution.py:462

commit v8 on v7

--- a/solution.py
+++ b/solution.py
@@ -22,7 +22,7 @@
     "finish": 48 * MIB,
     "last": 50 * MIB,
 }
-OUTER_TURN = 4
+OUTER_TURN = 5
 INNER_TURN = 53
 PAIR_TURN, CORE_TURN = INNER_TURN // 2, INNER_TURN % 2
 f32 = jnp.float32

time: 108 us -> 108 us (level)
  blocking collectives: 26.1 us -> 28 us
  starting transfers between devices: 54.7 us -> 52.9 us
    all_to_all x2, blocking collectives: 26.1 us -> 28 us  [exchange(): lax.all_to_all(blocks, axis, 0, 0, tiled=True, axis_index_groups=groups)]
    all_to_all x4, starting transfers between devices: 49.9 us -> 48.1 us  [exchange(): lax.all_to_all(blocks, axis, 0, 0, tiled=True, axis_index_groups=groups)]
where the time goes in v8:
time: 108 us
  starting transfers between devices  52.9 us (49%)
  blocking collectives  28 us (26%)
  Pallas kernels  20 us (19%)
  waiting for transfers between devices  6.02 us (6%)
    all_to_all x4, starting transfers between devices, exchange(): lax.all_to_all(blocks, axis, 0, 0, tiled=True, axis_index_groups=groups)  48.1 us
    all_to_all x2, blocking collectives, exchange(): lax.all_to_all(blocks, axis, 0, 0, tiled=True, axis_index_groups=groups)  28 us
    pallas_call x11, Pallas kernels, call(): pl.pallas_call(kernel, out_shape=out_shape, in_specs=in_specs, out_specs=...  20 us
    ppermute x2, starting transfers between devices, per_device(): recv = lax.ppermute(send, 'inner', swap)  4.81 us
    all_to_all x4, waiting for transfers between devices, exchange(): lax.all_to_all(blocks, axis, 0, 0, tiled=True, axis_index_groups=groups)  3.54 us
    ppermute x2, waiting for transfers between devices, per_device(): recv = lax.ppermute(send, 'inner', swap)  2.48 us
  transfers between devices with their start and end apart: 6, of which 4 were waited for; matrix products, arithmetic and copies ran while one was open for 0% of the time, Pallas kernels for 11%

profile of v8, /device:TPU:1, one launch (start us, length us, event | category | flops | bytes accessed | tf_op | source)
XLA Modules:
  0.0 107.7 jit_solution(12108862002769061387)
XLA Ops:
  0.6 2.6 %shard_map.77 = bf16[32,2,32,128]{3,2,1,0:T(8,128)(2,1)} custom-call(bf16[128,2048]{1,0:T(8,128)(2,1)} %k_ref.1, bf16[128,2048]{1,0:T(8,128)(2,1)} %v_ref.1), custom_call_target="tpu_custom_call" | custom-call | flops 67108864 | bytes 1572864 | tf_op jit(solution)/shard_map/pallas_call | solution.py:58
  3.2 15.1 %all-to-all-start = ((bf16[64,32,128]{2,1,0:T(8,128)(2,1)}), bf16[64,32,128]{2,1,0:T(8,128)(2,1)S(1)}, u32[]{:S(2)}, u32[]{:S(2)}) async-start(bf16[64,32,128]{2,1,0:T(8,128)(2,1)} %bitcast.2), calls=%async_computation | async-start | bytes 1048576 | tf_op jit(solution)/shard_map/all_to_all | solution.py:379
  18.4 0.0 copy-start.7
  18.4 2.1 %shard_map.75.after_far = bf16[4,128,1024]{2,1,0:T(8,128)(2,1)} custom-call(s32[1]{0:T(128)} %bitcast.core_ref, bf16[128,2048]{1,0:T(8,128)(2,1)} %q_far.3, bf16[128,2048]{1,0:T(8,128)(2,1)} %k_ref.1, bf16[128,2048]{1,0:T(8,128)(2,1)} %v_ref.1, bf16[128,2048]{1,0:T(8,128)(2,1)} %g_far.3), custom_call_target="tpu_custom_call" | custom-call | bytes 3145732 | tf_op jit(solution)/shard_map/pallas_call | solution.py:58
  20.5 0.0 copy-start.2
  20.5 0.0 copy-start.3
  20.5 0.0 copy-start.6
  20.5 2.5 %collective-permute-start = (bf16[4,128,1024]{2,1,0:T(8,128)(2,1)}, bf16[4,128,1024]{2,1,0:T(8,128)(2,1)}, u32[]{:S(2)}, u32[]{:S(2)}) collective-permute-start(bf16[4,128,1024]{2,1,0:T(8,128)(2,1)} %shard_map.75.after_far), channel_id=1, source_target_pairs={{0,1},{1,0},{2,3},{3,2},{4,5},{5,4},{6,7},{7,6},{8,9},{9,8},{10,11... | collective-permute-start | bytes 3145736 | tf_op jit(solution)/shard_map/ppermute | solution.py:423
  23.0 2.1 %all-to-all-done.parts_ref = bf16[64,32,128]{2,1,0:T(8,128)(2,1)S(1)} async-done(((bf16[64,32,128]{2,1,0:T(8,128)(2,1)}), bf16[64,32,128]{2,1,0:T(8,128)(2,1)S(1)}, u32[]{:S(2)}, u32[]{:S(2)}) %all-to-all-start) | async-done | bytes 524320 | tf_op jit(solution)/shard_map/all_to_all | solution.py:379
  25.0 0.7 shard_map.78
  25.8 12.3 %all-to-all-start.1 = ((bf16[8,32,128]{2,1,0:T(8,128)(2,1)}), bf16[8,32,128]{2,1,0:T(8,128)(2,1)S(1)}, u32[]{:S(2)}, u32[]{:S(2)}) async-start(bf16[8,32,128]{2,1,0:T(8,128)(2,1)} %shard_map.78), calls=%async_computation.1 | async-start | bytes 131072 | tf_op jit(solution)/shard_map/all_to_all | solution.py:379
  38.0 0.0 collective-permute-done.recv_far
  38.0 0.0 copy-done.7
  38.0 0.0 copy-done.2
  38.1 0.0 copy-done.3
  38.1 0.0 copy-done.6
  38.1 3.2 %shard_map.76 = (f32[256,1024]{1,0:T(8,128)}, bf16[2,256,1024]{2,1,0:T(8,128)(2,1)}, bf16[2,256,1024]{2,1,0:T(8,128)(2,1)}) custom-call(s32[1]{0:T(128)} %bitcast.core_ref, bf16[128,2048]{1,0:T(8,128)(2,1)S(1)} %copy-done.6, bf16[128,2048]{1,0:T(8,128)(2,1)S(1)} %copy-done.2, bf16[128,2048]{1,0:T(8,128)(2,1)S(1)} %copy-done.3, ...), custom_call_target="tpu_custom_call" | custom-call | flops 268435456 | bytes 6291460 | tf_op jit(solution)/shard_map/pallas_call | solution.py:58
  41.3 0.8 all-to-all-done.1.totals_ref
  42.1 0.0 copy-start
  42.1 0.0 copy-start.4
  42.1 0.1 shard_map.79
  42.2 13.0 %all_to_all.30.prior_far.prior_ref = bf16[32,32,128]{2,1,0:T(8,128)(2,1)S(1)} all-to-all(bf16[32,32,128]{2,1,0:T(8,128)(2,1)S(1)} %shard_map.79), channel_id=1, replica_groups={{52,54,48,50,60,62,56,58,36,38,32,34,44,46,40,42,20,22,16,18,28,30,24,2..., dimensions={0} | all-to-all | bytes 524288 | tf_op jit(solution)/shard_map/all_to_all | solution.py:379
  55.2 0.0 copy-start.5
  55.2 0.0 copy-done
  55.2 0.0 copy-done.4
  55.2 1.7 %shard_map.82 = bf16[32,32,128]{2,1,0:T(8,128)(2,1)} custom-call(bf16[2,256,1024]{2,1,0:T(8,128)(2,1)S(1)} %copy-done, f32[256,1024]{1,0:T(8,128)S(1)} %copy-done.4, bf16[32,32,128]{2,1,0:T(8,128)(2,1)S(1)} %all_to_all.30.prior_far.prior_ref), custom_call_target="tpu_custom_call" | custom-call | flops 134217728 | bytes 2621440 | tf_op jit(solution)/shard_map/pallas_call | solution.py:58
  56.9 0.0 copy-done.5
  56.9 8.4 %all-to-all-start.3 = ((bf16[32,32,128]{2,1,0:T(8,128)(2,1)}), bf16[32,32,128]{2,1,0:T(8,128)(2,1)S(1)}, u32[]{:S(2)}, u32[]{:S(2)}) async-start(bf16[32,32,128]{2,1,0:T(8,128)(2,1)} %shard_map.82), calls=%async_computation.3 | async-start | bytes 524288 | tf_op jit(solution)/shard_map/all_to_all | solution.py:379
  65.3 5.2 %shard_map.80 = (bf16[4,128,1024]{2,1,0:T(8,128)(2,1)}, bf16[4,128,1024]{2,1,0:T(8,128)(2,1)}) custom-call(s32[1]{0:T(128)} %bitcast.core_ref, bf16[2,256,1024]{2,1,0:T(8,128)(2,1)} %get-tuple-element.13.after_far.qg_far.qg_ref, bf16[2,256,1024]{2,1,0:T(8,128)(2,1)} %get-tuple-element.14.kv_far, f32[256,1024]{1,0:T(8,128)} %get-tuple-element.15.inner_far.inner_ref, ...), custom_call_target="tpu_custom_call" | custom-call | flops 671088640 | bytes 5505028 | tf_op jit(solution)/shard_map/pallas_call | solution.py:58
  70.5 0.0 all-to-all-done.3.parts_ref
  70.6 0.0 copy-start.1
  70.6 15.0 %all_to_all.31.totals_ref = bf16[8,32,128]{2,1,0:T(8,128)(2,1)S(1)} all-to-all(bf16[8,32,128]{2,1,0:T(8,128)(2,1)S(1)} %shard_map.83), channel_id=1, replica_groups={{320,256,448,384,64,0,192,128},{321,257,449,385,65,1,193,129},{322,258,..., dimensions={0} | all-to-all | bytes 131072 | tf_op jit(solution)/shard_map/all_to_all | solution.py:379
  85.6 0.8 shard_map.84
  86.4 12.3 %all-to-all-start.5 = ((bf16[64,32,128]{2,1,0:T(8,128)(2,1)}), bf16[64,32,128]{2,1,0:T(8,128)(2,1)}, u32[]{:S(2)}, u32[]{:S(2)}) async-start(bf16[64,32,128]{2,1,0:T(8,128)(2,1)} %bitcast.3), calls=%async_computation.5 | async-start | bytes 1048576 | tf_op jit(solution)/shard_map/all_to_all | solution.py:379
  98.7 2.3 %collective-permute-start.1 = (bf16[4,128,1024]{2,1,0:T(8,128)(2,1)}, bf16[4,128,1024]{2,1,0:T(8,128)(2,1)S(1)}, u32[]{:S(2)}, u32[]{:S(2)}) collective-permute-start(bf16[4,128,1024]{2,1,0:T(8,128)(2,1)} %get-tuple-element.17), channel_id=1, source_target_pairs={{0,1},{1,0},{2,3},{3,2},{4,5},{5,4},{6,7},{7,6},{8,9},{9,8},{10,11... | collective-permute-start | bytes 3145736 | tf_op jit(solution)/shard_map/ppermute | solution.py:462
  101.0 2.5 %collective-permute-done.1.recv_far = bf16[4,128,1024]{2,1,0:T(8,128)(2,1)S(1)} collective-permute-done((bf16[4,128,1024]{2,1,0:T(8,128)(2,1)}, bf16[4,128,1024]{2,1,0:T(8,128)(2,1)S(1)}, u32[]{:S(2)}, u32[]{:S(2)}) %collective-permute-start.1) | collective-permute-done | bytes 1048608 | tf_op jit(solution)/shard_map/ppermute | solution.py:462
  103.5 0.0 copy-done.1
  103.5 1.1 %shard_map.81 = (bf16[128,2048]{1,0:T(8,128)(2,1)}, bf16[128,2048]{1,0:T(8,128)(2,1)}) custom-call(s32[1]{0:T(128)} %bitcast.core_ref, bf16[4,128,1024]{2,1,0:T(8,128)(2,1)S(1)} %copy-done.1, bf16[4,128,1024]{2,1,0:T(8,128)(2,1)S(1)} %collective-permute-done.1.recv_far), custom_call_target="tpu_custom_call" | custom-call | bytes 3145732 | tf_op jit(solution)/shard_map/pallas_call | solution.py:58
  104.6 0.7 all-to-all-done.5.later_far
  105.3 2.4 %shard_map.85 = (bf16[128,2048]{1,0:T(8,128)(2,1)}, bf16[128,2048]{1,0:T(8,128)(2,1)}) custom-call(s32[1]{0:T(128)} %bitcast.core_ref, bf16[128,2048]{1,0:T(8,128)(2,1)S(1)} %copy-done.2, bf16[128,2048]{1,0:T(8,128)(2,1)S(1)} %copy-done.3, bf16[4,128,1024]{2,1,0:T(8,128)(2,1)S(1)} %copy-done.1, bf16[4,128,1024]{2,1,0:T(8,128)(2,1)S(1)} %collective-permute-done.1.recv_far, ...), custom_call_target="tpu_custom_call" | custom-call | flops 134217728 | bytes 4718596 | tf_op jit(solution)/shard_map/pallas_call | solution.py:58
  (1 shorter events, 0.0 us)
Async XLA Ops:
  3.2 21.8 %all-to-all-start = ((bf16[64,32,128]{2,1,0:T(8,128)(2,1)}), bf16[64,32,128]{2,1,0:T(8,128)(2,1)S(1)}, u32[]{:S(2)}, u32[]{:S(2)}) async-start(bf16[64,32,128]{2,1,0:T(8,128)(2,1)} %bitcast.2), calls=%async_computation | async-start | bytes 1048576 | tf_op jit(solution)/shard_map/all_to_all | solution.py:379
  18.4 19.7 %copy-start.7 = (bf16[128,2048]{1,0:T(8,128)(2,1)S(1)}, bf16[128,2048]{1,0:T(8,128)(2,1)}, u32[]{:S(2)}) copy-start(bf16[128,2048]{1,0:T(8,128)(2,1)} %g_far.3) | copy-start | bytes 1572868
  20.5 17.6 %copy-start.2 = (bf16[128,2048]{1,0:T(8,128)(2,1)S(1)}, bf16[128,2048]{1,0:T(8,128)(2,1)}, u32[]{:S(2)}) copy-start(bf16[128,2048]{1,0:T(8,128)(2,1)} %k_ref.1) | copy-start | bytes 1572868
  20.5 17.6 %copy-start.3 = (bf16[128,2048]{1,0:T(8,128)(2,1)S(1)}, bf16[128,2048]{1,0:T(8,128)(2,1)}, u32[]{:S(2)}) copy-start(bf16[128,2048]{1,0:T(8,128)(2,1)} %v_ref.1) | copy-start | bytes 1572868
  20.5 17.6 %copy-start.6 = (bf16[128,2048]{1,0:T(8,128)(2,1)S(1)}, bf16[128,2048]{1,0:T(8,128)(2,1)}, u32[]{:S(2)}) copy-start(bf16[128,2048]{1,0:T(8,128)(2,1)} %q_far.3) | copy-start | bytes 1572868
  20.5 17.5 %collective-permute-start = (bf16[4,128,1024]{2,1,0:T(8,128)(2,1)}, bf16[4,128,1024]{2,1,0:T(8,128)(2,1)}, u32[]{:S(2)}, u32[]{:S(2)}) collective-permute-start(bf16[4,128,1024]{2,1,0:T(8,128)(2,1)} %shard_map.75.after_far), channel_id=1, source_target_pairs={{0,1},{1,0},{2,3},{3,2},{4,5},{5,4},{6,7},{7,6},{8,9},{9,8},{10,11... | collective-permute-start | bytes 3145736 | tf_op jit(solution)/shard_map/ppermute | solution.py:423
  25.8 16.3 %all-to-all-start.1 = ((bf16[8,32,128]{2,1,0:T(8,128)(2,1)}), bf16[8,32,128]{2,1,0:T(8,128)(2,1)S(1)}, u32[]{:S(2)}, u32[]{:S(2)}) async-start(bf16[8,32,128]{2,1,0:T(8,128)(2,1)} %shard_map.78), calls=%async_computation.1 | async-start | bytes 131072 | tf_op jit(solution)/shard_map/all_to_all | solution.py:379
  42.1 13.1 %copy-start = (bf16[2,256,1024]{2,1,0:T(8,128)(2,1)S(1)}, bf16[2,256,1024]{2,1,0:T(8,128)(2,1)}, u32[]{:S(2)}) copy-start(bf16[2,256,1024]{2,1,0:T(8,128)(2,1)} %get-tuple-element.13.after_far.qg_far.qg_ref) | copy-start | bytes 3145732
  42.1 13.1 %copy-start.4 = (f32[256,1024]{1,0:T(8,128)S(1)}, f32[256,1024]{1,0:T(8,128)}, u32[]{:S(2)}) copy-start(f32[256,1024]{1,0:T(8,128)} %get-tuple-element.15.inner_far.inner_ref) | copy-start | bytes 3145732
  55.2 1.7 %copy-start.5 = (bf16[32,32,128]{2,1,0:T(8,128)(2,1)}, bf16[32,32,128]{2,1,0:T(8,128)(2,1)S(1)}, u32[]{:S(2)}) copy-start(bf16[32,32,128]{2,1,0:T(8,128)(2,1)S(1)} %all_to_all.30.prior_far.prior_ref) | copy-start | bytes 786436
  56.9 13.6 %all-to-all-start.3 = ((bf16[32,32,128]{2,1,0:T(8,128)(2,1)}), bf16[32,32,128]{2,1,0:T(8,128)(2,1)S(1)}, u32[]{:S(2)}, u32[]{:S(2)}) async-start(bf16[32,32,128]{2,1,0:T(8,128)(2,1)} %shard_map.82), calls=%async_computation.3 | async-start | bytes 524288 | tf_op jit(solution)/shard_map/all_to_all | solution.py:379
  70.6 32.9 %copy-start.1 = (bf16[4,128,1024]{2,1,0:T(8,128)(2,1)S(1)}, bf16[4,128,1024]{2,1,0:T(8,128)(2,1)}, u32[]{:S(2)}) copy-start(bf16[4,128,1024]{2,1,0:T(8,128)(2,1)} %get-tuple-element.16.own_far.after_far) | copy-start | bytes 3145732
  86.4 18.8 %all-to-all-start.5 = ((bf16[64,32,128]{2,1,0:T(8,128)(2,1)}), bf16[64,32,128]{2,1,0:T(8,128)(2,1)}, u32[]{:S(2)}, u32[]{:S(2)}) async-start(bf16[64,32,128]{2,1,0:T(8,128)(2,1)} %bitcast.3), calls=%async_computation.5 | async-start | bytes 1048576 | tf_op jit(solution)/shard_map/all_to_all | solution.py:379
  98.7 4.8 %collective-permute-start.1 = (bf16[4,128,1024]{2,1,0:T(8,128)(2,1)}, bf16[4,128,1024]{2,1,0:T(8,128)(2,1)S(1)}, u32[]{:S(2)}, u32[]{:S(2)}) collective-permute-start(bf16[4,128,1024]{2,1,0:T(8,128)(2,1)} %get-tuple-element.17), channel_id=1, source_target_pairs={{0,1},{1,0},{2,3},{3,2},{4,5},{5,4},{6,7},{7,6},{8,9},{9,8},{10,11... | collective-permute-start | bytes 3145736 | tf_op jit(solution)/shard_map/ppermute | solution.py:462
